TPU v7x, 512 devices: a whole 4x4x16 slice. The times are simulated.
512 devices in a mesh: slab: 32 (over z, core), sub: 16 (over x, y).
Axes of the slice: x: 4, y: 4, z: 16, core: 2. Of those that a mesh axis runs over, the one named last changes fastest.
Arguments:
- fields: float32 [6, 20, 131072], P(None, None, ('slab', 'sub')), may hold values from -6 to 6
- geometry: float32 [11, 131072], P(None, ('slab', 'sub')), as said below
- migrate_list: int32 [512, 32, 12], P(('slab', 'sub')), may hold values from -1 to 255, as said below
- trace_list: int32 [512, 16, 16], P(('slab', 'sub')), may hold values from 0 to 1535, as said below
- face_link: int32 [4, 196608], P(None, ('slab', 'sub')), may hold values from 0 to 1791, as said below
- face_orient: int32 [4, 196608], P(None, ('slab', 'sub')), may hold values from 0 to 6, as said below
Outputs:
- advanced: float32 [6, 20, 196608], P(None, None, ('slab', 'sub'))
- section_residual: float32 [6, 20, 196608], P(None, None, ('slab', 'sub'))
Inputs may be any that keep to these rules, and one draw needn't show every extreme that they name: `migrate_list`: for each device and destination slab, the first entries (at least one) are distinct local element indices and the rest are -1; over the 32 destinations each of the device's elements appears exactly once; one slab position receives 12 elements from every device. `trace_list`: face codes f * 384 + e of the sending device, all distinct within a device; they name occupied slots. `face_link`: codes below 1536 name a face of the device's own occupied slots; each code from 1536 on is named by exactly one face of the device; walls and empty slots hold 0. `face_orient`: every face of an empty slot is 6. `geometry`: each diagonal entry of G is positive and at least three times any other entry of G in magnitude; eps and mu are positive.
All inputs are finite; a program needn't handle non-finite values.
Results may differ from a plain program's by a relative error of at most 0.0003.
Values sent between devices are 32-bit elements; how exact they have to be, the bound alone decides.
No kernel may reach another device: no remote copies, remote signals or barrier semaphores. Data moves between devices by JAX's collectives and lax.ppermute only.
A program may use at most 64 MiB of HBM per device.

v0:
```python
import math

import jax
import jax.numpy as jnp
from jax import lax
from jax.sharding import PartitionSpec as P

time_step = 0.004
section_a2 = -0.4178904745
section_b1 = 0.1496590219993
section_b2 = 0.3792103129999
highest = lax.Precision.HIGHEST
coordinate_perms = ((0, 1, 2), (1, 2, 0), (2, 0, 1), (0, 2, 1), (2, 1, 0), (1, 0, 2))
reference_normals = ((0.0, 0.0, -1.0), (0.0, -1.0, 0.0), (1.0, 1.0, 1.0), (-1.0, 0.0, 0.0))


def volume_triples():
    result_list = []
    for first_idx in range(4):
        for second_idx in range(4 - first_idx):
            for third_idx in range(4 - first_idx - second_idx):
                result_list.append((first_idx, second_idx, third_idx))
    return result_list


def planar_pairs():
    result_list = []
    for first_idx in range(4):
        for second_idx in range(4 - first_idx):
            result_list.append((first_idx, second_idx))
    return result_list


def monomial_matrix(points, powers):
    result_rows = []
    for point_item in points:
        row_values = []
        for power_item in powers:
            product_value = 1.0
            for axis_id in range(len(power_item)):
                product_value = product_value * point_item[axis_id] ** power_item[axis_id]
            row_values.append(product_value)
        result_rows.append(row_values)
    return result_rows


def mat_mul(left_rows, right_rows):
    inner_count = len(right_rows)
    col_count = len(right_rows[0])
    return [
        [
            sum((left_row[k_id] * right_rows[k_id][c_id] for k_id in range(inner_count)))
            for c_id in range(col_count)
        ]
        for left_row in left_rows
    ]


def transposed(matrix_rows):
    return [list(row_item) for row_item in zip(*matrix_rows)]


def invert(matrix_rows):
    order = len(matrix_rows)
    work_rows = [
        list(matrix_rows[r_id]) + [1.0 if r_id == c_id else 0.0 for c_id in range(order)]
        for r_id in range(order)
    ]
    for col_id in range(order):
        pivot_row = max(range(col_id, order), key=lambda r_id: abs(work_rows[r_id][col_id]))
        work_rows[col_id], work_rows[pivot_row] = (work_rows[pivot_row], work_rows[col_id])
        pivot_value = work_rows[col_id][col_id]
        work_rows[col_id] = [value / pivot_value for value in work_rows[col_id]]
        for r_id in range(order):
            if r_id != col_id:
                factor = work_rows[r_id][col_id]
                if factor != 0.0:
                    work_rows[r_id] = [
                        work_rows[r_id][c_id] - factor * work_rows[col_id][c_id]
                        for c_id in range(2 * order)
                    ]
    return [row_item[order:] for row_item in work_rows]


def moment_matrix(powers, extra_dim):
    total_terms = len(powers)
    result_matrix = [[0.0] * total_terms for _ in range(total_terms)]
    for row_id in range(total_terms):
        for col_id in range(total_terms):
            joined = [
                powers[row_id][a_id] + powers[col_id][a_id] for a_id in range(len(powers[row_id]))
            ]
            numerator = 1.0
            for exponent in joined:
                numerator = numerator * math.factorial(exponent)
            result_matrix[row_id][col_id] = numerator / math.factorial(sum(joined) + extra_dim)
    return result_matrix


def dg_tables():
    triples = volume_triples()
    points = [tuple((value / 3.0 for value in triple)) for triple in triples]
    inverse = invert(monomial_matrix(points, triples))
    slopes = []
    for axis_id in range(3):
        lowered = [
            tuple(
                (max(triple[a_id] - 1, 0) if a_id == axis_id else triple[a_id] for a_id in range(3))
            )
            for triple in triples
        ]
        base_rows = monomial_matrix(points, lowered)
        slope_values = [
            [triples[c_id][axis_id] * base_rows[r_id][c_id] for c_id in range(20)]
            for r_id in range(20)
        ]
        slopes.append(mat_mul(slope_values, inverse))
    volume_mass = mat_mul(mat_mul(transposed(inverse), moment_matrix(triples, 3)), inverse)
    planar = planar_pairs()
    face_points = [tuple((value / 3.0 for value in pair_item)) for pair_item in planar]
    face_inverse = invert(monomial_matrix(face_points, planar))
    face_mass = mat_mul(mat_mul(transposed(face_inverse), moment_matrix(planar, 2)), face_inverse)
    face_axes = ((0, 1), (0, 2), (0, 1), (1, 2))
    face_mask = [[0] * 10 for _ in range(4)]
    for face_id in range(4):
        for node_id, triple in enumerate(triples):
            on_face = (
                triple[2] == 0,
                triple[1] == 0,
                triple[0] + triple[1] + triple[2] == 3,
                triple[0] == 0,
            )[face_id]
            if on_face:
                key_pair = (triple[face_axes[face_id][0]], triple[face_axes[face_id][1]])
                face_mask[face_id][planar.index(key_pair)] = node_id
    surface = [[0.0] * 40 for _ in range(20)]
    for face_id in range(4):
        for row_id in range(10):
            for col_id in range(10):
                surface[face_mask[face_id][row_id]][face_id * 10 + col_id] += face_mass[row_id][
                    col_id
                ]
    lifting = mat_mul(invert(volume_mass), surface)
    lift_alt = [
        [lifting[n_id][f_id * 10 + j_id] for j_id in range(10) for f_id in range(4)]
        for n_id in range(20)
    ]
    node_perms = []
    for turn_id in range(6):
        perm_row = []
        for pair_item in planar:
            triple_face = (pair_item[0], pair_item[1], 3 - pair_item[0] - pair_item[1])
            moved_triple = [triple_face[coordinate_perms[turn_id][axis_id]] for axis_id in range(3)]
            perm_row.append(planar.index((moved_triple[0], moved_triple[1])))
        node_perms.append(perm_row)
    node_picks = [face_mask[f_id][j_id] for j_id in range(10) for f_id in range(4)]
    return (
        jnp.asarray(slopes, dtype=jnp.float32),
        jnp.asarray(lift_alt, dtype=jnp.float32),
        node_picks,
        node_perms,
    )


def derive_geometry(raw_geometry):
    elements = raw_geometry.shape[1]
    inverse_jac = raw_geometry[:9].reshape(3, 3, elements)
    normal_table = jnp.asarray(reference_normals, dtype=jnp.float32)
    outward = jnp.einsum("fi,ijk->jfk", normal_table, inverse_jac, precision=highest)
    lengths = jnp.sqrt(jnp.sum(outward * outward, axis=0))
    unit_normals = outward / lengths[None]
    return jnp.concatenate(
        [raw_geometry[:9], unit_normals.reshape(12, elements), lengths, raw_geometry[9:11]], axis=0
    )


def identity_geometry():
    return jnp.concatenate(
        [jnp.eye(3, dtype=jnp.float32).reshape(9, 1), jnp.ones((2, 1), jnp.float32)], axis=0
    )


def cross_product(first_vec, second_vec):
    return jnp.stack(
        [
            first_vec[1] * second_vec[2] - first_vec[2] * second_vec[1],
            first_vec[2] * second_vec[0] - first_vec[0] * second_vec[2],
            first_vec[0] * second_vec[1] - first_vec[1] * second_vec[0],
        ]
    )


def device_rhs(state, extended, link_codes, orient_codes, derived, tables):
    slopes, lift_alt, node_picks, node_perms = tables
    components = state.shape[0]
    elements = state.shape[2]
    face_nodes = len(node_perms[0])
    interior = extended[:, :, : 4 * elements].reshape(components, face_nodes, 4, elements)
    gathered = extended[:, :, link_codes]
    picked = gathered
    for turn_id in range(6):
        picked = jnp.where(
            (orient_codes == turn_id)[None, None], gathered[:, node_perms[turn_id]], picked
        )
    wall_signs = jnp.array([1.0, 1.0, 1.0, -1.0, -1.0, -1.0], jnp.float32)[:, None, None, None]
    outside = jnp.where((orient_codes == 6)[None, None], wall_signs * interior, picked)
    inverse_jac = derived[:9].reshape(3, 3, elements)
    normals = derived[9:21].reshape(3, 1, 4, elements)
    lengths = derived[21:25]
    permittivity = derived[25]
    permeability = derived[26]
    local_slopes = jnp.einsum("amn,fnk->afmk", slopes, state, precision=highest)
    gradients = [
        inverse_jac[0, axis_id][None, None] * local_slopes[0]
        + inverse_jac[1, axis_id][None, None] * local_slopes[1]
        + inverse_jac[2, axis_id][None, None] * local_slopes[2]
        for axis_id in range(3)
    ]
    curl_h = jnp.stack(
        [
            gradients[1][2] - gradients[2][1],
            gradients[2][0] - gradients[0][2],
            gradients[0][1] - gradients[1][0],
        ]
    )
    curl_e = jnp.stack(
        [
            gradients[1][5] - gradients[2][4],
            gradients[2][3] - gradients[0][5],
            gradients[0][4] - gradients[1][3],
        ]
    )
    jump_all = outside - interior
    jump_h = jump_all[:3]
    jump_e = jump_all[3:]
    along_h = jnp.sum(normals * jump_h, axis=0)
    along_e = jnp.sum(normals * jump_e, axis=0)
    flux_h = -cross_product(normals, jump_e) + jump_h - normals * along_h
    flux_e = cross_product(normals, jump_h) + jump_e - normals * along_e
    scaled = jnp.concatenate([flux_h, flux_e], axis=0) * (0.5 * lengths)[None, None]
    lifted = jnp.einsum(
        "nc,fck->fnk",
        lift_alt,
        scaled.reshape(components, 4 * face_nodes, elements),
        precision=highest,
    )
    change_h = (lifted[:3] - curl_e) / permeability
    change_e = (curl_h + lifted[3:]) / permittivity
    return jnp.concatenate([change_h, change_e], axis=0)


def shards(fields, geometry, migrate_list, trace_list, face_link, face_orient):
    tables = dg_tables()
    node_picks = tables[2]
    face_nodes = len(tables[3][0])
    components = fields.shape[0]
    node_count = fields.shape[1]
    old_count = fields.shape[2]
    field_rows = components * node_count
    carried = derive_geometry(geometry)
    fallback = derive_geometry(identity_geometry())
    payload = jnp.concatenate([fields.reshape(field_rows, old_count), carried], axis=0)
    default_column = jnp.concatenate([jnp.zeros((field_rows, 1), jnp.float32), fallback], axis=0)
    send_slots = migrate_list[0]
    parcel = jnp.where(
        (send_slots >= 0)[None], payload[:, jnp.maximum(send_slots, 0)], default_column[:, :, None]
    )
    arrived = lax.all_to_all(parcel, "slab", split_axis=1, concat_axis=1, tiled=True)
    new_count = arrived.shape[1] * arrived.shape[2]
    arrived = arrived.reshape(arrived.shape[0], new_count)
    state0 = arrived[:field_rows].reshape(components, node_count, new_count)
    derived = arrived[field_rows:]
    own_list = trace_list[0]

    def section_rhs(current):
        face_values = current[:, node_picks, :].reshape(components, face_nodes, 4 * new_count)
        outgoing = face_values[:, :, own_list]
        incoming = lax.all_to_all(outgoing, "sub", split_axis=2, concat_axis=2, tiled=True)
        extended = jnp.concatenate(
            [face_values, incoming.reshape(components, face_nodes, -1)], axis=2
        )
        return device_rhs(current, extended, face_link, face_orient, derived, tables)

    first_res = time_step * section_rhs(state0)
    middle = state0 + section_b1 * first_res
    second_res = section_a2 * first_res + time_step * section_rhs(middle)
    return (middle + section_b2 * second_res, second_res)


def solution(mesh):
    return jax.shard_map(
        shards,
        mesh=mesh,
        in_specs=(
            P(None, None, ("slab", "sub")),
            P(None, ("slab", "sub")),
            P(("slab", "sub"), None, None),
            P(("slab", "sub"), None, None),
            P(None, ("slab", "sub")),
            P(None, ("slab", "sub")),
        ),
        out_specs=(P(None, None, ("slab", "sub")), P(None, None, ("slab", "sub"))),
        check_vma=False,
    )
```

profile of v0, /device:TPU:2, one launch (start us, length us, event | category | flops | bytes accessed | tf_op | source)
XLA Modules:
  0.0 171.2 jit_solution(10390858577449532124)
XLA Ops:
  7.2 1.7 gather_fusion
  9.7 1.3 reshape.374
  11.0 15.5 %all-to-all-start = ((f32[32,1,1764]{2,1,0:T(1,128)}), f32[32,1,1764]{2,1,0:T(1,128)S(1)}, u32[]{:S(2)}, u32[]{:S(2)}) async-start(f32[32,1,1764]{2,1,0:T(1,128)} %reshape.374), calls=%async_computation | async-start | bytes 458752 | tf_op jit(solution)/shard_map/all_to_all | solution.py:268
  31.5 16.4 %all-to-all-done = f32[32,1,1764]{2,1,0:T(1,128)S(1)} async-done(((f32[32,1,1764]{2,1,0:T(1,128)}), f32[32,1,1764]{2,1,0:T(1,128)S(1)}, u32[]{:S(2)}, u32[]{:S(2)}) %all-to-all-start) | async-done | bytes 225824 | tf_op jit(solution)/shard_map/all_to_all | solution.py:268
  48.4 1.2 reduce.25
  51.5 1.3 slice_multiply_fusion
  54.4 4.2 %copy.307 = f32[6,10,1536]{1,0,2:T(8,128)} copy(f32[6,10,1536]{2,1,0:T(8,128)S(1)} %reshape.192) | data formatting | bytes 737280 | tf_op jit(solution)/shard_map/reshape | solution.py:276
  58.6 3.6 %gather_fusion.2 = f32[256,6,10]{2,1,0:T(8,128)S(1)} fusion(f32[6,10,1536]{1,0,2:T(8,128)} %copy.307, s32[1024]{0:T(1024)S(1)} %pad_clamp_fusion.7), kind=kCustom, calls=%fused_computation.2 | custom fusion | bytes 123904 | tf_op jit(solution)/shard_map/gather | solution.py:277
  63.0 0.9 reshape.376
  64.0 7.5 %all-to-all-start.1 = ((f32[16,1,960]{2,1,0:T(1,128)}), f32[16,1,960]{2,1,0:T(1,128)S(1)}, u32[]{:S(2)}, u32[]{:S(2)}) async-start(f32[16,1,960]{2,1,0:T(1,128)} %reshape.376), calls=%async_computation.1 | async-start | bytes 131072 | tf_op jit(solution)/shard_map/all_to_all | solution.py:278
  71.4 1.2 copy.318
  74.3 1.3 copy.311
  75.7 1.3 copy.299
  77.7 1.3 copy.312
  83.4 6.9 %pad_maximum_fusion = f32[6,10,1792]{1,0,2:T(8,128)} fusion(f32[6,10,256]{1,0,2:T(8,128)S(1)} %bitcast.195, f32[6,10,1536]{1,0,2:T(8,128)} %copy.307), kind=kLoop, calls=%fused_computation.19 | loop fusion | flops 107520 | bytes 860160 | tf_op jit(solution)/shard_map/concatenate | solution.py:279
  90.3 7.7 %gather_fusion.3 = f32[1536,6,10]{2,1,0:T(8,128)} fusion(f32[6,10,1792]{1,0,2:T(8,128)} %pad_maximum_fusion, s32[2048]{0:T(1024)S(1)} %copy-done.13), kind=kCustom, calls=%fused_computation.3 | custom fusion | bytes 743424 | tf_op jit(solution)/shard_map/gather | solution.py:199
  98.0 4.2 %copy.348 = f32[4,384,6,10]{1,0,2,3:T(4,128)S(1)} copy(f32[4,384,6,10]{3,2,1,0:T(8,128)} %bitcast.194) | data formatting | bytes 737280 | tf_op jit(solution)/shard_map/gather | solution.py:199
  104.1 1.0 gather_fusion.7
  107.0 1.6 gather_fusion.4
  108.7 1.4 fusion.17
  112.8 4.2 %copy.329 = f32[6,10,1536]{1,0,2:T(8,128)} copy(f32[6,10,1536]{2,1,0:T(8,128)S(1)} %reshape.195) | data formatting | bytes 737280 | tf_op jit(solution)/shard_map/reshape | solution.py:276
  117.0 3.5 %gather_fusion.11 = f32[256,6,10]{2,1,0:T(8,128)S(1)} fusion(f32[6,10,1536]{1,0,2:T(8,128)} %copy.329, s32[1024]{0:T(1024)S(1)} %pad_clamp_fusion.7), kind=kCustom, calls=%fused_computation.11 | custom fusion | bytes 123904 | tf_op jit(solution)/shard_map/gather | solution.py:277
  122.3 7.2 %all-to-all-start.2 = ((f32[16,1,960]{2,1,0:T(1,128)}), f32[16,1,960]{2,1,0:T(1,128)S(1)}, u32[]{:S(2)}, u32[]{:S(2)}) async-start(f32[16,1,960]{2,1,0:T(1,128)} %reshape.378), calls=%async_computation.2 | async-start | bytes 131072 | tf_op jit(solution)/shard_map/all_to_all | solution.py:278
  130.4 5.4 %all-to-all-done.2 = f32[16,1,960]{2,1,0:T(1,128)S(1)} async-done(((f32[16,1,960]{2,1,0:T(1,128)}), f32[16,1,960]{2,1,0:T(1,128)S(1)}, u32[]{:S(2)}, u32[]{:S(2)}) %all-to-all-start.2) | async-done | bytes 61472 | tf_op jit(solution)/shard_map/all_to_all | solution.py:278
  137.6 6.9 %pad_maximum_fusion.1 = f32[6,10,1792]{1,0,2:T(8,128)} fusion(f32[6,10,256]{1,0,2:T(8,128)S(1)} %bitcast.196, f32[6,10,1536]{1,0,2:T(8,128)} %copy.329), kind=kLoop, calls=%fused_computation.20 | loop fusion | flops 107520 | bytes 860160 | tf_op jit(solution)/shard_map/concatenate | solution.py:279
  144.5 7.7 %gather_fusion.12 = f32[1536,6,10]{2,1,0:T(8,128)} fusion(f32[6,10,1792]{1,0,2:T(8,128)} %pad_maximum_fusion.1, s32[2048]{0:T(1024)S(1)} %copy-done.14), kind=kCustom, calls=%fused_computation.12 | custom fusion | bytes 743424 | tf_op jit(solution)/shard_map/gather | solution.py:199
  152.2 4.2 %copy.352 = f32[4,384,6,10]{1,0,2,3:T(4,128)S(1)} copy(f32[4,384,6,10]{3,2,1,0:T(8,128)} %bitcast.176) | data formatting | bytes 737280 | tf_op jit(solution)/shard_map/gather | solution.py:199
  156.5 4.2 %copy.353 = f32[4,384,6,10]{1,0,3,2:T(4,128)S(1)} copy(f32[4,384,6,10]{3,2,1,0:T(8,128)} %bitcast.177) | data formatting | bytes 737280 | tf_op jit(solution)/shard_map/gather | solution.py:199
  161.7 1.0 gather_fusion.16
  164.6 1.6 gather_fusion.13
  167.2 1.4 fusion.10
  169.2 1.1 convolution_bitcast_fusion.2
  (233 shorter events, 39.4 us)
Async XLA Ops:
  7.1 19.4 %copy-start.57 = (s32[40]{0:T(128)S(1)}, s32[40]{0:T(128)}, u32[]{:S(2)}) copy-start(s32[40]{0:T(128)} %constant.108) | copy-start | bytes 484
  7.1 19.4 %copy-start.45 = (s32[1,16,16]{2,1,0:T(8,128)S(1)}, s32[1,16,16]{2,1,0:T(8,128)}, u32[]{:S(2)}) copy-start(s32[1,16,16]{2,1,0:T(8,128)} %param.29) | copy-start | bytes 3076
  7.1 19.5 %copy-start.47 = (s32[4,384]{1,0:T(4,128)S(1)}, s32[4,384]{1,0:T(4,128)}, u32[]{:S(2)}) copy-start(s32[4,384]{1,0:T(4,128)} %param.30) | copy-start | bytes 18436
  7.1 20.1 %copy-start.56 = (s32[10]{0:T(128)S(1)}, s32[10]{0:T(128)}, u32[]{:S(2)}) copy-start(s32[10]{0:T(128)} %constant.113) | copy-start | bytes 124
  7.1 20.7 %copy-start.55 = (s32[10]{0:T(128)S(1)}, s32[10]{0:T(128)}, u32[]{:S(2)}) copy-start(s32[10]{0:T(128)} %constant.112) | copy-start | bytes 124
  7.2 21.3 %copy-start.54 = (s32[10]{0:T(128)S(1)}, s32[10]{0:T(128)}, u32[]{:S(2)}) copy-start(s32[10]{0:T(128)} %constant.111) | copy-start | bytes 124
  7.2 21.9 %copy-start.53 = (s32[10]{0:T(128)S(1)}, s32[10]{0:T(128)}, u32[]{:S(2)}) copy-start(s32[10]{0:T(128)} %constant.110) | copy-start | bytes 124
  7.2 22.5 %copy-start.52 = (s32[10]{0:T(128)S(1)}, s32[10]{0:T(128)}, u32[]{:S(2)}) copy-start(s32[10]{0:T(128)} %constant.109) | copy-start | bytes 124
  7.2 23.7 %copy-start.48 = (s32[4,384]{1,0:T(4,128)S(1)}, s32[4,384]{1,0:T(4,128)}, u32[]{:S(2)}) copy-start(s32[4,384]{1,0:T(4,128)} %param.31) | copy-start | bytes 18436
  11.0 36.9 %all-to-all-start = ((f32[32,1,1764]{2,1,0:T(1,128)}), f32[32,1,1764]{2,1,0:T(1,128)S(1)}, u32[]{:S(2)}, u32[]{:S(2)}) async-start(f32[32,1,1764]{2,1,0:T(1,128)} %reshape.374), calls=%async_computation | async-start | bytes 458752 | tf_op jit(solution)/shard_map/all_to_all | solution.py:268
  26.5 27.8 %copy-start.46 = (s32[1024]{0:T(1024)}, s32[1024]{0:T(1024)S(1)}, u32[]{:S(2)}) copy-start(s32[1024]{0:T(1024)S(1)} %pad_clamp_fusion.8) | copy-start | bytes 12292
  54.3 18.6 %copy-start.5 = (f32[3,20,20,1]{2,1,3,0:T(8,128)S(1)}, f32[3,20,20,1]{2,1,3,0:T(8,128)}, u32[]{:S(2)}) copy-start(f32[3,20,20,1]{2,1,3,0:T(8,128)} %constant.122) | copy-start | bytes 14404
  58.6 21.6 %copy-start = (f32[4,32,12]{0,2,1:T(8,128)S(1)}, f32[4,32,12]{0,2,1:T(8,128)}, u32[]{:S(2)}) copy-start(f32[4,32,12]{0,2,1:T(8,128)} %get-tuple-element.25) | copy-start | bytes 18436
  64.0 17.6 %all-to-all-start.1 = ((f32[16,1,960]{2,1,0:T(1,128)}), f32[16,1,960]{2,1,0:T(1,128)S(1)}, u32[]{:S(2)}, u32[]{:S(2)}) async-start(f32[16,1,960]{2,1,0:T(1,128)} %reshape.376), calls=%async_computation.1 | async-start | bytes 131072 | tf_op jit(solution)/shard_map/all_to_all | solution.py:278
  75.7 34.5 %copy-start.7 = (f32[4,384]{1,0:T(4,128)}, f32[4,384]{1,0:T(4,128)S(1)}, u32[]{:S(2)}) copy-start(f32[4,384]{1,0:T(4,128)S(1)} %mul.239) | copy-start | bytes 18436
  90.3 18.4 %copy-start.31 = (pred[4,384]{1,0:T(4,128)(4,1)S(1)}, pred[4,384]{1,0:T(4,128)(4,1)}, u32[]{:S(2)}) copy-start(pred[4,384]{1,0:T(4,128)(4,1)} %get-tuple-element.77) | copy-start | bytes 4612
  90.3 18.4 %copy-start.33 = (pred[4,384]{1,0:T(4,128)(4,1)S(1)}, pred[4,384]{1,0:T(4,128)(4,1)}, u32[]{:S(2)}) copy-start(pred[4,384]{1,0:T(4,128)(4,1)} %get-tuple-element.78) | copy-start | bytes 4612
  90.3 18.4 %copy-start.35 = (pred[4,384]{1,0:T(4,128)(4,1)S(1)}, pred[4,384]{1,0:T(4,128)(4,1)}, u32[]{:S(2)}) copy-start(pred[4,384]{1,0:T(4,128)(4,1)} %get-tuple-element.79) | copy-start | bytes 4612
  90.3 18.4 %copy-start.37 = (pred[4,384]{1,0:T(4,128)(4,1)S(1)}, pred[4,384]{1,0:T(4,128)(4,1)}, u32[]{:S(2)}) copy-start(pred[4,384]{1,0:T(4,128)(4,1)} %get-tuple-element.80) | copy-start | bytes 4612
  90.3 18.4 %copy-start.39 = (pred[4,384]{1,0:T(4,128)(4,1)S(1)}, pred[4,384]{1,0:T(4,128)(4,1)}, u32[]{:S(2)}) copy-start(pred[4,384]{1,0:T(4,128)(4,1)} %get-tuple-element.81) | copy-start | bytes 4612
  90.3 18.4 %copy-start.41 = (pred[4,384]{1,0:T(4,128)(4,1)S(1)}, pred[4,384]{1,0:T(4,128)(4,1)}, u32[]{:S(2)}) copy-start(pred[4,384]{1,0:T(4,128)(4,1)} %get-tuple-element.82) | copy-start | bytes 4612
  90.3 18.4 %copy-start.43 = (pred[4,384]{1,0:T(4,128)(4,1)S(1)}, pred[4,384]{1,0:T(4,128)(4,1)}, u32[]{:S(2)}) copy-start(pred[4,384]{1,0:T(4,128)(4,1)} %get-tuple-element.83) | copy-start | bytes 4612
  90.3 18.4 %copy-start.50 = (f32[6]{0:T(128)S(1)}, f32[6]{0:T(128)}, u32[]{:S(2)}) copy-start(f32[6]{0:T(128)} %constant.76.clone) | copy-start | bytes 76
  98.0 12.2 %copy-start.9 = (f32[4,384]{1,0:T(4,128)S(1)}, f32[4,384]{1,0:T(4,128)}, u32[]{:S(2)}) copy-start(f32[4,384]{1,0:T(4,128)} %mul.234) | copy-start | bytes 18436
  98.0 12.2 %copy-start.11 = (f32[4,384]{1,0:T(4,128)S(1)}, f32[4,384]{1,0:T(4,128)}, u32[]{:S(2)}) copy-start(f32[4,384]{1,0:T(4,128)} %mul.483) | copy-start | bytes 18436
  112.6 16.9 %copy-start.19 = (f32[384]{0:T(512)S(1)}, f32[384]{0:T(512)}, u32[]{:S(2)}) copy-start(f32[384]{0:T(512)} %copy-done.18) | copy-start | bytes 4612
  112.6 16.9 %copy-start.21 = (f32[384]{0:T(512)S(1)}, f32[384]{0:T(512)}, u32[]{:S(2)}) copy-start(f32[384]{0:T(512)} %copy-done.20) | copy-start | bytes 4612
  112.6 16.9 %copy-start.23 = (f32[384]{0:T(512)S(1)}, f32[384]{0:T(512)}, u32[]{:S(2)}) copy-start(f32[384]{0:T(512)} %copy-done.22) | copy-start | bytes 4612
  112.7 16.9 %copy-start.25 = (f32[384]{0:T(512)S(1)}, f32[384]{0:T(512)}, u32[]{:S(2)}) copy-start(f32[384]{0:T(512)} %copy-done.24) | copy-start | bytes 4612
  122.3 13.5 %all-to-all-start.2 = ((f32[16,1,960]{2,1,0:T(1,128)}), f32[16,1,960]{2,1,0:T(1,128)S(1)}, u32[]{:S(2)}, u32[]{:S(2)}) async-start(f32[16,1,960]{2,1,0:T(1,128)} %reshape.378), calls=%async_computation.2 | async-start | bytes 131072 | tf_op jit(solution)/shard_map/all_to_all | solution.py:278
  156.5 12.2 %copy-start.8 = (f32[4,384]{1,0:T(4,128)S(1)}, f32[4,384]{1,0:T(4,128)}, u32[]{:S(2)}) copy-start(f32[4,384]{1,0:T(4,128)} %copy-done.7) | copy-start | bytes 18436
  156.5 12.2 %copy-start.10 = (f32[4,384]{1,0:T(4,128)S(1)}, f32[4,384]{1,0:T(4,128)}, u32[]{:S(2)}) copy-start(f32[4,384]{1,0:T(4,128)} %mul.234) | copy-start | bytes 18436
  (29 other events, 212.6 us)
where the time goes:
time: 172 us; the launch traced here: 171 us
  local copies, waits for them, and re-layouts  83.9 us (49%)
  starting transfers between devices  30.2 us (18%)
  other arithmetic  29.5 us (17%)
  waiting for transfers between devices  21.7 us (13%)
  matrix products  3.8 us (2%)
  between operations  2 us (1%)
    gather x5, local copies, waits for them, and re-layouts, device_rhs(): gathered = extended[:, :, link_codes]  28 us
    all_to_all x1, waiting for transfers between devices, shards(): lax.all_to_all(parcel, 'slab', split_axis=1, concat_axis=1, tiled=True)  16.4 us
    all_to_all x1, starting transfers between devices, shards(): lax.all_to_all(parcel, 'slab', split_axis=1, concat_axis=1, tiled=True)  15.5 us
    all_to_all x2, starting transfers between devices, section_rhs(): lax.all_to_all(outgoing, 'sub', split_axis=2, concat_axis=2, tiled=True)  14.7 us
    concatenate x2, other arithmetic, section_rhs(): jnp.concatenate([face_values, incoming.reshape(components, face_nodes, -1...  13.8 us
    gather x12, local copies, waits for them, and re-layouts, device_rhs(): gathered[:, node_perms[turn_id]]  12.7 us
    gather x4, local copies, waits for them, and re-layouts, section_rhs(): outgoing = face_values[:, :, own_list]  8.79 us
    reshape x4, local copies, waits for them, and re-layouts, section_rhs(): current[:, node_picks, :].reshape(components, face_nodes, 4 * new_count)  8.44 us
  transfers between devices with their start and end apart: 3, of which 2 were waited for; matrix products, arithmetic and copies ran while one was open for 9% of the time, Pallas kernels for 0%

commit v1 on v0

v1 whole, which is shorter than its diff:
```python
import math

import jax
import jax.numpy as jnp
import ml_dtypes
import numpy as np
from jax import lax
from jax.experimental import pallas as pl
from jax.experimental.pallas import tpu as pltpu
from jax.sharding import PartitionSpec as P

time_step = 0.004
section_a2 = -0.4178904745
section_b1 = 0.1496590219993
section_b2 = 0.3792103129999
coordinate_perms = ((0, 1, 2), (1, 2, 0), (2, 0, 1), (0, 2, 1), (2, 1, 0), (1, 0, 2))
components = 6
node_count = 20
face_nodes = 10
faces = 4
old_count = 256
slots = 12
slabs = 32
subs = 16
traces = 16
new_count = slots * slabs
column_count = faces * new_count
remote_count = subs * traces
lane = 128
tiles = new_count // lane
block_rows = slots + 1


def volume_triples():
    result_list = []
    for first_idx in range(4):
        for second_idx in range(4 - first_idx):
            for third_idx in range(4 - first_idx - second_idx):
                result_list.append((first_idx, second_idx, third_idx))
    return result_list


def planar_pairs():
    result_list = []
    for first_idx in range(4):
        for second_idx in range(4 - first_idx):
            result_list.append((first_idx, second_idx))
    return result_list


def monomial_matrix(points, powers):
    result_rows = []
    for point_item in points:
        row_values = []
        for power_item in powers:
            product_value = 1.0
            for axis_id in range(len(power_item)):
                product_value = product_value * point_item[axis_id] ** power_item[axis_id]
            row_values.append(product_value)
        result_rows.append(row_values)
    return result_rows


def mat_mul(left_rows, right_rows):
    inner_count = len(right_rows)
    col_count = len(right_rows[0])
    return [
        [
            sum((left_row[k_id] * right_rows[k_id][c_id] for k_id in range(inner_count)))
            for c_id in range(col_count)
        ]
        for left_row in left_rows
    ]


def transposed(matrix_rows):
    return [list(row_item) for row_item in zip(*matrix_rows)]


def invert(matrix_rows):
    order = len(matrix_rows)
    work_rows = [
        list(matrix_rows[r_id]) + [1.0 if r_id == c_id else 0.0 for c_id in range(order)]
        for r_id in range(order)
    ]
    for col_id in range(order):
        pivot_row = max(range(col_id, order), key=lambda r_id: abs(work_rows[r_id][col_id]))
        work_rows[col_id], work_rows[pivot_row] = (work_rows[pivot_row], work_rows[col_id])
        pivot_value = work_rows[col_id][col_id]
        work_rows[col_id] = [value / pivot_value for value in work_rows[col_id]]
        for r_id in range(order):
            if r_id != col_id:
                factor = work_rows[r_id][col_id]
                if factor != 0.0:
                    work_rows[r_id] = [
                        work_rows[r_id][c_id] - factor * work_rows[col_id][c_id]
                        for c_id in range(2 * order)
                    ]
    return [row_item[order:] for row_item in work_rows]


def moment_matrix(powers, extra_dim):
    total_terms = len(powers)
    result_matrix = [[0.0] * total_terms for _ in range(total_terms)]
    for row_id in range(total_terms):
        for col_id in range(total_terms):
            joined = [
                powers[row_id][a_id] + powers[col_id][a_id] for a_id in range(len(powers[row_id]))
            ]
            numerator = 1.0
            for exponent in joined:
                numerator = numerator * math.factorial(exponent)
            result_matrix[row_id][col_id] = numerator / math.factorial(sum(joined) + extra_dim)
    return result_matrix


def dg_tables():
    triples = volume_triples()
    points = [tuple((value / 3.0 for value in triple)) for triple in triples]
    inverse = invert(monomial_matrix(points, triples))
    slopes = []
    for axis_id in range(3):
        lowered = [
            tuple(
                (max(triple[a_id] - 1, 0) if a_id == axis_id else triple[a_id] for a_id in range(3))
            )
            for triple in triples
        ]
        base_rows = monomial_matrix(points, lowered)
        slope_values = [
            [triples[c_id][axis_id] * base_rows[r_id][c_id] for c_id in range(20)]
            for r_id in range(20)
        ]
        slopes.append(mat_mul(slope_values, inverse))
    volume_mass = mat_mul(mat_mul(transposed(inverse), moment_matrix(triples, 3)), inverse)
    planar = planar_pairs()
    face_points = [tuple((value / 3.0 for value in pair_item)) for pair_item in planar]
    face_inverse = invert(monomial_matrix(face_points, planar))
    face_mass = mat_mul(mat_mul(transposed(face_inverse), moment_matrix(planar, 2)), face_inverse)
    face_axes = ((0, 1), (0, 2), (0, 1), (1, 2))
    face_mask = [[0] * 10 for _ in range(4)]
    for face_id in range(4):
        for node_id, triple in enumerate(triples):
            on_face = (
                triple[2] == 0,
                triple[1] == 0,
                triple[0] + triple[1] + triple[2] == 3,
                triple[0] == 0,
            )[face_id]
            if on_face:
                key_pair = (triple[face_axes[face_id][0]], triple[face_axes[face_id][1]])
                face_mask[face_id][planar.index(key_pair)] = node_id
    surface = [[0.0] * 40 for _ in range(20)]
    for face_id in range(4):
        for row_id in range(10):
            for col_id in range(10):
                surface[face_mask[face_id][row_id]][face_id * 10 + col_id] += face_mass[row_id][
                    col_id
                ]
    lifting = mat_mul(invert(volume_mass), surface)
    lift_alt = [
        [lifting[n_id][f_id * 10 + j_id] for j_id in range(10) for f_id in range(4)]
        for n_id in range(20)
    ]
    node_perms = []
    for turn_id in range(6):
        perm_row = []
        for pair_item in planar:
            triple_face = (pair_item[0], pair_item[1], 3 - pair_item[0] - pair_item[1])
            moved_triple = [triple_face[coordinate_perms[turn_id][axis_id]] for axis_id in range(3)]
            perm_row.append(planar.index((moved_triple[0], moved_triple[1])))
        node_perms.append(perm_row)
    node_picks = [face_mask[f_id][j_id] for j_id in range(10) for f_id in range(4)]
    return slopes, lifting, face_mask, node_perms


def bf16_pair(matrix):
    wide = np.asarray(matrix, np.float32)
    high = wide.astype(ml_dtypes.bfloat16)
    rest = (wide - high.astype(np.float32)).astype(ml_dtypes.bfloat16)
    return high, rest


slope_table, lift_table, face_mask, node_perms = dg_tables()


def slope_operand():
    stacked = np.zeros((80, 32), np.float64)
    for axis_id in range(3):
        first_row = axis_id * 24
        stacked[first_row : first_row + node_count, :node_count] = slope_table[axis_id]
    high, rest = bf16_pair(stacked)
    return jnp.asarray(np.concatenate([high, high, rest], axis=1))


def lift_operand():
    stacked = np.zeros((32, 48), np.float64)
    for face_id in range(faces):
        for node_id in range(face_nodes):
            for row_id in range(node_count):
                stacked[row_id, node_id * faces + face_id] = lift_table[row_id][
                    face_id * face_nodes + node_id
                ]
    high, rest = bf16_pair(stacked)
    return jnp.asarray(np.concatenate([high, high, rest], axis=1))


def select_operand():
    table = np.zeros((2, faces * 2 * lane, lane), np.float32)
    for half in range(2):
        for face_id in range(faces):
            for part_id in range(2):
                for node_id in range(face_nodes):
                    for comp_id in range(components):
                        row_id = (face_id * 2 + part_id) * lane
                        row_id += comp_id * node_count + face_mask[face_id][node_id]
                        table[half, row_id, half * 64 + node_id * components + comp_id] = 1.0
    return jnp.asarray(table.astype(ml_dtypes.bfloat16))


def split_two(value):
    high = value.astype(jnp.bfloat16)
    rest = (value - high.astype(jnp.float32)).astype(jnp.bfloat16)
    return high, rest


def split_three(value):
    high = value.astype(jnp.bfloat16)
    left = value - high.astype(jnp.float32)
    middle = left.astype(jnp.bfloat16)
    rest = (left - middle.astype(jnp.float32)).astype(jnp.bfloat16)
    return high, middle, rest


def dot_rows(left, right):
    return lax.dot_general(
        left, right, (((1,), (0,)), ((), ())), preferred_element_type=jnp.float32
    )


def dot_lanes(left, right):
    return lax.dot_general(
        left, right, (((1,), (1,)), ((), ())), preferred_element_type=jnp.float32
    )


def one_hot(mask):
    return jnp.where(mask, 1.0, 0.0).astype(jnp.bfloat16)


def face_of(codes):
    return sum((codes >= step * new_count).astype(jnp.int32) for step in range(1, faces))


def pack_kernel(fields_ref, geometry_ref, list_ref, out_ref, held_ref):
    field_rows = components * node_count
    for comp_id in range(components):
        held_ref[comp_id * node_count : (comp_id + 1) * node_count, :] = fields_ref[comp_id]
    held_ref[field_rows : field_rows + 11, :] = geometry_ref[...]
    held_ref[field_rows + 11 :, :] = jnp.zeros((13, old_count), jnp.float32)
    parts = jnp.concatenate(split_three(held_ref[...]), axis=1)
    parts = jnp.concatenate([parts, jnp.zeros((112, 3 * old_count), jnp.bfloat16)], axis=0)
    codes = list_ref[0]
    lanes = lax.broadcasted_iota(jnp.int32, (slabs, old_count), 1)
    picks = jnp.concatenate(
        [one_hot(codes[:, slot_id : slot_id + 1] == lanes) for slot_id in range(slots)], axis=0
    )
    moved = dot_lanes(jnp.concatenate([picks, picks, picks], axis=1), parts)
    short = lax.broadcasted_iota(jnp.int32, (slabs, lane), 1)
    diagonal = (short == field_rows) | (short == field_rows + 4)
    tail = jnp.zeros((slabs, lane), jnp.float32)
    for slot_id in range(slots):
        empty = codes[:, slot_id : slot_id + 1] < 0
        block = moved[slot_id * slabs : (slot_id + 1) * slabs]
        out_ref[pl.ds(slot_id, slabs, stride=block_rows), :] = jnp.where(
            empty & diagonal, 1.0, block[:, :lane]
        )
        ending = jnp.where(empty & (short < 3), 1.0, block[:, lane:])
        if slot_id:
            ending = pltpu.roll(ending, 3 * slot_id, 1)
        tail = tail + ending
    out_ref[pl.ds(slots, slabs, stride=block_rows), :] = tail


def trace_rows(values, codes, select_ref, trace_ref):
    high, rest = split_two(values)
    face = face_of(codes)
    element = codes - new_count * face
    lanes = lax.broadcasted_iota(jnp.int32, (subs, new_count), 1)
    picks = jnp.concatenate(
        [one_hot(element[:, idx : idx + 1] == lanes) for idx in range(traces)], axis=0
    )
    found = dot_lanes(picks, jnp.concatenate([high, rest], axis=0)).astype(jnp.bfloat16)
    face_rows = jnp.concatenate(
        [
            jnp.broadcast_to(face[:, idx : idx + 1], (subs, 2 * lane))
            for idx in range(traces)
        ],
        axis=0,
    )
    zeros = jnp.zeros(found.shape, jnp.float32)
    wide = found.astype(jnp.float32)
    spread = jnp.concatenate(
        [
            jnp.where(face_rows == face_id, wide, zeros).astype(jnp.bfloat16)
            for face_id in range(faces)
        ],
        axis=1,
    )
    half = remote_count // 2
    rows = dot_rows(spread[:half], select_ref[0]) + dot_rows(spread[half:], select_ref[1])
    for idx in range(traces // 2):
        trace_ref[pl.ds(idx, subs, stride=traces // 2), :] = rows[idx * subs : (idx + 1) * subs]


def unpack_kernel(
    came_ref, list_ref, select_ref, state_ref, derived_ref, trace_ref, rows_ref, tail_ref, main_ref
):
    field_rows = components * node_count
    tail = came_ref[pl.ds(slots, slabs, stride=block_rows), :]
    for slot_id in range(slots):
        rows_ref[pl.ds(slot_id, slabs, stride=slots), :] = came_ref[
            pl.ds(slot_id, slabs, stride=block_rows), :
        ]
        shifted = pltpu.roll(tail, lane - 3 * slot_id, 1) if slot_id else tail
        tail_ref[pl.ds(slot_id, slabs, stride=slots), :] = shifted
    main = jnp.transpose(rows_ref[...])
    trace_rows(main, list_ref[0], select_ref, trace_ref)
    main_ref[...] = main
    extra = jnp.transpose(tail_ref[...])[:8]
    for comp_id in range(components):
        state_ref[comp_id] = main_ref[comp_id * node_count : (comp_id + 1) * node_count, :]
    geo = [main_ref[field_rows + row_id : field_rows + row_id + 1, :] for row_id in range(8)]
    geo.append(extra[0:1])
    derived_ref[0:8, :] = main_ref[field_rows : field_rows + 8, :]
    derived_ref[8:9, :] = extra[0:1]
    derived_ref[9:10, :] = 1.0 / extra[1:2]
    derived_ref[10:11, :] = 1.0 / extra[2:3]
    total = None
    for axis_id in range(3):
        first, second, third = geo[axis_id], geo[3 + axis_id], geo[6 + axis_id]
        normal = 0.5 * jnp.concatenate([-third, -second, first + second + third, -first], axis=0)
        square = normal * normal
        total = square if total is None else total + square
        normal_rows = jnp.concatenate([normal, normal], axis=0)
        derived_ref[16 + 8 * axis_id : 24 + 8 * axis_id, :] = normal_rows
    length = jnp.sqrt(total)
    derived_ref[40:48, :] = jnp.concatenate([length, length], axis=0)
    inverse = 1.0 / length
    derived_ref[48:56, :] = jnp.concatenate([inverse, inverse], axis=0)


def oriented(planes, orient):
    masks = [orient == turn_id for turn_id in range(6)]
    result = []
    for node_id in range(face_nodes):
        sources = {}
        for turn_id in range(6):
            sources.setdefault(node_perms[turn_id][node_id], []).append(turn_id)
        value = None
        for source, turn_ids in sources.items():
            if value is None:
                value = planes[source]
                continue
            mask = masks[turn_ids[0]]
            for turn_id in turn_ids[1:]:
                mask = mask | masks[turn_id]
            value = jnp.where(mask, planes[source], value)
        result.append(value)
    return result


def lifted_flux(jump_ref, flux_ref, derived_ref, lift_ref):
    groups = faces * face_nodes // 8

    def jump_of(comp_id):
        rows = strided_load(jump_ref, comp_id, faces * face_nodes, 8)
        return rows.reshape(groups, 8, new_count)

    jump_h = [jump_of(comp_id) for comp_id in range(3)]
    jump_e = [jump_of(comp_id) for comp_id in range(3, 6)]
    normal = [derived_ref[16 + 8 * axis_id : 24 + 8 * axis_id, :][None] for axis_id in range(3)]
    length = derived_ref[40:48, :][None]
    inverse = derived_ref[48:56, :][None]

    def along(jump):
        total = normal[0] * jump[0] + normal[1] * jump[1] + normal[2] * jump[2]
        return total * inverse

    along_h = along(jump_h)
    along_e = along(jump_e)
    for axis_id in range(3):
        after, last = (axis_id + 1) % 3, (axis_id + 2) % 3
        cross_e = normal[after] * jump_e[last] - normal[last] * jump_e[after]
        cross_h = normal[after] * jump_h[last] - normal[last] * jump_h[after]
        flux_h = length * jump_h[axis_id] - normal[axis_id] * along_h - cross_e
        flux_e = length * jump_e[axis_id] - normal[axis_id] * along_e + cross_h
        for comp_id, value in ((axis_id, flux_h), (3 + axis_id, flux_e)):
            flux_ref[0:40, comp_id * new_count : (comp_id + 1) * new_count] = value.reshape(
                faces * face_nodes, new_count
            )
    flux_ref[40:48, :] = jnp.zeros((8, components * new_count), jnp.float32)
    high, rest = split_two(flux_ref[...])
    return dot_rows(lift_ref[...], jnp.concatenate([high, rest, high], axis=0))


def strided_load(ref, start, size, stride):
    return jnp.concatenate(
        [ref[tile, pl.ds(start, size, stride=stride), :] for tile in range(tiles)], axis=1
    )


def tiled_store(ref, rows, value):
    for tile in range(tiles):
        ref[tile, rows, :] = value[:, tile * lane : (tile + 1) * lane]


def tiled_load(ref, rows):
    return jnp.concatenate([ref[tile, rows, :] for tile in range(tiles)], axis=1)


def column_block(matrix, comp_id):
    return matrix[:24, comp_id * new_count : (comp_id + 1) * new_count]


def local_kernel(
    state_ref,
    derived_ref,
    link_ref,
    orient_ref,
    slope_ref,
    lift_ref,
    part_ref,
    nodes_ref,
    flat_ref,
    jump_ref,
    flux_ref,
):
    nodes_ref[...] = jnp.zeros(nodes_ref.shape, jnp.float32)
    flat_ref[node_count:32, :] = jnp.zeros((12, components * new_count), jnp.float32)
    for comp_id in range(components):
        current = state_ref[comp_id]
        tiled_store(nodes_ref, pl.ds(comp_id, node_count, stride=8), current)
        flat_ref[0:node_count, comp_id * new_count : (comp_id + 1) * new_count] = current
    stacked = jnp.concatenate(split_two(tiled_load(nodes_ref, slice(None))), axis=0)
    rows = lax.broadcasted_iota(jnp.int32, (new_count, new_count), 0)
    comp_rows = lax.broadcasted_iota(jnp.int32, (8, new_count), 0)
    wall_gain = jnp.where(comp_rows >= 3, -2.0, 0.0)
    for face_id in range(faces):
        link = link_ref[face_id : face_id + 1, :]
        orient = orient_ref[face_id : face_id + 1, :]
        owner = face_of(link)
        element = jnp.where(link < column_count, link - new_count * owner, -1)
        found = dot_rows(stacked, one_hot(rows == element))
        found = found[: 8 * node_count] + found[8 * node_count :]
        owner_masks = [owner == other for other in range(faces)]
        planes = []
        for node_id in range(face_nodes):
            value = None
            for other in range(faces):
                first_row = 8 * face_mask[other][node_id]
                plane = found[first_row : first_row + 8]
                value = plane if value is None else jnp.where(owner_masks[other], plane, value)
            planes.append(value)
        outside = oriented(planes, orient)
        wall = orient == 6
        for node_id in range(face_nodes):
            first_row = 8 * face_mask[face_id][node_id]
            inside = tiled_load(nodes_ref, slice(first_row, first_row + 8))
            jump = jnp.where(wall, wall_gain * inside, outside[node_id] - inside)
            target = 8 * (node_id * faces + face_id)
            tiled_store(jump_ref, slice(target, target + 8), jump)
    lifted = lifted_flux(jump_ref, flux_ref, derived_ref, lift_ref)
    high, rest = split_two(flat_ref[...])
    slopes = dot_rows(slope_ref[...], jnp.concatenate([high, rest, high], axis=0))
    inverse_jac = [
        [derived_ref[3 * row_id + axis_id : 3 * row_id + axis_id + 1, :] for axis_id in range(3)]
        for row_id in range(3)
    ]

    def gradient(axis_id, comp_id):
        columns = slice(comp_id * new_count, (comp_id + 1) * new_count)
        return (
            inverse_jac[0][axis_id] * slopes[0:24, columns]
            + inverse_jac[1][axis_id] * slopes[24:48, columns]
            + inverse_jac[2][axis_id] * slopes[48:72, columns]
        )

    inverse_eps = derived_ref[9:10, :]
    inverse_mu = derived_ref[10:11, :]
    for axis_id in range(3):
        after, last = (axis_id + 1) % 3, (axis_id + 2) % 3
        curl_h = gradient(after, last) - gradient(last, after)
        curl_e = gradient(after, 3 + last) - gradient(last, 3 + after)
        change_h = (column_block(lifted, axis_id) - curl_e) * inverse_mu
        change_e = (column_block(lifted, 3 + axis_id) + curl_h) * inverse_eps
        part_ref[axis_id] = change_h[:node_count]
        part_ref[3 + axis_id] = change_e[:node_count]


def remote_part(came_ref, link_ref, orient_ref, derived_ref, lift_ref, turned_ref, table_ref, jump_ref, flux_ref):
    turned_ref[...] = jnp.transpose(came_ref[...])
    table_ref[...] = jnp.zeros(table_ref.shape, jnp.float32)
    for half in range(2):
        for node_id in range(face_nodes):
            first_row = half * 64 + node_id * components
            table_ref[8 * node_id : 8 * node_id + components, half * lane : (half + 1) * lane] = (
                turned_ref[first_row : first_row + components, :]
            )
    stacked = jnp.concatenate(split_two(table_ref[...]), axis=0)
    rows = lax.broadcasted_iota(jnp.int32, (remote_count, new_count), 0)
    for face_id in range(faces):
        far = link_ref[face_id : face_id + 1, :] - column_count
        orient = orient_ref[face_id : face_id + 1, :]
        column = ((far >> 3) & 1) * lane + (far >> 4) * 8 + (far & 7)
        column = jnp.where((far >= 0) & (orient < 6), column, -1)
        found = dot_rows(stacked, one_hot(rows == column))
        found = found[: 8 * face_nodes] + found[8 * face_nodes :]
        planes = [found[8 * node_id : 8 * node_id + 8] for node_id in range(face_nodes)]
        outside = oriented(planes, orient)
        for node_id in range(face_nodes):
            target = 8 * (node_id * faces + face_id)
            tiled_store(jump_ref, slice(target, target + 8), outside[node_id])
    lifted = lifted_flux(jump_ref, flux_ref, derived_ref, lift_ref)
    inverse_eps = derived_ref[9:10, :]
    inverse_mu = derived_ref[10:11, :]
    changes = []
    for comp_id in range(components):
        scale = inverse_mu if comp_id < 3 else inverse_eps
        changes.append((column_block(lifted, comp_id) * scale)[:node_count])
    return changes


def first_kernel(
    came_ref,
    part_ref,
    state_ref,
    derived_ref,
    link_ref,
    orient_ref,
    lift_ref,
    list_ref,
    select_ref,
    residual_ref,
    middle_ref,
    trace_ref,
    turned_ref,
    table_ref,
    jump_ref,
    flux_ref,
    main_ref,
):
    changes = remote_part(
        came_ref, link_ref, orient_ref, derived_ref, lift_ref, turned_ref, table_ref, jump_ref, flux_ref
    )
    for comp_id in range(components):
        residual = time_step * (part_ref[comp_id] + changes[comp_id])
        middle = state_ref[comp_id] + section_b1 * residual
        residual_ref[comp_id] = residual
        middle_ref[comp_id] = middle
        main_ref[comp_id * node_count : (comp_id + 1) * node_count, :] = middle
    main_ref[components * node_count :, :] = jnp.zeros((8, new_count), jnp.float32)
    trace_rows(main_ref[...], list_ref[0], select_ref, trace_ref)


def second_kernel(
    came_ref,
    part_ref,
    middle_ref,
    first_ref,
    derived_ref,
    link_ref,
    orient_ref,
    lift_ref,
    advanced_ref,
    residual_ref,
    turned_ref,
    table_ref,
    jump_ref,
    flux_ref,
):
    changes = remote_part(
        came_ref, link_ref, orient_ref, derived_ref, lift_ref, turned_ref, table_ref, jump_ref, flux_ref
    )
    for comp_id in range(components):
        residual = section_a2 * first_ref[comp_id] + time_step * (
            part_ref[comp_id] + changes[comp_id]
        )
        residual_ref[comp_id] = residual
        advanced_ref[comp_id] = middle_ref[comp_id] + section_b2 * residual


def floats(*shape):
    return jax.ShapeDtypeStruct(shape, jnp.float32)


def scratch(*shape):
    return pltpu.VMEM(shape, jnp.float32)


def run(kernel, name, outs, scratches, operands, flops=10**8):
    return pl.pallas_call(
        kernel,
        name=name,
        out_shape=outs,
        scratch_shapes=scratches,
        compiler_params=pltpu.CompilerParams(vmem_limit_bytes=24 * 2**20),
        cost_estimate=pl.CostEstimate(flops=flops, bytes_accessed=10**6, transcendentals=0),
    )(*operands)


def shards(fields, geometry, migrate_list, trace_list, face_link, face_orient):
    slopes = slope_operand()
    lift = lift_operand()
    select = select_operand()
    state_shape = floats(components, node_count, new_count)
    trace_shape = floats(subs * traces // 2, lane)
    remote_scratch = [
        scratch(lane, lane),
        scratch(8 * face_nodes, remote_count),
        scratch(tiles, 8 * faces * face_nodes, lane),
        scratch(48, components * new_count),
    ]
    parcel = run(
        pack_kernel,
        "pack",
        floats(slabs * block_rows, lane),
        [scratch(144, old_count)],
        (fields, geometry, migrate_list),
    )
    arrived = lax.all_to_all(
        parcel.reshape(slabs, block_rows * lane), "slab", split_axis=0, concat_axis=0, tiled=True
    ).reshape(slabs * block_rows, lane)
    state, derived, outgoing = run(
        unpack_kernel,
        "unpack",
        (state_shape, floats(64, new_count), trace_shape),
        [scratch(new_count, lane), scratch(new_count, lane), scratch(lane, new_count)],
        (arrived, trace_list, select),
    )

    def local(current):
        return run(
            local_kernel,
            "local",
            state_shape,
            [
                scratch(tiles, 8 * node_count, lane),
                scratch(32, components * new_count),
                scratch(tiles, 8 * faces * face_nodes, lane),
                scratch(48, components * new_count),
            ],
            (current, derived, face_link, face_orient, slopes, lift),
        )

    def exchange(rows):
        blocks = rows.reshape(subs, traces // 2, lane)
        came = lax.all_to_all(blocks, "sub", split_axis=0, concat_axis=0, tiled=True)
        return came.reshape(subs * traces // 2, lane)

    incoming = exchange(outgoing)
    part = local(state)
    first_res, middle, outgoing = run(
        first_kernel,
        "first",
        (state_shape, state_shape, trace_shape),
        remote_scratch + [scratch(lane, new_count)],
        (incoming, part, state, derived, face_link, face_orient, lift, trace_list, select),
    )
    incoming = exchange(outgoing)
    part = local(middle)
    return run(
        second_kernel,
        "second",
        (state_shape, state_shape),
        remote_scratch,
        (incoming, part, middle, first_res, derived, face_link, face_orient, lift),
    )


def solution(mesh):
    return jax.shard_map(
        shards,
        mesh=mesh,
        in_specs=(
            P(None, None, ("slab", "sub")),
            P(None, ("slab", "sub")),
            P(("slab", "sub"), None, None),
            P(("slab", "sub"), None, None),
            P(None, ("slab", "sub")),
            P(None, ("slab", "sub")),
        ),
        out_specs=(P(None, None, ("slab", "sub")), P(None, None, ("slab", "sub"))),
        check_vma=False,
    )
```

time: 172 us -> 70 us (0.41)
  local copies, waits for them, and re-layouts: 83.9 us -> 2.48 us
  blocking collectives: 0 us -> 36 us
  other arithmetic: 29.5 us -> 0 us
  starting transfers between devices: 30.2 us -> 12.5 us
  waiting for transfers between devices: 21.7 us -> 9.7 us
  Pallas kernels: 0 us -> 8.24 us
  matrix products: 3.8 us -> 0 us
    gather x27 -> x0, local copies, waits for them, and re-layouts: 52.6 us -> none  [the longest x5 28 us: device_rhs(): gathered = extended[:, :, link_codes]]
    all_to_all x0 -> x1, blocking collectives: none -> 36 us  [shards(): lax.all_to_all(parcel.reshape(slabs, block_rows * lane), 'slab', split_ax...]
    all_to_all x3 -> x2, starting transfers between devices: 30.2 us -> 12.5 us  [exchange(): lax.all_to_all(blocks, 'sub', split_axis=0, concat_axis=0, tiled=True)]
    concatenate x2 -> x0, other arithmetic: 13.8 us -> none  [section_rhs(): jnp.concatenate([face_values, incoming.reshape(components, face_nodes, -1...]
    reshape x16 -> x0, local copies, waits for them, and re-layouts: 13.6 us -> none  [the longest x4 8.44 us: section_rhs(): current[:, node_picks, :].reshape(components, face_nodes, 4 * new_count)]
    all_to_all x3 -> x2, waiting for transfers between devices: 21.7 us -> 9.7 us  [exchange(): lax.all_to_all(blocks, 'sub', split_axis=0, concat_axis=0, tiled=True)]
    pallas_call x0 -> x6, Pallas kernels: none -> 8.24 us  [run(): pl.pallas_call(kernel, name=name, out_shape=outs, scratch_shapes=scratche...]
    slice x12 -> x0, local copies, waits for them, and re-layouts: 7.63 us -> none  [the longest x2 2.07 us: device_rhs(): inverse_jac = derived[:9].reshape(3, 3, elements)]
  transfers between devices with their start and end apart: 3 -> 2, of which waited for: 2 -> 2; matrix products, arithmetic and copies ran while one was open for 9% -> 0% of each run, Pallas kernels for 0% -> 4%
where the time goes in v1:
time: 70 us; the launch traced here: 69.5 us
  blocking collectives  36 us (51%)
  starting transfers between devices  12.5 us (18%)
  waiting for transfers between devices  9.7 us (14%)
  Pallas kernels  8.24 us (12%)
  local copies, waits for them, and re-layouts  2.48 us (4%)
    all_to_all x1, blocking collectives, shards(): lax.all_to_all(parcel.reshape(slabs, block_rows * lane), 'slab', split_ax...  36 us
    all_to_all x2, starting transfers between devices, exchange(): lax.all_to_all(blocks, 'sub', split_axis=0, concat_axis=0, tiled=True)  12.5 us
    all_to_all x2, waiting for transfers between devices, exchange(): lax.all_to_all(blocks, 'sub', split_axis=0, concat_axis=0, tiled=True)  9.7 us
    pallas_call x6, Pallas kernels, run(): pl.pallas_call(kernel, name=name, out_shape=outs, scratch_shapes=scratche...  8.24 us
    unnamed x17, local copies, waits for them, and re-layouts  2.48 us
  transfers between devices with their start and end apart: 2, of which 2 were waited for; matrix products, arithmetic and copies ran while one was open for 0% of the time, Pallas kernels for 4%

profile of v1, /device:TPU:2, one launch (start us, length us, event | category | flops | bytes accessed | tf_op | source)
XLA Modules:
  0.0 69.5 jit_solution(807199205360918960)
XLA Ops:
  0.6 0.0 copy-start
  0.6 0.8 %copy.12.list_ref = s32[1,32,12]{2,1,0:T(8,128)S(1)} copy(s32[1,32,12]{1,0,2:T(1,128)} %param.11) | data formatting | bytes 3072 | tf_op args[2]
  1.5 0.0 copy-start.2
  1.5 0.9 %copy-done.2 = f32[6,20,256]{2,1,0:T(8,128)S(1)} copy-done((f32[6,20,256]{2,1,0:T(8,128)S(1)}, f32[6,20,256]{2,1,0:T(8,128)}, u32[]{:S(2)}) %copy-start.2) | copy-done | bytes 122904
  2.4 0.0 copy-start.7
  2.4 0.7 %copy-done.7 = f32[11,256]{1,0:T(8,128)S(1)} copy-done((f32[11,256]{1,0:T(8,128)S(1)}, f32[11,256]{1,0:T(8,128)}, u32[]{:S(2)}) %copy-start.7) | copy-done | bytes 11288
  3.1 0.4 pack.1
  3.5 0.0 copy-start.6
  3.5 36.0 %all_to_all.19 = f32[32,1,1664]{2,1,0:T(1,128)S(1)} all-to-all(f32[32,1,1664]{2,1,0:T(1,128)S(1)} %bitcast.6), channel_id=1, replica_groups=mesh['slab'=32,'sub'=16] {'slab'}, dimensions={0} | all-to-all | bytes 425984 | tf_op jit(solution)/shard_map/all_to_all | solution.py:631
  39.5 0.0 copy-done
  39.5 0.0 copy-done.6
  39.5 1.4 %unpack.1 = (f32[6,20,384]{2,1,0:T(8,128)S(1)}, f32[64,384]{1,0:T(8,128)S(1)}, f32[128,128]{1,0:T(8,128)}) custom-call(f32[416,128]{1,0:T(8,128)S(1)} %bitcast.7, s32[1,16,16]{2,1,0:T(8,128)S(1)} %copy-done.6, bf16[2,1024,128]{2,1,0:T(8,128)(2,1)S(1)} %copy-done), custom_call_target="tpu_custom_call" | custom-call | flops 100000000 | bytes 1000000 | tf_op jit(solution)/shard_map/unpack/pallas_call | solution.py:602
  40.9 0.0 copy-start.1
  40.9 0.0 copy-start.3
  40.9 0.0 copy-start.4
  40.9 0.0 copy-start.5
  40.9 7.6 %all-to-all-start.1 = ((f32[16,8,128]{2,1,0:T(8,128)}), f32[16,8,128]{2,1,0:T(8,128)S(1)}, u32[]{:S(2)}, u32[]{:S(2)}) async-start(f32[16,8,128]{2,1,0:T(8,128)} %bitcast.2), calls=%async_computation.1 | async-start | bytes 131072 | tf_op jit(solution)/shard_map/all_to_all | solution.py:658
  48.5 0.0 copy-done.1
  48.5 0.0 copy-done.3
  48.5 0.0 copy-done.4
  48.6 0.0 copy-done.5
  48.6 1.4 %local.2.part_ref = f32[6,20,384]{2,1,0:T(8,128)S(1)} custom-call(f32[6,20,384]{2,1,0:T(8,128)S(1)} %get-tuple-element.9.state_ref, f32[64,384]{1,0:T(8,128)S(1)} %get-tuple-element.10.derived_ref, s32[4,384]{1,0:T(4,128)S(1)} %copy-done.3, s32[4,384]{1,0:T(4,128)S(1)} %copy-done.4, bf16[80,96]{1,0:T(8,128)(2,1)S(1)} %copy-done.5, bf16[32,144]{1,0:T(8,128)(2,1)S(1)} %copy-done.1), custom_call_target="tpu_custom_call" | custom-call | flops 100000000 | bytes 1000000 | tf_op jit(solution)/shard_map/local/pallas_call | solution.py:602
  50.0 4.8 %all-to-all-done.1 = f32[16,8,128]{2,1,0:T(8,128)S(1)} async-done(((f32[16,8,128]{2,1,0:T(8,128)}), f32[16,8,128]{2,1,0:T(8,128)S(1)}, u32[]{:S(2)}, u32[]{:S(2)}) %all-to-all-start.1) | async-done | bytes 65568 | tf_op jit(solution)/shard_map/all_to_all | solution.py:658
  54.8 2.0 %first.1 = (f32[6,20,384]{2,1,0:T(8,128)S(1)}, f32[6,20,384]{2,1,0:T(8,128)S(1)}, f32[128,128]{1,0:T(8,128)}) custom-call(f32[128,128]{1,0:T(8,128)S(1)} %bitcast.8, f32[6,20,384]{2,1,0:T(8,128)S(1)} %local.2.part_ref, f32[6,20,384]{2,1,0:T(8,128)S(1)} %get-tuple-element.9.state_ref, f32[64,384]{1,0:T(8,128)S(1)} %get-tuple-element.10.derived_ref, ...), custom_call_target="tpu_custom_call" | custom-call | flops 100000000 | bytes 1000000 | tf_op jit(solution)/shard_map/first/pallas_call | solution.py:602
  56.8 4.8 %all-to-all-start.2 = ((f32[16,8,128]{2,1,0:T(8,128)}), f32[16,8,128]{2,1,0:T(8,128)S(1)}, u32[]{:S(2)}, u32[]{:S(2)}) async-start(f32[16,8,128]{2,1,0:T(8,128)} %bitcast.4), calls=%async_computation.2 | async-start | bytes 131072 | tf_op jit(solution)/shard_map/all_to_all | solution.py:658
  61.7 1.4 %local.3.part_ref = f32[6,20,384]{2,1,0:T(8,128)S(1)} custom-call(f32[6,20,384]{2,1,0:T(8,128)S(1)} %get-tuple-element.12.state_ref.middle_ref, f32[64,384]{1,0:T(8,128)S(1)} %get-tuple-element.10.derived_ref, s32[4,384]{1,0:T(4,128)S(1)} %copy-done.3, s32[4,384]{1,0:T(4,128)S(1)} %copy-done.4, bf16[80,96]{1,0:T(8,128)(2,1)S(1)} %copy-done.5, ...), custom_call_target="tpu_custom_call" | custom-call | flops 100000000 | bytes 1000000 | tf_op jit(solution)/shard_map/local/pallas_call | solution.py:602
  63.1 4.9 %all-to-all-done.2 = f32[16,8,128]{2,1,0:T(8,128)S(1)} async-done(((f32[16,8,128]{2,1,0:T(8,128)}), f32[16,8,128]{2,1,0:T(8,128)S(1)}, u32[]{:S(2)}, u32[]{:S(2)}) %all-to-all-start.2) | async-done | bytes 65568 | tf_op jit(solution)/shard_map/all_to_all | solution.py:658
  68.0 1.6 %second.1 = (f32[6,20,384]{2,1,0:T(8,128)}, f32[6,20,384]{2,1,0:T(8,128)}) custom-call(f32[128,128]{1,0:T(8,128)S(1)} %bitcast.9, f32[6,20,384]{2,1,0:T(8,128)S(1)} %local.3.part_ref, f32[6,20,384]{2,1,0:T(8,128)S(1)} %get-tuple-element.12.state_ref.middle_ref, f32[6,20,384]{2,1,0:T(8,128)S(1)} %get-tuple-element.13.first_ref, ...), custom_call_target="tpu_custom_call" | custom-call | flops 100000000 | bytes 1000000 | tf_op jit(solution)/shard_map/second/pallas_call | solution.py:602
Async XLA Ops:
  0.6 38.9 %copy-start = (bf16[2,1024,128]{2,1,0:T(8,128)(2,1)S(1)}, bf16[2,1024,128]{2,1,0:T(8,128)(2,1)}, u32[]{:S(2)}) copy-start(bf16[2,1024,128]{2,1,0:T(8,128)(2,1)} %constant.8.clone.select_ref) | copy-start | bytes 1572868
  1.5 0.9 %copy-start.2 = (f32[6,20,256]{2,1,0:T(8,128)S(1)}, f32[6,20,256]{2,1,0:T(8,128)}, u32[]{:S(2)}) copy-start(f32[6,20,256]{2,1,0:T(8,128)} %fields_ref.1) | copy-start | bytes 368644
  2.4 0.7 %copy-start.7 = (f32[11,256]{1,0:T(8,128)S(1)}, f32[11,256]{1,0:T(8,128)}, u32[]{:S(2)}) copy-start(f32[11,256]{1,0:T(8,128)} %geometry_ref.1) | copy-start | bytes 33796
  3.5 36.0 %copy-start.6 = (s32[1,16,16]{2,1,0:T(8,128)S(1)}, s32[1,16,16]{2,1,0:T(8,128)}, u32[]{:S(2)}) copy-start(s32[1,16,16]{2,1,0:T(8,128)} %list_ref.4) | copy-start | bytes 3076
  40.9 7.6 %copy-start.1 = (bf16[32,144]{1,0:T(8,128)(2,1)S(1)}, bf16[32,144]{1,0:T(8,128)(2,1)}, u32[]{:S(2)}) copy-start(bf16[32,144]{1,0:T(8,128)(2,1)} %constant.7.clone.lift_ref) | copy-start | bytes 27652
  40.9 7.6 %copy-start.3 = (s32[4,384]{1,0:T(4,128)S(1)}, s32[4,384]{1,0:T(4,128)}, u32[]{:S(2)}) copy-start(s32[4,384]{1,0:T(4,128)} %link_ref.7) | copy-start | bytes 18436
  40.9 7.6 %copy-start.4 = (s32[4,384]{1,0:T(4,128)S(1)}, s32[4,384]{1,0:T(4,128)}, u32[]{:S(2)}) copy-start(s32[4,384]{1,0:T(4,128)} %orient_ref.7) | copy-start | bytes 18436
  40.9 7.7 %copy-start.5 = (bf16[80,96]{1,0:T(8,128)(2,1)S(1)}, bf16[80,96]{1,0:T(8,128)(2,1)}, u32[]{:S(2)}) copy-start(bf16[80,96]{1,0:T(8,128)(2,1)} %constant.6.clone.slope_ref) | copy-start | bytes 46084
  40.9 13.9 %all-to-all-start.1 = ((f32[16,8,128]{2,1,0:T(8,128)}), f32[16,8,128]{2,1,0:T(8,128)S(1)}, u32[]{:S(2)}, u32[]{:S(2)}) async-start(f32[16,8,128]{2,1,0:T(8,128)} %bitcast.2), calls=%async_computation.1 | async-start | bytes 131072 | tf_op jit(solution)/shard_map/all_to_all | solution.py:658
  56.8 11.1 %all-to-all-start.2 = ((f32[16,8,128]{2,1,0:T(8,128)}), f32[16,8,128]{2,1,0:T(8,128)S(1)}, u32[]{:S(2)}, u32[]{:S(2)}) async-start(f32[16,8,128]{2,1,0:T(8,128)} %bitcast.4), calls=%async_computation.2 | async-start | bytes 131072 | tf_op jit(solution)/shard_map/all_to_all | solution.py:658

commit v2 on v1

--- a/solution.py
+++ b/solution.py
@@ -27,6 +27,7 @@
 column_count = faces * new_count
 remote_count = subs * traces
 lane = 128
+half_lane = lane // 2
 tiles = new_count // lane
 block_rows = slots + 1
 
@@ -205,16 +206,26 @@
     return jnp.asarray(np.concatenate([high, high, rest], axis=1))
 
 
+def remote_lift_operand():
+    stacked = np.zeros((32, 16 * faces), np.float64)
+    for face_id in range(faces):
+        for node_id in range(face_nodes):
+            for row_id in range(node_count):
+                stacked[row_id, face_id * 16 + node_id] = lift_table[row_id][
+                    face_id * face_nodes + node_id
+                ]
+    high, rest = bf16_pair(stacked)
+    return jnp.asarray(np.concatenate([high, high, rest], axis=1))
+
+
 def select_operand():
-    table = np.zeros((2, faces * 2 * lane, lane), np.float32)
-    for half in range(2):
-        for face_id in range(faces):
-            for part_id in range(2):
-                for node_id in range(face_nodes):
-                    for comp_id in range(components):
-                        row_id = (face_id * 2 + part_id) * lane
-                        row_id += comp_id * node_count + face_mask[face_id][node_id]
-                        table[half, row_id, half * 64 + node_id * components + comp_id] = 1.0
+    table = np.zeros((2 * lane, faces * half_lane), np.float32)
+    for face_id in range(faces):
+        for part_id in range(2):
+            for node_id in range(face_nodes):
+                for comp_id in range(components):
+                    row_id = part_id * lane + comp_id * node_count + face_mask[face_id][node_id]
+                    table[row_id, face_id * half_lane + node_id * components + comp_id] = 1.0
     return jnp.asarray(table.astype(ml_dtypes.bfloat16))
 
 
@@ -224,14 +235,6 @@
     return high, rest
 
 
-def split_three(value):
-    high = value.astype(jnp.bfloat16)
-    left = value - high.astype(jnp.float32)
-    middle = left.astype(jnp.bfloat16)
-    rest = (left - middle.astype(jnp.float32)).astype(jnp.bfloat16)
-    return high, middle, rest
-
-
 def dot_rows(left, right):
     return lax.dot_general(
         left, right, (((1,), (0,)), ((), ())), preferred_element_type=jnp.float32
@@ -252,20 +255,33 @@
     return sum((codes >= step * new_count).astype(jnp.int32) for step in range(1, faces))
 
 
-def pack_kernel(fields_ref, geometry_ref, list_ref, out_ref, held_ref):
+def pack_kernel(fields_ref, geometry_ref, list_ref, out_ref, took_ref, geo_ref, codes_ref, held_ref, sems):
     field_rows = components * node_count
-    for comp_id in range(components):
-        held_ref[comp_id * node_count : (comp_id + 1) * node_count, :] = fields_ref[comp_id]
-    held_ref[field_rows : field_rows + 11, :] = geometry_ref[...]
-    held_ref[field_rows + 11 :, :] = jnp.zeros((13, old_count), jnp.float32)
-    parts = jnp.concatenate(split_three(held_ref[...]), axis=1)
-    parts = jnp.concatenate([parts, jnp.zeros((112, 3 * old_count), jnp.bfloat16)], axis=0)
-    codes = list_ref[0]
+    copies = [
+        pltpu.make_async_copy(list_ref, codes_ref, sems.at[0]),
+        pltpu.make_async_copy(fields_ref, took_ref, sems.at[1]),
+        pltpu.make_async_copy(geometry_ref, geo_ref, sems.at[2]),
+    ]
+    for copy in copies:
+        copy.start()
+    copies[0].wait()
+    turned = jnp.concatenate([codes_ref[slot_id] for slot_id in range(slots)], axis=0)
+    turned = jnp.concatenate([turned, jnp.zeros((lane - slots, slabs), jnp.int32)], axis=0)
+    turned = jnp.concatenate([turned, jnp.zeros((lane, lane - slabs), jnp.int32)], axis=1)
+    codes = jnp.transpose(turned)[:slabs]
     lanes = lax.broadcasted_iota(jnp.int32, (slabs, old_count), 1)
     picks = jnp.concatenate(
         [one_hot(codes[:, slot_id : slot_id + 1] == lanes) for slot_id in range(slots)], axis=0
     )
-    moved = dot_lanes(jnp.concatenate([picks, picks, picks], axis=1), parts)
+    copies[1].wait()
+    copies[2].wait()
+    for comp_id in range(components):
+        held_ref[comp_id * node_count : (comp_id + 1) * node_count, :] = took_ref[comp_id]
+    held_ref[field_rows : field_rows + 11, :] = geo_ref[...]
+    held_ref[field_rows + 11 :, :] = jnp.zeros((13, old_count), jnp.float32)
+    parts = jnp.concatenate(split_two(held_ref[...]), axis=1)
+    parts = jnp.concatenate([parts, jnp.zeros((112, 2 * old_count), jnp.bfloat16)], axis=0)
+    moved = dot_lanes(jnp.concatenate([picks, picks], axis=1), parts)
     short = lax.broadcasted_iota(jnp.int32, (slabs, lane), 1)
     diagonal = (short == field_rows) | (short == field_rows + 4)
     tail = jnp.zeros((slabs, lane), jnp.float32)
@@ -282,40 +298,65 @@
     out_ref[pl.ds(slots, slabs, stride=block_rows), :] = tail
 
 
-def trace_rows(values, codes, select_ref, trace_ref):
-    high, rest = split_two(values)
+def plan_kernel(
+    list_ref, link_ref, orient_ref, came_pick_ref, slot_pick_ref, face_ref, spread_ref, about_ref, codes_ref
+):
+    codes = list_ref[0]
+    half = traces // 2
+    for idx in range(traces):
+        rows = pl.ds((idx // half) * lane + idx % half, subs, stride=half)
+        codes_ref[rows, :] = jnp.broadcast_to(codes[:, idx : idx + 1], (subs, lane))
+    codes = codes_ref[...]
     face = face_of(codes)
     element = codes - new_count * face
-    lanes = lax.broadcasted_iota(jnp.int32, (subs, new_count), 1)
-    picks = jnp.concatenate(
-        [one_hot(element[:, idx : idx + 1] == lanes) for idx in range(traces)], axis=0
-    )
-    found = dot_lanes(picks, jnp.concatenate([high, rest], axis=0)).astype(jnp.bfloat16)
-    face_rows = jnp.concatenate(
-        [
-            jnp.broadcast_to(face[:, idx : idx + 1], (subs, 2 * lane))
-            for idx in range(traces)
-        ],
-        axis=0,
-    )
-    zeros = jnp.zeros(found.shape, jnp.float32)
-    wide = found.astype(jnp.float32)
-    spread = jnp.concatenate(
-        [
-            jnp.where(face_rows == face_id, wide, zeros).astype(jnp.bfloat16)
-            for face_id in range(faces)
-        ],
-        axis=1,
-    )
+    face_ref[...] = face
+    lanes = lax.broadcasted_iota(jnp.int32, (remote_count, lane), 1)
+    slot_pick_ref[...] = jnp.concatenate(
+        [one_hot(element == lanes + tile * lane) for tile in range(tiles)], axis=1
+    )
+    came_row = element + ((element * 5462) >> 16)
+    came_pick_ref[...] = jnp.concatenate(
+        [one_hot(came_row == lanes + tile * lane) for tile in range(tiles + 1)], axis=1
+    )
+    rows = lax.broadcasted_iota(jnp.int32, (remote_count, new_count), 0)
+    about_rows = lax.broadcasted_iota(jnp.int32, (16, new_count), 0)
+    about = None
+    spread = None
+    for face_id in range(faces):
+        far = link_ref[face_id : face_id + 1, :] - column_count
+        orient = orient_ref[face_id : face_id + 1, :]
+        column = ((far >> 3) & 1) * lane + (far >> 4) * 8 + (far & 7)
+        column = jnp.where((far >= 0) & (orient < 6), column, -1)
+        picks = one_hot(rows == column)
+        facts = jnp.where(about_rows == 0, orient, jnp.where(about_rows == 1, face_id, 0))
+        term = dot_lanes(facts.astype(jnp.float32).astype(jnp.bfloat16), picks)
+        about = term if about is None else about + term
+        spread = picks if spread is None else spread + picks
+    spread_ref[...] = spread
+    about_ref[...] = about[:8]
+
+
+def trace_rows(found, face, select_ref, trace_ref):
+    wide = dot_rows(found.astype(jnp.bfloat16), select_ref[...])
+    near = jnp.where(face >= 2, wide[:, lane:], wide[:, :lane])
+    odd = (face & 1) == 1
     half = remote_count // 2
-    rows = dot_rows(spread[:half], select_ref[0]) + dot_rows(spread[half:], select_ref[1])
-    for idx in range(traces // 2):
-        trace_ref[pl.ds(idx, subs, stride=traces // 2), :] = rows[idx * subs : (idx + 1) * subs]
-
-
-def unpack_kernel(
-    came_ref, list_ref, select_ref, state_ref, derived_ref, trace_ref, rows_ref, tail_ref, main_ref
-):
+    upper, lower = near[:half], near[half:]
+    upper = jnp.where(odd[:half], pltpu.roll(upper, half_lane, 1), upper)
+    lower = jnp.where(odd[half:], lower, pltpu.roll(lower, half_lane, 1))
+    lanes = lax.broadcasted_iota(jnp.int32, (half, lane), 1)
+    trace_ref[...] = jnp.where(lanes < half_lane, upper, lower)
+
+
+def start_kernel(came_ref, pick_ref, face_ref, select_ref, trace_ref):
+    parts = jnp.concatenate(split_two(came_ref[...]), axis=1)
+    parts = jnp.concatenate(
+        [parts, jnp.zeros((4 * lane - slabs * block_rows, 2 * lane), jnp.bfloat16)], axis=0
+    )
+    trace_rows(dot_rows(pick_ref[...], parts), face_ref[...], select_ref, trace_ref)
+
+
+def unpack(came_ref, state_ref, derived_ref, rows_ref, tail_ref, main_ref):
     field_rows = components * node_count
     tail = came_ref[pl.ds(slots, slabs, stride=block_rows), :]
     for slot_id in range(slots):
@@ -324,9 +365,7 @@
         ]
         shifted = pltpu.roll(tail, lane - 3 * slot_id, 1) if slot_id else tail
         tail_ref[pl.ds(slot_id, slabs, stride=slots), :] = shifted
-    main = jnp.transpose(rows_ref[...])
-    trace_rows(main, list_ref[0], select_ref, trace_ref)
-    main_ref[...] = main
+    main_ref[...] = jnp.transpose(rows_ref[...])
     extra = jnp.transpose(tail_ref[...])[:8]
     for comp_id in range(components):
         state_ref[comp_id] = main_ref[comp_id * node_count : (comp_id + 1) * node_count, :]
@@ -350,6 +389,22 @@
     derived_ref[48:56, :] = jnp.concatenate([inverse, inverse], axis=0)
 
 
+def compact(derived_ref, spread_ref, about_ref, far_ref):
+    stacked = jnp.concatenate(split_two(derived_ref[16:64, :]), axis=0)
+    found = dot_lanes(stacked, spread_ref[...])
+    found = found[:48] + found[48:]
+    face = about_ref[1:2, :]
+    for block in range(5):
+        first_row = 8 * block
+        value = found[first_row : first_row + 1]
+        for face_id in range(1, faces):
+            row_id = first_row + face_id
+            value = jnp.where(face == face_id, found[row_id : row_id + 1], value)
+        far_ref[block : block + 1, :] = value
+    far_ref[5:7, :] = about_ref[0:2, :]
+    far_ref[7:8, :] = jnp.zeros((1, remote_count), jnp.float32)
+
+
 def oriented(planes, orient):
     masks = [orient == turn_id for turn_id in range(6)]
     result = []
@@ -370,18 +425,9 @@
     return result
 
 
-def lifted_flux(jump_ref, flux_ref, derived_ref, lift_ref):
-    groups = faces * face_nodes // 8
-
-    def jump_of(comp_id):
-        rows = strided_load(jump_ref, comp_id, faces * face_nodes, 8)
-        return rows.reshape(groups, 8, new_count)
-
+def face_flux(jump_of, normal, length, inverse):
     jump_h = [jump_of(comp_id) for comp_id in range(3)]
     jump_e = [jump_of(comp_id) for comp_id in range(3, 6)]
-    normal = [derived_ref[16 + 8 * axis_id : 24 + 8 * axis_id, :][None] for axis_id in range(3)]
-    length = derived_ref[40:48, :][None]
-    inverse = derived_ref[48:56, :][None]
 
     def along(jump):
         total = normal[0] * jump[0] + normal[1] * jump[1] + normal[2] * jump[2]
@@ -389,16 +435,29 @@
 
     along_h = along(jump_h)
     along_e = along(jump_e)
+    flux_h, flux_e = [], []
     for axis_id in range(3):
         after, last = (axis_id + 1) % 3, (axis_id + 2) % 3
         cross_e = normal[after] * jump_e[last] - normal[last] * jump_e[after]
         cross_h = normal[after] * jump_h[last] - normal[last] * jump_h[after]
-        flux_h = length * jump_h[axis_id] - normal[axis_id] * along_h - cross_e
-        flux_e = length * jump_e[axis_id] - normal[axis_id] * along_e + cross_h
-        for comp_id, value in ((axis_id, flux_h), (3 + axis_id, flux_e)):
-            flux_ref[0:40, comp_id * new_count : (comp_id + 1) * new_count] = value.reshape(
-                faces * face_nodes, new_count
-            )
+        flux_h.append(length * jump_h[axis_id] - normal[axis_id] * along_h - cross_e)
+        flux_e.append(length * jump_e[axis_id] - normal[axis_id] * along_e + cross_h)
+    return flux_h + flux_e
+
+
+def lifted_flux(jump_ref, flux_ref, derived_ref, lift_ref):
+    groups = faces * face_nodes // 8
+
+    def jump_of(comp_id):
+        rows = strided_load(jump_ref, comp_id, faces * face_nodes, 8)
+        return rows.reshape(groups, 8, new_count)
+
+    normal = [derived_ref[16 + 8 * axis_id : 24 + 8 * axis_id, :][None] for axis_id in range(3)]
+    fluxes = face_flux(jump_of, normal, derived_ref[40:48, :][None], derived_ref[48:56, :][None])
+    for comp_id, value in enumerate(fluxes):
+        flux_ref[0:40, comp_id * new_count : (comp_id + 1) * new_count] = value.reshape(
+            faces * face_nodes, new_count
+        )
     flux_ref[40:48, :] = jnp.zeros((8, components * new_count), jnp.float32)
     high, rest = split_two(flux_ref[...])
     return dot_rows(lift_ref[...], jnp.concatenate([high, rest, high], axis=0))
@@ -406,12 +465,12 @@
 
 def strided_load(ref, start, size, stride):
     return jnp.concatenate(
-        [ref[tile, pl.ds(start, size, stride=stride), :] for tile in range(tiles)], axis=1
+        [ref[tile, pl.ds(start, size, stride=stride), :] for tile in range(ref.shape[0])], axis=1
     )
 
 
 def tiled_store(ref, rows, value):
-    for tile in range(tiles):
+    for tile in range(ref.shape[0]):
         ref[tile, rows, :] = value[:, tile * lane : (tile + 1) * lane]
 
 
@@ -423,18 +482,8 @@
     return matrix[:24, comp_id * new_count : (comp_id + 1) * new_count]
 
 
-def local_kernel(
-    state_ref,
-    derived_ref,
-    link_ref,
-    orient_ref,
-    slope_ref,
-    lift_ref,
-    part_ref,
-    nodes_ref,
-    flat_ref,
-    jump_ref,
-    flux_ref,
+def local_part(
+    state_ref, derived_ref, link_ref, orient_ref, slope_ref, lift_ref, part_ref, nodes_ref, flat_ref, jump_ref, flux_ref
 ):
     nodes_ref[...] = jnp.zeros(nodes_ref.shape, jnp.float32)
     flat_ref[node_count:32, :] = jnp.zeros((12, components * new_count), jnp.float32)
@@ -498,37 +547,84 @@
         part_ref[3 + axis_id] = change_e[:node_count]
 
 
-def remote_part(came_ref, link_ref, orient_ref, derived_ref, lift_ref, turned_ref, table_ref, jump_ref, flux_ref):
+def arrive_kernel(
+    came_ref,
+    link_ref,
+    orient_ref,
+    slope_ref,
+    lift_ref,
+    spread_ref,
+    about_ref,
+    state_ref,
+    derived_ref,
+    far_ref,
+    part_ref,
+    rows_ref,
+    tail_ref,
+    main_ref,
+    *scratches,
+):
+    derived_ref[...] = jnp.zeros(derived_ref.shape, jnp.float32)
+    unpack(came_ref, state_ref, derived_ref, rows_ref, tail_ref, main_ref)
+    compact(derived_ref, spread_ref, about_ref, far_ref)
+    local_part(state_ref, derived_ref, link_ref, orient_ref, slope_ref, lift_ref, part_ref, *scratches)
+
+
+def local_kernel(*refs):
+    local_part(*refs)
+
+
+def remote_part(came_ref, far_ref, spread_ref, lift_ref, derived_ref, turned_ref, table_ref, jump_ref, flux_ref):
     turned_ref[...] = jnp.transpose(came_ref[...])
     table_ref[...] = jnp.zeros(table_ref.shape, jnp.float32)
     for half in range(2):
         for node_id in range(face_nodes):
-            first_row = half * 64 + node_id * components
-            table_ref[8 * node_id : 8 * node_id + components, half * lane : (half + 1) * lane] = (
-                turned_ref[first_row : first_row + components, :]
-            )
-    stacked = jnp.concatenate(split_two(table_ref[...]), axis=0)
-    rows = lax.broadcasted_iota(jnp.int32, (remote_count, new_count), 0)
+            first_row = half * half_lane + node_id * components
+            table_ref[half, 8 * node_id : 8 * node_id + components, :] = turned_ref[
+                first_row : first_row + components, :
+            ]
+    planes = [
+        jnp.concatenate(
+            [table_ref[half, 8 * node_id : 8 * node_id + 8, :] for half in range(2)], axis=1
+        )
+        for node_id in range(face_nodes)
+    ]
+    outside = oriented(planes, far_ref[5:6, :])
+    for node_id in range(face_nodes):
+        tiled_store(jump_ref, slice(8 * node_id, 8 * node_id + 8), outside[node_id])
+    fluxes = face_flux(
+        lambda comp_id: strided_load(jump_ref, comp_id, face_nodes, 8),
+        [far_ref[axis_id : axis_id + 1, :] for axis_id in range(3)],
+        far_ref[3:4, :],
+        far_ref[4:5, :],
+    )
+    flux_ref[...] = jnp.zeros(flux_ref.shape, jnp.float32)
+    face = far_ref[6:7, :]
     for face_id in range(faces):
-        far = link_ref[face_id : face_id + 1, :] - column_count
-        orient = orient_ref[face_id : face_id + 1, :]
-        column = ((far >> 3) & 1) * lane + (far >> 4) * 8 + (far & 7)
-        column = jnp.where((far >= 0) & (orient < 6), column, -1)
-        found = dot_rows(stacked, one_hot(rows == column))
-        found = found[: 8 * face_nodes] + found[8 * face_nodes :]
-        planes = [found[8 * node_id : 8 * node_id + 8] for node_id in range(face_nodes)]
-        outside = oriented(planes, orient)
-        for node_id in range(face_nodes):
-            target = 8 * (node_id * faces + face_id)
-            tiled_store(jump_ref, slice(target, target + 8), outside[node_id])
-    lifted = lifted_flux(jump_ref, flux_ref, derived_ref, lift_ref)
+        here = face == face_id
+        for comp_id, value in enumerate(fluxes):
+            columns = slice(comp_id * remote_count, (comp_id + 1) * remote_count)
+            flux_ref[16 * face_id : 16 * face_id + face_nodes, columns] = jnp.where(here, value, 0.0)
+    high, rest = split_two(flux_ref[...])
+    lifted = dot_rows(lift_ref[...], jnp.concatenate([high, rest, high], axis=0))
+    stacked = jnp.concatenate(
+        [
+            lifted[:24, comp_id * remote_count : (comp_id + 1) * remote_count]
+            for comp_id in range(components)
+        ],
+        axis=0,
+    )
+    placed = dot_rows(jnp.concatenate(split_two(stacked), axis=0), spread_ref[...])
+    rows = 24 * components
+    placed = placed[:rows] + placed[rows:]
     inverse_eps = derived_ref[9:10, :]
     inverse_mu = derived_ref[10:11, :]
-    changes = []
-    for comp_id in range(components):
-        scale = inverse_mu if comp_id < 3 else inverse_eps
-        changes.append((column_block(lifted, comp_id) * scale)[:node_count])
-    return changes
+    return [
+        (placed[24 * comp_id : 24 * comp_id + 24] * (inverse_mu if comp_id < 3 else inverse_eps))[
+            :node_count
+        ]
+        for comp_id in range(components)
+    ]
 
 
 def first_kernel(
@@ -536,31 +632,28 @@
     part_ref,
     state_ref,
     derived_ref,
-    link_ref,
-    orient_ref,
+    far_ref,
+    spread_ref,
     lift_ref,
-    list_ref,
+    pick_ref,
+    face_ref,
     select_ref,
     residual_ref,
     middle_ref,
     trace_ref,
-    turned_ref,
-    table_ref,
-    jump_ref,
-    flux_ref,
     main_ref,
+    *scratches,
 ):
-    changes = remote_part(
-        came_ref, link_ref, orient_ref, derived_ref, lift_ref, turned_ref, table_ref, jump_ref, flux_ref
-    )
+    changes = remote_part(came_ref, far_ref, spread_ref, lift_ref, derived_ref, *scratches)
+    main_ref[components * node_count :, :] = jnp.zeros((8, new_count), jnp.float32)
     for comp_id in range(components):
         residual = time_step * (part_ref[comp_id] + changes[comp_id])
         middle = state_ref[comp_id] + section_b1 * residual
         residual_ref[comp_id] = residual
         middle_ref[comp_id] = middle
         main_ref[comp_id * node_count : (comp_id + 1) * node_count, :] = middle
-    main_ref[components * node_count :, :] = jnp.zeros((8, new_count), jnp.float32)
-    trace_rows(main_ref[...], list_ref[0], select_ref, trace_ref)
+    parts = jnp.concatenate(split_two(main_ref[...]), axis=0)
+    trace_rows(dot_lanes(pick_ref[...], parts), face_ref[...], select_ref, trace_ref)
 
 
 def second_kernel(
@@ -569,19 +662,14 @@
     middle_ref,
     first_ref,
     derived_ref,
-    link_ref,
-    orient_ref,
+    far_ref,
+    spread_ref,
     lift_ref,
     advanced_ref,
     residual_ref,
-    turned_ref,
-    table_ref,
-    jump_ref,
-    flux_ref,
+    *scratches,
 ):
-    changes = remote_part(
-        came_ref, link_ref, orient_ref, derived_ref, lift_ref, turned_ref, table_ref, jump_ref, flux_ref
-    )
+    changes = remote_part(came_ref, far_ref, spread_ref, lift_ref, derived_ref, *scratches)
     for comp_id in range(components):
         residual = section_a2 * first_ref[comp_id] + time_step * (
             part_ref[comp_id] + changes[comp_id]
@@ -594,87 +682,132 @@
     return jax.ShapeDtypeStruct(shape, jnp.float32)
 
 
+def near(*shape):
+    return pltpu.VMEM(shape, jnp.float32)
+
+
+def halves(*shape):
+    return jax.ShapeDtypeStruct(shape, jnp.bfloat16)
+
+
 def scratch(*shape):
     return pltpu.VMEM(shape, jnp.float32)
 
 
-def run(kernel, name, outs, scratches, operands, flops=10**8):
+def run(kernel, name, outs, scratches, operands, in_specs=None):
     return pl.pallas_call(
         kernel,
         name=name,
         out_shape=outs,
+        in_specs=in_specs or [pl.BlockSpec(memory_space=pltpu.VMEM)] * len(operands),
         scratch_shapes=scratches,
         compiler_params=pltpu.CompilerParams(vmem_limit_bytes=24 * 2**20),
-        cost_estimate=pl.CostEstimate(flops=flops, bytes_accessed=10**6, transcendentals=0),
+        cost_estimate=pl.CostEstimate(flops=10**8, bytes_accessed=10**6, transcendentals=0),
     )(*operands)
 
 
 def shards(fields, geometry, migrate_list, trace_list, face_link, face_orient):
     slopes = slope_operand()
     lift = lift_operand()
+    remote_lift = remote_lift_operand()
     select = select_operand()
     state_shape = floats(components, node_count, new_count)
-    trace_shape = floats(subs * traces // 2, lane)
+    trace_shape = near(remote_count // 2, lane)
+    local_scratch = [
+        scratch(tiles, 8 * node_count, lane),
+        scratch(32, components * new_count),
+        scratch(tiles, 8 * faces * face_nodes, lane),
+        scratch(48, components * new_count),
+    ]
     remote_scratch = [
         scratch(lane, lane),
-        scratch(8 * face_nodes, remote_count),
-        scratch(tiles, 8 * faces * face_nodes, lane),
-        scratch(48, components * new_count),
+        scratch(2, 8 * face_nodes, lane),
+        scratch(2, 8 * face_nodes, lane),
+        scratch(16 * faces, components * remote_count),
     ]
     parcel = run(
         pack_kernel,
         "pack",
-        floats(slabs * block_rows, lane),
-        [scratch(144, old_count)],
-        (fields, geometry, migrate_list),
+        near(slabs * block_rows, lane),
+        [
+            scratch(components, node_count, old_count),
+            scratch(11, old_count),
+            pltpu.VMEM((slots, 1, slabs), jnp.int32),
+            scratch(144, old_count),
+            pltpu.SemaphoreType.DMA((3,)),
+        ],
+        [
+            pltpu.with_memory_space_constraint(operand, pltpu.HBM)
+            for operand in (fields, geometry, jnp.transpose(migrate_list, (2, 0, 1)))
+        ],
+        [pl.BlockSpec(memory_space=pltpu.HBM)] * 3,
     )
     arrived = lax.all_to_all(
         parcel.reshape(slabs, block_rows * lane), "slab", split_axis=0, concat_axis=0, tiled=True
     ).reshape(slabs * block_rows, lane)
-    state, derived, outgoing = run(
-        unpack_kernel,
-        "unpack",
-        (state_shape, floats(64, new_count), trace_shape),
-        [scratch(new_count, lane), scratch(new_count, lane), scratch(lane, new_count)],
-        (arrived, trace_list, select),
-    )
-
-    def local(current):
-        return run(
-            local_kernel,
-            "local",
-            state_shape,
-            [
-                scratch(tiles, 8 * node_count, lane),
-                scratch(32, components * new_count),
-                scratch(tiles, 8 * faces * face_nodes, lane),
-                scratch(48, components * new_count),
-            ],
-            (current, derived, face_link, face_orient, slopes, lift),
-        )
+    came_pick, slot_pick, trace_face, spread, about = run(
+        plan_kernel,
+        "plan",
+        (
+            halves(remote_count, 4 * lane),
+            halves(remote_count, new_count),
+            jax.ShapeDtypeStruct((remote_count, lane), jnp.int32),
+            halves(remote_count, new_count),
+            floats(8, remote_count),
+        ),
+        [pltpu.VMEM((remote_count, lane), jnp.int32)],
+        (trace_list, face_link, face_orient),
+    )
+    outgoing = run(
+        start_kernel, "start", trace_shape, [], (arrived, came_pick, trace_face, select)
+    )
 
     def exchange(rows):
         blocks = rows.reshape(subs, traces // 2, lane)
         came = lax.all_to_all(blocks, "sub", split_axis=0, concat_axis=0, tiled=True)
-        return came.reshape(subs * traces // 2, lane)
+        return came.reshape(remote_count // 2, lane)
 
     incoming = exchange(outgoing)
-    part = local(state)
+    state, derived, far, part = run(
+        arrive_kernel,
+        "arrive",
+        (state_shape, floats(64, new_count), floats(8, remote_count), state_shape),
+        [scratch(new_count, lane), scratch(new_count, lane), scratch(lane, new_count)]
+        + local_scratch,
+        (arrived, face_link, face_orient, slopes, lift, spread, about),
+    )
     first_res, middle, outgoing = run(
         first_kernel,
         "first",
         (state_shape, state_shape, trace_shape),
-        remote_scratch + [scratch(lane, new_count)],
-        (incoming, part, state, derived, face_link, face_orient, lift, trace_list, select),
+        [scratch(lane, new_count)] + remote_scratch,
+        (
+            incoming,
+            part,
+            state,
+            derived,
+            far,
+            spread,
+            remote_lift,
+            slot_pick,
+            trace_face,
+            select,
+        ),
     )
     incoming = exchange(outgoing)
-    part = local(middle)
+    part = run(
+        local_kernel,
+        "local",
+        state_shape,
+        local_scratch,
+        (middle, derived, face_link, face_orient, slopes, lift),
+    )
     return run(
         second_kernel,
         "second",
         (state_shape, state_shape),
         remote_scratch,
-        (incoming, part, middle, first_res, derived, face_link, face_orient, lift),
+        (incoming, part, middle, first_res, derived, far, spread, remote_lift),
     )
 
 

time: 70 us -> 68.6 us (0.980)
  blocking collectives: 36 us -> 0 us
  waiting for transfers between devices: 9.7 us -> 29.6 us
  starting transfers between devices: 12.5 us -> 28.1 us
  local copies, waits for them, and re-layouts: 2.48 us -> 0.04 us
  Pallas kernels: 8.24 us -> 9.65 us
    all_to_all x1 -> x0, blocking collectives: 36 us -> none  [shards(): lax.all_to_all(parcel.reshape(slabs, block_rows * lane), 'slab', split_ax...]
    all_to_all x0 -> x1, waiting for transfers between devices: none -> 20.1 us  [shards(): lax.all_to_all(parcel.reshape(slabs, block_rows * lane), 'slab', split_ax...]
    all_to_all x0 -> x1, starting transfers between devices: none -> 15.6 us  [shards(): lax.all_to_all(parcel.reshape(slabs, block_rows * lane), 'slab', split_ax...]
    unnamed x17 -> x14, local copies, waits for them, and re-layouts: 2.48 us -> 0.04 us
    pallas_call x6 -> x7, Pallas kernels: 8.24 us -> 9.65 us  [run(): pl.pallas_call(kernel, name=name, out_shape=outs, in_specs=in_specs or [p...]
  transfers between devices with their start and end apart: 2 -> 3, of which waited for: 2 -> 3; matrix products, arithmetic and copies ran while one was open for 0% -> 0% of each run, Pallas kernels for 4% -> 5%
where the time goes in v2:
time: 68.6 us; the launch traced here: 68.1 us
  waiting for transfers between devices  29.6 us (43%)
  starting transfers between devices  28.1 us (41%)
  Pallas kernels  9.65 us (14%)
  between operations  0.75 us (1%)
    all_to_all x1, waiting for transfers between devices, shards(): lax.all_to_all(parcel.reshape(slabs, block_rows * lane), 'slab', split_ax...  20.1 us
    all_to_all x1, starting transfers between devices, shards(): lax.all_to_all(parcel.reshape(slabs, block_rows * lane), 'slab', split_ax...  15.6 us
    all_to_all x2, starting transfers between devices, exchange(): lax.all_to_all(blocks, 'sub', split_axis=0, concat_axis=0, tiled=True)  12.4 us
    pallas_call x7, Pallas kernels, run(): pl.pallas_call(kernel, name=name, out_shape=outs, in_specs=in_specs or [p...  9.65 us
    all_to_all x2, waiting for transfers between devices, exchange(): lax.all_to_all(blocks, 'sub', split_axis=0, concat_axis=0, tiled=True)  9.51 us
  transfers between devices with their start and end apart: 3, of which 3 were waited for; matrix products, arithmetic and copies ran while one was open for 0% of the time, Pallas kernels for 5%

profile of v2, /device:TPU:2, one launch (start us, length us, event | category | flops | bytes accessed | tf_op | source)
XLA Modules:
  0.0 68.1 jit_solution(5969451273471067985)
XLA Ops:
  0.6 2.0 %pack.1 = f32[416,128]{1,0:T(8,128)} custom-call(f32[6,20,256]{2,1,0:T(8,128)} %fields_ref.1, f32[11,256]{1,0:T(8,128)} %geometry_ref.1, s32[12,1,32]{2,1,0:T(1,128)} %bitcast.11), custom_call_target="tpu_custom_call" | custom-call | flops 100000000 | bytes 1000000 | tf_op jit(solution)/shard_map/pack/pallas_call | solution.py:698
  2.6 0.0 copy-start.4
  2.6 0.0 copy-start.5
  2.6 0.0 copy-start.6
  2.7 15.6 %all-to-all-start = ((f32[32,1,1664]{2,1,0:T(1,128)}), f32[32,1,1664]{2,1,0:T(1,128)S(1)}, u32[]{:S(2)}, u32[]{:S(2)}) async-start(f32[32,1,1664]{2,1,0:T(1,128)} %bitcast.1), calls=%async_computation | async-start | bytes 425984 | tf_op jit(solution)/shard_map/all_to_all | solution.py:745
  18.3 0.0 copy-done.4
  18.3 0.0 copy-done.5
  18.3 0.0 copy-done.6
  18.3 0.0 copy-start
  18.3 0.5 plan.1
  18.9 20.1 %all-to-all-done = f32[32,1,1664]{2,1,0:T(1,128)S(1)} async-done(((f32[32,1,1664]{2,1,0:T(1,128)}), f32[32,1,1664]{2,1,0:T(1,128)S(1)}, u32[]{:S(2)}, u32[]{:S(2)}) %all-to-all-start) | async-done | bytes 213024 | tf_op jit(solution)/shard_map/all_to_all | solution.py:745
  39.0 0.0 copy-done
  39.0 1.1 %start.1 = f32[128,128]{1,0:T(8,128)} custom-call(f32[416,128]{1,0:T(8,128)S(1)} %bitcast.7, bf16[256,512]{1,0:T(8,128)(2,1)S(1)} %get-tuple-element.14.pick_ref, s32[256,128]{1,0:T(8,128)S(1)} %get-tuple-element.15.face_ref, bf16[256,256]{1,0:T(8,128)(2,1)S(1)} %copy-done), custom_call_target="tpu_custom_call" | custom-call | flops 100000000 | bytes 1000000 | tf_op jit(solution)/shard_map/start/pallas_call | solution.py:698
  40.1 0.0 copy-start.1
  40.1 0.0 copy-start.3
  40.1 7.6 %all-to-all-start.1 = ((f32[16,8,128]{2,1,0:T(8,128)}), f32[16,8,128]{2,1,0:T(8,128)S(1)}, u32[]{:S(2)}, u32[]{:S(2)}) async-start(f32[16,8,128]{2,1,0:T(8,128)} %bitcast.3), calls=%async_computation.1 | async-start | bytes 131072 | tf_op jit(solution)/shard_map/all_to_all | solution.py:767
  47.7 0.0 copy-done.1
  47.7 0.0 copy-done.3
  47.7 0.0 copy-start.2
  47.7 1.6 %arrive.1 = (f32[6,20,384]{2,1,0:T(8,128)S(1)}, f32[64,384]{1,0:T(8,128)S(1)}, f32[8,256]{1,0:T(8,128)S(1)}, f32[6,20,384]{2,1,0:T(8,128)S(1)}) custom-call(f32[416,128]{1,0:T(8,128)S(1)} %bitcast.8, s32[4,384]{1,0:T(4,128)S(1)} %copy-done.4, s32[4,384]{1,0:T(4,128)S(1)} %copy-done.5, bf16[80,96]{1,0:T(8,128)(2,1)S(1)} %copy-done.1, ...), custom_call_target="tpu_custom_call" | custom-call | flops 100000000 | bytes 1000000 | tf_op jit(solution)/shard_map/arrive/pallas_call | solution.py:698
  49.4 4.6 %all-to-all-done.1 = f32[16,8,128]{2,1,0:T(8,128)S(1)} async-done(((f32[16,8,128]{2,1,0:T(8,128)}), f32[16,8,128]{2,1,0:T(8,128)S(1)}, u32[]{:S(2)}, u32[]{:S(2)}) %all-to-all-start.1) | async-done | bytes 65568 | tf_op jit(solution)/shard_map/all_to_all | solution.py:767
  54.0 0.0 copy-done.2
  54.0 1.7 %first.1 = (f32[6,20,384]{2,1,0:T(8,128)S(1)}, f32[6,20,384]{2,1,0:T(8,128)S(1)}, f32[128,128]{1,0:T(8,128)}) custom-call(f32[128,128]{1,0:T(8,128)S(1)} %bitcast.9, f32[6,20,384]{2,1,0:T(8,128)S(1)} %get-tuple-element.18.part_ref, f32[6,20,384]{2,1,0:T(8,128)S(1)} %get-tuple-element.19.state_ref, f32[64,384]{1,0:T(8,128)S(1)} %get-tuple-element.20.derived_ref.refs_1_, ...), custom_call_target="tpu_custom_call" | custom-call | flops 100000000 | bytes 1000000 | tf_op jit(solution)/shard_map/first/pallas_call | solution.py:698
  55.7 4.8 %all-to-all-start.2 = ((f32[16,8,128]{2,1,0:T(8,128)}), f32[16,8,128]{2,1,0:T(8,128)S(1)}, u32[]{:S(2)}, u32[]{:S(2)}) async-start(f32[16,8,128]{2,1,0:T(8,128)} %bitcast.5), calls=%async_computation.2 | async-start | bytes 131072 | tf_op jit(solution)/shard_map/all_to_all | solution.py:767
  60.5 1.4 %local.1.part_ref = f32[6,20,384]{2,1,0:T(8,128)S(1)} custom-call(f32[6,20,384]{2,1,0:T(8,128)S(1)} %get-tuple-element.24.refs_0_.middle_ref, f32[64,384]{1,0:T(8,128)S(1)} %get-tuple-element.20.derived_ref.refs_1_, s32[4,384]{1,0:T(4,128)S(1)} %copy-done.4, s32[4,384]{1,0:T(4,128)S(1)} %copy-done.5, bf16[80,96]{1,0:T(8,128)(2,1)S(1)} %copy-done.1, ...), custom_call_target="tpu_custom_call" | custom-call | flops 100000000 | bytes 1000000 | tf_op jit(solution)/shard_map/local/pallas_call | solution.py:698
  61.9 4.9 %all-to-all-done.2 = f32[16,8,128]{2,1,0:T(8,128)S(1)} async-done(((f32[16,8,128]{2,1,0:T(8,128)}), f32[16,8,128]{2,1,0:T(8,128)S(1)}, u32[]{:S(2)}, u32[]{:S(2)}) %all-to-all-start.2) | async-done | bytes 65568 | tf_op jit(solution)/shard_map/all_to_all | solution.py:767
  66.8 1.3 %second.1 = (f32[6,20,384]{2,1,0:T(8,128)}, f32[6,20,384]{2,1,0:T(8,128)}) custom-call(f32[128,128]{1,0:T(8,128)S(1)} %bitcast.10, f32[6,20,384]{2,1,0:T(8,128)S(1)} %local.1.part_ref, f32[6,20,384]{2,1,0:T(8,128)S(1)} %get-tuple-element.24.refs_0_.middle_ref, f32[6,20,384]{2,1,0:T(8,128)S(1)} %get-tuple-element.25.first_ref, ...), custom_call_target="tpu_custom_call" | custom-call | flops 100000000 | bytes 1000000 | tf_op jit(solution)/shard_map/second/pallas_call | solution.py:698
Async XLA Ops:
  2.6 15.7 %copy-start.4 = (s32[4,384]{1,0:T(4,128)S(1)}, s32[4,384]{1,0:T(4,128)}, u32[]{:S(2)}) copy-start(s32[4,384]{1,0:T(4,128)} %refs_2_.1) | copy-start | bytes 18436
  2.6 15.7 %copy-start.5 = (s32[4,384]{1,0:T(4,128)S(1)}, s32[4,384]{1,0:T(4,128)}, u32[]{:S(2)}) copy-start(s32[4,384]{1,0:T(4,128)} %refs_3_.1) | copy-start | bytes 18436
  2.6 15.7 %copy-start.6 = (s32[1,16,16]{2,1,0:T(8,128)S(1)}, s32[1,16,16]{2,1,0:T(8,128)}, u32[]{:S(2)}) copy-start(s32[1,16,16]{2,1,0:T(8,128)} %list_ref.1) | copy-start | bytes 3076
  2.7 36.3 %all-to-all-start = ((f32[32,1,1664]{2,1,0:T(1,128)}), f32[32,1,1664]{2,1,0:T(1,128)S(1)}, u32[]{:S(2)}, u32[]{:S(2)}) async-start(f32[32,1,1664]{2,1,0:T(1,128)} %bitcast.1), calls=%async_computation | async-start | bytes 425984 | tf_op jit(solution)/shard_map/all_to_all | solution.py:745
  18.3 20.7 %copy-start = (bf16[256,256]{1,0:T(8,128)(2,1)S(1)}, bf16[256,256]{1,0:T(8,128)(2,1)}, u32[]{:S(2)}) copy-start(bf16[256,256]{1,0:T(8,128)(2,1)} %constant.11.clone.select_ref) | copy-start | bytes 393220
  40.1 7.6 %copy-start.1 = (bf16[80,96]{1,0:T(8,128)(2,1)S(1)}, bf16[80,96]{1,0:T(8,128)(2,1)}, u32[]{:S(2)}) copy-start(bf16[80,96]{1,0:T(8,128)(2,1)} %constant.8.clone.slope_ref.refs_4_) | copy-start | bytes 46084
  40.1 7.6 %copy-start.3 = (bf16[32,144]{1,0:T(8,128)(2,1)S(1)}, bf16[32,144]{1,0:T(8,128)(2,1)}, u32[]{:S(2)}) copy-start(bf16[32,144]{1,0:T(8,128)(2,1)} %constant.9.clone.lift_ref.refs_5_) | copy-start | bytes 27652
  40.1 13.9 %all-to-all-start.1 = ((f32[16,8,128]{2,1,0:T(8,128)}), f32[16,8,128]{2,1,0:T(8,128)S(1)}, u32[]{:S(2)}, u32[]{:S(2)}) async-start(f32[16,8,128]{2,1,0:T(8,128)} %bitcast.3), calls=%async_computation.1 | async-start | bytes 131072 | tf_op jit(solution)/shard_map/all_to_all | solution.py:767
  47.7 6.2 %copy-start.2 = (bf16[32,192]{1,0:T(8,128)(2,1)S(1)}, bf16[32,192]{1,0:T(8,128)(2,1)}, u32[]{:S(2)}) copy-start(bf16[32,192]{1,0:T(8,128)(2,1)} %constant.10.clone.lift_ref) | copy-start | bytes 36868
  55.7 11.1 %all-to-all-start.2 = ((f32[16,8,128]{2,1,0:T(8,128)}), f32[16,8,128]{2,1,0:T(8,128)S(1)}, u32[]{:S(2)}, u32[]{:S(2)}) async-start(f32[16,8,128]{2,1,0:T(8,128)} %bitcast.5), calls=%async_computation.2 | async-start | bytes 131072 | tf_op jit(solution)/shard_map/all_to_all | solution.py:767

commit v3 on v2

--- a/solution.py
+++ b/solution.py
@@ -30,6 +30,10 @@
 half_lane = lane // 2
 tiles = new_count // lane
 block_rows = slots + 1
+slab_first = 22
+sub_first = 10
+slab_order = [(slab_first + place) % slabs for place in range(slabs)]
+sub_order = [(sub_first + place) % subs for place in range(subs)]
 
 
 def volume_triples():
@@ -269,6 +273,7 @@
     turned = jnp.concatenate([turned, jnp.zeros((lane - slots, slabs), jnp.int32)], axis=0)
     turned = jnp.concatenate([turned, jnp.zeros((lane, lane - slabs), jnp.int32)], axis=1)
     codes = jnp.transpose(turned)[:slabs]
+    codes = jnp.concatenate([codes[slab_first:], codes[:slab_first]], axis=0)
     lanes = lax.broadcasted_iota(jnp.int32, (slabs, old_count), 1)
     picks = jnp.concatenate(
         [one_hot(codes[:, slot_id : slot_id + 1] == lanes) for slot_id in range(slots)], axis=0
@@ -302,6 +307,7 @@
     list_ref, link_ref, orient_ref, came_pick_ref, slot_pick_ref, face_ref, spread_ref, about_ref, codes_ref
 ):
     codes = list_ref[0]
+    codes = jnp.concatenate([codes[sub_first:], codes[:sub_first]], axis=0)
     half = traces // 2
     for idx in range(traces):
         rows = pl.ds((idx // half) * lane + idx % half, subs, stride=half)
@@ -314,7 +320,9 @@
     slot_pick_ref[...] = jnp.concatenate(
         [one_hot(element == lanes + tile * lane) for tile in range(tiles)], axis=1
     )
-    came_row = element + ((element * 5462) >> 16)
+    source = (element * 5462) >> 16
+    place = (source + slabs - slab_first) & (slabs - 1)
+    came_row = place * block_rows + element - source * slots
     came_pick_ref[...] = jnp.concatenate(
         [one_hot(came_row == lanes + tile * lane) for tile in range(tiles + 1)], axis=1
     )
@@ -325,7 +333,8 @@
     for face_id in range(faces):
         far = link_ref[face_id : face_id + 1, :] - column_count
         orient = orient_ref[face_id : face_id + 1, :]
-        column = ((far >> 3) & 1) * lane + (far >> 4) * 8 + (far & 7)
+        place = ((far >> 4) + subs - sub_first) & (subs - 1)
+        column = ((far >> 3) & 1) * lane + place * 8 + (far & 7)
         column = jnp.where((far >= 0) & (orient < 6), column, -1)
         picks = one_hot(rows == column)
         facts = jnp.where(about_rows == 0, orient, jnp.where(about_rows == 1, face_id, 0))
@@ -358,11 +367,19 @@
 
 def unpack(came_ref, state_ref, derived_ref, rows_ref, tail_ref, main_ref):
     field_rows = components * node_count
-    tail = came_ref[pl.ds(slots, slabs, stride=block_rows), :]
+    runs = ((slab_first, 0, slabs - slab_first), (0, slabs - slab_first, slab_first))
+    tail = jnp.concatenate(
+        [
+            came_ref[pl.ds(place * block_rows + slots, count, stride=block_rows), :]
+            for _, place, count in reversed(runs)
+        ],
+        axis=0,
+    )
     for slot_id in range(slots):
-        rows_ref[pl.ds(slot_id, slabs, stride=slots), :] = came_ref[
-            pl.ds(slot_id, slabs, stride=block_rows), :
-        ]
+        for source, place, count in runs:
+            rows_ref[pl.ds(source * slots + slot_id, count, stride=slots), :] = came_ref[
+                pl.ds(place * block_rows + slot_id, count, stride=block_rows), :
+            ]
         shifted = pltpu.roll(tail, lane - 3 * slot_id, 1) if slot_id else tail
         tail_ref[pl.ds(slot_id, slabs, stride=slots), :] = shifted
     main_ref[...] = jnp.transpose(rows_ref[...])
@@ -743,7 +760,8 @@
         [pl.BlockSpec(memory_space=pltpu.HBM)] * 3,
     )
     arrived = lax.all_to_all(
-        parcel.reshape(slabs, block_rows * lane), "slab", split_axis=0, concat_axis=0, tiled=True
+        parcel.reshape(slabs, block_rows * lane), "slab", split_axis=0, concat_axis=0, tiled=True,
+        axis_index_groups=[slab_order],
     ).reshape(slabs * block_rows, lane)
     came_pick, slot_pick, trace_face, spread, about = run(
         plan_kernel,
@@ -764,7 +782,9 @@
 
     def exchange(rows):
         blocks = rows.reshape(subs, traces // 2, lane)
-        came = lax.all_to_all(blocks, "sub", split_axis=0, concat_axis=0, tiled=True)
+        came = lax.all_to_all(
+            blocks, "sub", split_axis=0, concat_axis=0, tiled=True, axis_index_groups=[sub_order]
+        )
         return came.reshape(remote_count // 2, lane)
 
     incoming = exchange(outgoing)

time: 68.6 us -> 59.2 us (0.86)
  waiting for transfers between devices: 29.6 us -> 17.2 us
  starting transfers between devices: 28.1 us -> 31.1 us
    all_to_all x1, waiting for transfers between devices: 20.1 us -> 12 us  [shards(): lax.all_to_all(parcel.reshape(slabs, block_rows * lane), 'slab', split_ax...]
    all_to_all x2, waiting for transfers between devices: 9.51 us -> 5.24 us  [exchange(): lax.all_to_all(blocks, 'sub', split_axis=0, concat_axis=0, tiled=True, ax...]
    all_to_all x2, starting transfers between devices: 12.4 us -> 14.6 us  [exchange(): lax.all_to_all(blocks, 'sub', split_axis=0, concat_axis=0, tiled=True, ax...]
    all_to_all x1, starting transfers between devices: 15.6 us -> 16.4 us  [shards(): lax.all_to_all(parcel.reshape(slabs, block_rows * lane), 'slab', split_ax...]
  transfers between devices with their start and end apart: 3 -> 3, of which waited for: 3 -> 3; matrix products, arithmetic and copies ran while one was open for 0% -> 0% of each run, Pallas kernels for 5% -> 6%
where the time goes in v3:
time: 59.2 us; the launch traced here: 58.8 us
  starting transfers between devices  31.1 us (53%)
  waiting for transfers between devices  17.2 us (29%)
  Pallas kernels  9.69 us (16%)
  between operations  0.75 us (1%)
    all_to_all x1, starting transfers between devices, shards(): lax.all_to_all(parcel.reshape(slabs, block_rows * lane), 'slab', split_ax...  16.4 us
    all_to_all x2, starting transfers between devices, exchange(): lax.all_to_all(blocks, 'sub', split_axis=0, concat_axis=0, tiled=True, ax...  14.6 us
    all_to_all x1, waiting for transfers between devices, shards(): lax.all_to_all(parcel.reshape(slabs, block_rows * lane), 'slab', split_ax...  12 us
    pallas_call x7, Pallas kernels, run(): pl.pallas_call(kernel, name=name, out_shape=outs, in_specs=in_specs or [p...  9.69 us
    all_to_all x2, waiting for transfers between devices, exchange(): lax.all_to_all(blocks, 'sub', split_axis=0, concat_axis=0, tiled=True, ax...  5.24 us
  transfers between devices with their start and end apart: 3, of which 3 were waited for; matrix products, arithmetic and copies ran while one was open for 0% of the time, Pallas kernels for 6%

profile of v3, /device:TPU:2, one launch (start us, length us, event | category | flops | bytes accessed | tf_op | source)
XLA Modules:
  0.0 58.8 jit_solution(203106259875792593)
XLA Ops:
  0.6 2.0 %pack.1 = f32[416,128]{1,0:T(8,128)} custom-call(f32[6,20,256]{2,1,0:T(8,128)} %fields_ref.1, f32[11,256]{1,0:T(8,128)} %geometry_ref.1, s32[12,1,32]{2,1,0:T(1,128)} %bitcast.11), custom_call_target="tpu_custom_call" | custom-call | flops 100000000 | bytes 1000000 | tf_op jit(solution)/shard_map/pack/pallas_call | solution.py:715
  2.6 0.0 copy-start.4
  2.6 0.0 copy-start.5
  2.6 0.0 copy-start.6
  2.7 16.4 %all-to-all-start = ((f32[32,1,1664]{2,1,0:T(1,128)}), f32[32,1,1664]{2,1,0:T(1,128)S(1)}, u32[]{:S(2)}, u32[]{:S(2)}) async-start(f32[32,1,1664]{2,1,0:T(1,128)} %bitcast.1), calls=%async_computation | async-start | bytes 425984 | tf_op jit(solution)/shard_map/all_to_all | solution.py:762
  19.1 0.0 copy-done.4
  19.1 0.0 copy-done.5
  19.1 0.0 copy-done.6
  19.1 0.0 copy-start
  19.2 0.5 plan.1
  19.7 12.0 %all-to-all-done = f32[32,1,1664]{2,1,0:T(1,128)S(1)} async-done(((f32[32,1,1664]{2,1,0:T(1,128)}), f32[32,1,1664]{2,1,0:T(1,128)S(1)}, u32[]{:S(2)}, u32[]{:S(2)}) %all-to-all-start) | async-done | bytes 213024 | tf_op jit(solution)/shard_map/all_to_all | solution.py:762
  31.7 0.0 copy-done
  31.7 1.1 %start.1 = f32[128,128]{1,0:T(8,128)} custom-call(f32[416,128]{1,0:T(8,128)S(1)} %bitcast.7, bf16[256,512]{1,0:T(8,128)(2,1)S(1)} %get-tuple-element.14.pick_ref, s32[256,128]{1,0:T(8,128)S(1)} %get-tuple-element.15.face_ref, bf16[256,256]{1,0:T(8,128)(2,1)S(1)} %copy-done), custom_call_target="tpu_custom_call" | custom-call | flops 100000000 | bytes 1000000 | tf_op jit(solution)/shard_map/start/pallas_call | solution.py:715
  32.8 0.0 copy-start.1
  32.8 0.0 copy-start.3
  32.8 7.6 %all-to-all-start.1 = ((f32[16,8,128]{2,1,0:T(8,128)}), f32[16,8,128]{2,1,0:T(8,128)S(1)}, u32[]{:S(2)}, u32[]{:S(2)}) async-start(f32[16,8,128]{2,1,0:T(8,128)} %bitcast.3), calls=%async_computation.1 | async-start | bytes 131072 | tf_op jit(solution)/shard_map/all_to_all | solution.py:785
  40.4 0.0 copy-done.1
  40.4 0.0 copy-done.3
  40.4 0.0 copy-start.2
  40.4 1.6 %arrive.1 = (f32[6,20,384]{2,1,0:T(8,128)S(1)}, f32[64,384]{1,0:T(8,128)S(1)}, f32[8,256]{1,0:T(8,128)S(1)}, f32[6,20,384]{2,1,0:T(8,128)S(1)}) custom-call(f32[416,128]{1,0:T(8,128)S(1)} %bitcast.8, s32[4,384]{1,0:T(4,128)S(1)} %copy-done.4, s32[4,384]{1,0:T(4,128)S(1)} %copy-done.5, bf16[80,96]{1,0:T(8,128)(2,1)S(1)} %copy-done.1, ...), custom_call_target="tpu_custom_call" | custom-call | flops 100000000 | bytes 1000000 | tf_op jit(solution)/shard_map/arrive/pallas_call | solution.py:715
  42.0 2.5 %all-to-all-done.1 = f32[16,8,128]{2,1,0:T(8,128)S(1)} async-done(((f32[16,8,128]{2,1,0:T(8,128)}), f32[16,8,128]{2,1,0:T(8,128)S(1)}, u32[]{:S(2)}, u32[]{:S(2)}) %all-to-all-start.1) | async-done | bytes 65568 | tf_op jit(solution)/shard_map/all_to_all | solution.py:785
  44.5 0.0 copy-done.2
  44.6 1.7 %first.1 = (f32[6,20,384]{2,1,0:T(8,128)S(1)}, f32[6,20,384]{2,1,0:T(8,128)S(1)}, f32[128,128]{1,0:T(8,128)}) custom-call(f32[128,128]{1,0:T(8,128)S(1)} %bitcast.9, f32[6,20,384]{2,1,0:T(8,128)S(1)} %get-tuple-element.18.part_ref, f32[6,20,384]{2,1,0:T(8,128)S(1)} %get-tuple-element.19.state_ref, f32[64,384]{1,0:T(8,128)S(1)} %get-tuple-element.20.derived_ref.refs_1_, ...), custom_call_target="tpu_custom_call" | custom-call | flops 100000000 | bytes 1000000 | tf_op jit(solution)/shard_map/first/pallas_call | solution.py:715
  46.2 7.0 %all-to-all-start.2 = ((f32[16,8,128]{2,1,0:T(8,128)}), f32[16,8,128]{2,1,0:T(8,128)S(1)}, u32[]{:S(2)}, u32[]{:S(2)}) async-start(f32[16,8,128]{2,1,0:T(8,128)} %bitcast.5), calls=%async_computation.2 | async-start | bytes 131072 | tf_op jit(solution)/shard_map/all_to_all | solution.py:785
  53.3 1.4 %local.1.part_ref = f32[6,20,384]{2,1,0:T(8,128)S(1)} custom-call(f32[6,20,384]{2,1,0:T(8,128)S(1)} %get-tuple-element.24.refs_0_.middle_ref, f32[64,384]{1,0:T(8,128)S(1)} %get-tuple-element.20.derived_ref.refs_1_, s32[4,384]{1,0:T(4,128)S(1)} %copy-done.4, s32[4,384]{1,0:T(4,128)S(1)} %copy-done.5, bf16[80,96]{1,0:T(8,128)(2,1)S(1)} %copy-done.1, ...), custom_call_target="tpu_custom_call" | custom-call | flops 100000000 | bytes 1000000 | tf_op jit(solution)/shard_map/local/pallas_call | solution.py:715
  54.7 2.7 %all-to-all-done.2 = f32[16,8,128]{2,1,0:T(8,128)S(1)} async-done(((f32[16,8,128]{2,1,0:T(8,128)}), f32[16,8,128]{2,1,0:T(8,128)S(1)}, u32[]{:S(2)}, u32[]{:S(2)}) %all-to-all-start.2) | async-done | bytes 65568 | tf_op jit(solution)/shard_map/all_to_all | solution.py:785
  57.4 1.4 %second.1 = (f32[6,20,384]{2,1,0:T(8,128)}, f32[6,20,384]{2,1,0:T(8,128)}) custom-call(f32[128,128]{1,0:T(8,128)S(1)} %bitcast.10, f32[6,20,384]{2,1,0:T(8,128)S(1)} %local.1.part_ref, f32[6,20,384]{2,1,0:T(8,128)S(1)} %get-tuple-element.24.refs_0_.middle_ref, f32[6,20,384]{2,1,0:T(8,128)S(1)} %get-tuple-element.25.first_ref, ...), custom_call_target="tpu_custom_call" | custom-call | flops 100000000 | bytes 1000000 | tf_op jit(solution)/shard_map/second/pallas_call | solution.py:715
Async XLA Ops:
  2.6 16.5 %copy-start.4 = (s32[4,384]{1,0:T(4,128)S(1)}, s32[4,384]{1,0:T(4,128)}, u32[]{:S(2)}) copy-start(s32[4,384]{1,0:T(4,128)} %refs_2_.1) | copy-start | bytes 18436
  2.6 16.5 %copy-start.5 = (s32[4,384]{1,0:T(4,128)S(1)}, s32[4,384]{1,0:T(4,128)}, u32[]{:S(2)}) copy-start(s32[4,384]{1,0:T(4,128)} %refs_3_.1) | copy-start | bytes 18436
  2.6 16.5 %copy-start.6 = (s32[1,16,16]{2,1,0:T(8,128)S(1)}, s32[1,16,16]{2,1,0:T(8,128)}, u32[]{:S(2)}) copy-start(s32[1,16,16]{2,1,0:T(8,128)} %list_ref.1) | copy-start | bytes 3076
  2.7 29.0 %all-to-all-start = ((f32[32,1,1664]{2,1,0:T(1,128)}), f32[32,1,1664]{2,1,0:T(1,128)S(1)}, u32[]{:S(2)}, u32[]{:S(2)}) async-start(f32[32,1,1664]{2,1,0:T(1,128)} %bitcast.1), calls=%async_computation | async-start | bytes 425984 | tf_op jit(solution)/shard_map/all_to_all | solution.py:762
  19.1 12.5 %copy-start = (bf16[256,256]{1,0:T(8,128)(2,1)S(1)}, bf16[256,256]{1,0:T(8,128)(2,1)}, u32[]{:S(2)}) copy-start(bf16[256,256]{1,0:T(8,128)(2,1)} %constant.11.clone.select_ref) | copy-start | bytes 393220
  32.8 7.6 %copy-start.1 = (bf16[80,96]{1,0:T(8,128)(2,1)S(1)}, bf16[80,96]{1,0:T(8,128)(2,1)}, u32[]{:S(2)}) copy-start(bf16[80,96]{1,0:T(8,128)(2,1)} %constant.8.clone.slope_ref.refs_4_) | copy-start | bytes 46084
  32.8 7.6 %copy-start.3 = (bf16[32,144]{1,0:T(8,128)(2,1)S(1)}, bf16[32,144]{1,0:T(8,128)(2,1)}, u32[]{:S(2)}) copy-start(bf16[32,144]{1,0:T(8,128)(2,1)} %constant.9.clone.lift_ref.refs_5_) | copy-start | bytes 27652
  32.8 11.8 %all-to-all-start.1 = ((f32[16,8,128]{2,1,0:T(8,128)}), f32[16,8,128]{2,1,0:T(8,128)S(1)}, u32[]{:S(2)}, u32[]{:S(2)}) async-start(f32[16,8,128]{2,1,0:T(8,128)} %bitcast.3), calls=%async_computation.1 | async-start | bytes 131072 | tf_op jit(solution)/shard_map/all_to_all | solution.py:785
  40.4 4.1 %copy-start.2 = (bf16[32,192]{1,0:T(8,128)(2,1)S(1)}, bf16[32,192]{1,0:T(8,128)(2,1)}, u32[]{:S(2)}) copy-start(bf16[32,192]{1,0:T(8,128)(2,1)} %constant.10.clone.lift_ref) | copy-start | bytes 36868
  46.2 11.2 %all-to-all-start.2 = ((f32[16,8,128]{2,1,0:T(8,128)}), f32[16,8,128]{2,1,0:T(8,128)S(1)}, u32[]{:S(2)}, u32[]{:S(2)}) async-start(f32[16,8,128]{2,1,0:T(8,128)} %bitcast.5), calls=%async_computation.2 | async-start | bytes 131072 | tf_op jit(solution)/shard_map/all_to_all | solution.py:785

commit v4 on v3

--- a/solution.py
+++ b/solution.py
@@ -30,7 +30,7 @@
 half_lane = lane // 2
 tiles = new_count // lane
 block_rows = slots + 1
-slab_first = 22
+slab_first = 21
 sub_first = 10
 slab_order = [(slab_first + place) % slabs for place in range(slabs)]
 sub_order = [(sub_first + place) % subs for place in range(subs)]
@@ -211,11 +211,11 @@
 
 
 def remote_lift_operand():
-    stacked = np.zeros((32, 16 * faces), np.float64)
+    stacked = np.zeros((24 * faces, 16), np.float64)
     for face_id in range(faces):
         for node_id in range(face_nodes):
             for row_id in range(node_count):
-                stacked[row_id, face_id * 16 + node_id] = lift_table[row_id][
+                stacked[24 * face_id + row_id, node_id] = lift_table[row_id][
                     face_id * face_nodes + node_id
                 ]
     high, rest = bf16_pair(stacked)
@@ -303,9 +303,7 @@
     out_ref[pl.ds(slots, slabs, stride=block_rows), :] = tail
 
 
-def plan_kernel(
-    list_ref, link_ref, orient_ref, came_pick_ref, slot_pick_ref, face_ref, spread_ref, about_ref, codes_ref
-):
+def trace_codes(list_ref, codes_ref):
     codes = list_ref[0]
     codes = jnp.concatenate([codes[sub_first:], codes[:sub_first]], axis=0)
     half = traces // 2
@@ -314,18 +312,20 @@
         codes_ref[rows, :] = jnp.broadcast_to(codes[:, idx : idx + 1], (subs, lane))
     codes = codes_ref[...]
     face = face_of(codes)
-    element = codes - new_count * face
+    return face, codes - new_count * face
+
+
+def lane_picks(chosen, count):
+    lanes = lax.broadcasted_iota(jnp.int32, (remote_count, lane), 1)
+    return jnp.concatenate(
+        [one_hot(chosen == lanes + tile * lane) for tile in range(count)], axis=1
+    )
+
+
+def plan(list_ref, link_ref, orient_ref, slot_pick_ref, face_ref, spread_ref, about_ref, codes_ref):
+    face, element = trace_codes(list_ref, codes_ref)
     face_ref[...] = face
-    lanes = lax.broadcasted_iota(jnp.int32, (remote_count, lane), 1)
-    slot_pick_ref[...] = jnp.concatenate(
-        [one_hot(element == lanes + tile * lane) for tile in range(tiles)], axis=1
-    )
-    source = (element * 5462) >> 16
-    place = (source + slabs - slab_first) & (slabs - 1)
-    came_row = place * block_rows + element - source * slots
-    came_pick_ref[...] = jnp.concatenate(
-        [one_hot(came_row == lanes + tile * lane) for tile in range(tiles + 1)], axis=1
-    )
+    slot_pick_ref[...] = lane_picks(element, tiles)
     rows = lax.broadcasted_iota(jnp.int32, (remote_count, new_count), 0)
     about_rows = lax.broadcasted_iota(jnp.int32, (16, new_count), 0)
     about = None
@@ -357,12 +357,16 @@
     trace_ref[...] = jnp.where(lanes < half_lane, upper, lower)
 
 
-def start_kernel(came_ref, pick_ref, face_ref, select_ref, trace_ref):
+def start_kernel(came_ref, list_ref, select_ref, trace_ref, codes_ref):
+    face, element = trace_codes(list_ref, codes_ref)
+    source = (element * 5462) >> 16
+    place = (source + slabs - slab_first) & (slabs - 1)
+    picks = lane_picks(place * block_rows + element - source * slots, tiles + 1)
     parts = jnp.concatenate(split_two(came_ref[...]), axis=1)
     parts = jnp.concatenate(
         [parts, jnp.zeros((4 * lane - slabs * block_rows, 2 * lane), jnp.bfloat16)], axis=0
     )
-    trace_rows(dot_rows(pick_ref[...], parts), face_ref[...], select_ref, trace_ref)
+    trace_rows(dot_rows(picks, parts), face, select_ref, trace_ref)
 
 
 def unpack(came_ref, state_ref, derived_ref, rows_ref, tail_ref, main_ref):
@@ -570,17 +574,22 @@
     orient_ref,
     slope_ref,
     lift_ref,
-    spread_ref,
-    about_ref,
+    list_ref,
     state_ref,
     derived_ref,
     far_ref,
     part_ref,
+    slot_pick_ref,
+    face_ref,
+    spread_ref,
     rows_ref,
     tail_ref,
     main_ref,
+    about_ref,
+    codes_ref,
     *scratches,
 ):
+    plan(list_ref, link_ref, orient_ref, slot_pick_ref, face_ref, spread_ref, about_ref, codes_ref)
     derived_ref[...] = jnp.zeros(derived_ref.shape, jnp.float32)
     unpack(came_ref, state_ref, derived_ref, rows_ref, tail_ref, main_ref)
     compact(derived_ref, spread_ref, about_ref, far_ref)
@@ -591,46 +600,40 @@
     local_part(*refs)
 
 
-def remote_part(came_ref, far_ref, spread_ref, lift_ref, derived_ref, turned_ref, table_ref, jump_ref, flux_ref):
+def remote_part(came_ref, far_ref, spread_ref, lift_ref, derived_ref, turned_ref, jump_ref):
     turned_ref[...] = jnp.transpose(came_ref[...])
-    table_ref[...] = jnp.zeros(table_ref.shape, jnp.float32)
-    for half in range(2):
-        for node_id in range(face_nodes):
-            first_row = half * half_lane + node_id * components
-            table_ref[half, 8 * node_id : 8 * node_id + components, :] = turned_ref[
-                first_row : first_row + components, :
-            ]
-    planes = [
-        jnp.concatenate(
-            [table_ref[half, 8 * node_id : 8 * node_id + 8, :] for half in range(2)], axis=1
-        )
-        for node_id in range(face_nodes)
-    ]
+    planes = []
+    for node_id in range(face_nodes):
+        first_row = node_id * components
+        halves_of = [
+            turned_ref[half * half_lane + first_row : half * half_lane + first_row + 8, :]
+            for half in range(2)
+        ]
+        planes.append(jnp.concatenate(halves_of, axis=1))
     outside = oriented(planes, far_ref[5:6, :])
     for node_id in range(face_nodes):
         tiled_store(jump_ref, slice(8 * node_id, 8 * node_id + 8), outside[node_id])
+    blank = jnp.zeros((8 * (16 - face_nodes), remote_count), jnp.float32)
+    tiled_store(jump_ref, slice(8 * face_nodes, 128), blank)
     fluxes = face_flux(
-        lambda comp_id: strided_load(jump_ref, comp_id, face_nodes, 8),
+        lambda comp_id: strided_load(jump_ref, comp_id, 16, 8),
         [far_ref[axis_id : axis_id + 1, :] for axis_id in range(3)],
         far_ref[3:4, :],
         far_ref[4:5, :],
     )
-    flux_ref[...] = jnp.zeros(flux_ref.shape, jnp.float32)
+    high, rest = split_two(jnp.concatenate(fluxes, axis=1))
+    lifted = dot_rows(lift_ref[...], jnp.concatenate([high, rest, high], axis=0))
     face = far_ref[6:7, :]
-    for face_id in range(faces):
-        here = face == face_id
-        for comp_id, value in enumerate(fluxes):
-            columns = slice(comp_id * remote_count, (comp_id + 1) * remote_count)
-            flux_ref[16 * face_id : 16 * face_id + face_nodes, columns] = jnp.where(here, value, 0.0)
-    high, rest = split_two(flux_ref[...])
-    lifted = dot_rows(lift_ref[...], jnp.concatenate([high, rest, high], axis=0))
-    stacked = jnp.concatenate(
-        [
-            lifted[:24, comp_id * remote_count : (comp_id + 1) * remote_count]
-            for comp_id in range(components)
-        ],
-        axis=0,
-    )
+    blocks = []
+    for comp_id in range(components):
+        columns = slice(comp_id * remote_count, (comp_id + 1) * remote_count)
+        block = lifted[:24, columns]
+        for face_id in range(1, faces):
+            block = jnp.where(
+                face == face_id, lifted[24 * face_id : 24 * face_id + 24, columns], block
+            )
+        blocks.append(block)
+    stacked = jnp.concatenate(blocks, axis=0)
     placed = dot_rows(jnp.concatenate(split_two(stacked), axis=0), spread_ref[...])
     rows = 24 * components
     placed = placed[:rows] + placed[rows:]
@@ -736,12 +739,7 @@
         scratch(tiles, 8 * faces * face_nodes, lane),
         scratch(48, components * new_count),
     ]
-    remote_scratch = [
-        scratch(lane, lane),
-        scratch(2, 8 * face_nodes, lane),
-        scratch(2, 8 * face_nodes, lane),
-        scratch(16 * faces, components * remote_count),
-    ]
+    remote_scratch = [scratch(lane, lane), scratch(2, lane, lane)]
     parcel = run(
         pack_kernel,
         "pack",
@@ -763,21 +761,9 @@
         parcel.reshape(slabs, block_rows * lane), "slab", split_axis=0, concat_axis=0, tiled=True,
         axis_index_groups=[slab_order],
     ).reshape(slabs * block_rows, lane)
-    came_pick, slot_pick, trace_face, spread, about = run(
-        plan_kernel,
-        "plan",
-        (
-            halves(remote_count, 4 * lane),
-            halves(remote_count, new_count),
-            jax.ShapeDtypeStruct((remote_count, lane), jnp.int32),
-            halves(remote_count, new_count),
-            floats(8, remote_count),
-        ),
-        [pltpu.VMEM((remote_count, lane), jnp.int32)],
-        (trace_list, face_link, face_orient),
-    )
+    code_scratch = pltpu.VMEM((remote_count, lane), jnp.int32)
     outgoing = run(
-        start_kernel, "start", trace_shape, [], (arrived, came_pick, trace_face, select)
+        start_kernel, "start", trace_shape, [code_scratch], (arrived, trace_list, select)
     )
 
     def exchange(rows):
@@ -788,13 +774,27 @@
         return came.reshape(remote_count // 2, lane)
 
     incoming = exchange(outgoing)
-    state, derived, far, part = run(
+    state, derived, far, part, slot_pick, trace_face, spread = run(
         arrive_kernel,
         "arrive",
-        (state_shape, floats(64, new_count), floats(8, remote_count), state_shape),
-        [scratch(new_count, lane), scratch(new_count, lane), scratch(lane, new_count)]
+        (
+            state_shape,
+            floats(64, new_count),
+            floats(8, remote_count),
+            state_shape,
+            halves(remote_count, new_count),
+            jax.ShapeDtypeStruct((remote_count, lane), jnp.int32),
+            halves(remote_count, new_count),
+        ),
+        [
+            scratch(new_count, lane),
+            scratch(new_count, lane),
+            scratch(lane, new_count),
+            scratch(8, remote_count),
+            code_scratch,
+        ]
         + local_scratch,
-        (arrived, face_link, face_orient, slopes, lift, spread, about),
+        (arrived, face_link, face_orient, slopes, lift, trace_list),
     )
     first_res, middle, outgoing = run(
         first_kernel,

time: 59.2 us -> 57.9 us (0.978)
  blocking collectives: 0 us -> 28.4 us
  starting transfers between devices: 31.1 us -> 14.6 us
  waiting for transfers between devices: 17.2 us -> 4.85 us
  Pallas kernels: 9.69 us -> 8.97 us
    all_to_all x0 -> x1, blocking collectives: none -> 28.4 us  [shards(): lax.all_to_all(parcel.reshape(slabs, block_rows * lane), 'slab', split_ax...]
    all_to_all x1 -> x0, starting transfers between devices: 16.4 us -> none  [shards(): lax.all_to_all(parcel.reshape(slabs, block_rows * lane), 'slab', split_ax...]
    all_to_all x1 -> x0, waiting for transfers between devices: 12 us -> none  [shards(): lax.all_to_all(parcel.reshape(slabs, block_rows * lane), 'slab', split_ax...]
    pallas_call x7 -> x6, Pallas kernels: 9.69 us -> 8.97 us  [run(): pl.pallas_call(kernel, name=name, out_shape=outs, in_specs=in_specs or [p...]
  transfers between devices with their start and end apart: 3 -> 2, of which waited for: 3 -> 2; matrix products, arithmetic and copies ran while one was open for 0% -> 0% of each run, Pallas kernels for 6% -> 6%
where the time goes in v4:
time: 57.9 us; the launch traced here: 57.6 us
  blocking collectives  28.4 us (49%)
  starting transfers between devices  14.6 us (25%)
  Pallas kernels  8.97 us (15%)
  waiting for transfers between devices  4.85 us (8%)
  between operations  0.71 us (1%)
    all_to_all x1, blocking collectives, shards(): lax.all_to_all(parcel.reshape(slabs, block_rows * lane), 'slab', split_ax...  28.4 us
    all_to_all x2, starting transfers between devices, exchange(): lax.all_to_all(blocks, 'sub', split_axis=0, concat_axis=0, tiled=True, ax...  14.6 us
    pallas_call x6, Pallas kernels, run(): pl.pallas_call(kernel, name=name, out_shape=outs, in_specs=in_specs or [p...  8.97 us
    all_to_all x2, waiting for transfers between devices, exchange(): lax.all_to_all(blocks, 'sub', split_axis=0, concat_axis=0, tiled=True, ax...  4.85 us
  transfers between devices with their start and end apart: 2, of which 2 were waited for; matrix products, arithmetic and copies ran while one was open for 0% of the time, Pallas kernels for 6%

profile of v4, /device:TPU:2, one launch (start us, length us, event | category | flops | bytes accessed | tf_op | source)
XLA Modules:
  0.0 57.6 jit_solution(1213984906601107065)
XLA Ops:
  0.6 1.3 %pack.1 = f32[416,128]{1,0:T(8,128)S(1)} custom-call(f32[6,20,256]{2,1,0:T(8,128)} %fields_ref.1, f32[11,256]{1,0:T(8,128)} %geometry_ref.1, s32[12,1,32]{2,1,0:T(1,128)} %bitcast.12), custom_call_target="tpu_custom_call" | custom-call | flops 100000000 | bytes 1000000 | tf_op jit(solution)/shard_map/pack/pallas_call | solution.py:718
  1.9 0.0 copy-start
  2.0 0.0 copy-start.4
  2.0 28.4 %all_to_all.19 = f32[32,1,1664]{2,1,0:T(1,128)S(1)} all-to-all(f32[32,1,1664]{2,1,0:T(1,128)S(1)} %bitcast.9), channel_id=1, replica_groups={{336,352,368,384,400,416,432,448,464,480,496,0,16,32,48,64,80,96,112,12..., dimensions={0} | all-to-all | bytes 425984 | tf_op jit(solution)/shard_map/all_to_all | solution.py:760
  30.3 0.0 copy-done
  30.3 0.0 copy-done.4
  30.3 1.2 %start.1 = f32[128,128]{1,0:T(8,128)} custom-call(f32[416,128]{1,0:T(8,128)S(1)} %bitcast.7, s32[1,16,16]{2,1,0:T(8,128)S(1)} %copy-done.4, bf16[256,256]{1,0:T(8,128)(2,1)S(1)} %copy-done), custom_call_target="tpu_custom_call" | custom-call | flops 100000000 | bytes 1000000 | tf_op jit(solution)/shard_map/start/pallas_call | solution.py:718
  31.5 0.0 copy-start.2
  31.5 0.0 copy-start.3
  31.5 0.0 copy-start.5
  31.5 0.0 copy-start.6
  31.5 7.6 %all-to-all-start.1 = ((f32[16,8,128]{2,1,0:T(8,128)}), f32[16,8,128]{2,1,0:T(8,128)S(1)}, u32[]{:S(2)}, u32[]{:S(2)}) async-start(f32[16,8,128]{2,1,0:T(8,128)} %bitcast.3), calls=%async_computation.1 | async-start | bytes 131072 | tf_op jit(solution)/shard_map/all_to_all | solution.py:771
  39.2 0.0 copy-done.2
  39.2 0.0 copy-done.3
  39.2 0.0 copy-done.5
  39.2 0.0 copy-done.6
  39.2 0.0 copy-start.1
  39.2 2.1 %arrive.1 = (f32[6,20,384]{2,1,0:T(8,128)S(1)}, f32[64,384]{1,0:T(8,128)S(1)}, f32[8,256]{1,0:T(8,128)S(1)}, f32[6,20,384]{2,1,0:T(8,128)S(1)}, bf16[256,384]{1,...) custom-call(f32[416,128]{1,0:T(8,128)S(1)} %bitcast.8, s32[4,384]{1,0:T(4,128)S(1)} %copy-done.5, ...), custom_call_target="tpu_custom_call" | custom-call | flops 100000000 | bytes 1000000 | tf_op jit(solution)/shard_map/arrive/pallas_call | solution.py:718
  41.3 2.1 %all-to-all-done.1 = f32[16,8,128]{2,1,0:T(8,128)S(1)} async-done(((f32[16,8,128]{2,1,0:T(8,128)}), f32[16,8,128]{2,1,0:T(8,128)S(1)}, u32[]{:S(2)}, u32[]{:S(2)}) %all-to-all-start.1) | async-done | bytes 65568 | tf_op jit(solution)/shard_map/all_to_all | solution.py:771
  43.4 0.0 copy-done.1
  43.4 1.6 %first.1 = (f32[6,20,384]{2,1,0:T(8,128)S(1)}, f32[6,20,384]{2,1,0:T(8,128)S(1)}, f32[128,128]{1,0:T(8,128)}) custom-call(f32[128,128]{1,0:T(8,128)S(1)} %bitcast.10, f32[6,20,384]{2,1,0:T(8,128)S(1)} %get-tuple-element.12.part_ref, f32[6,20,384]{2,1,0:T(8,128)S(1)} %get-tuple-element.13.state_ref, f32[64,384]{1,0:T(8,128)S(1)} %get-tuple-element.14.derived_ref.refs_1_, ...), custom_call_target="tpu_custom_call" | custom-call | flops 100000000 | bytes 1000000 | tf_op jit(solution)/shard_map/first/pallas_call | solution.py:718
  45.1 7.0 %all-to-all-start.2 = ((f32[16,8,128]{2,1,0:T(8,128)}), f32[16,8,128]{2,1,0:T(8,128)S(1)}, u32[]{:S(2)}, u32[]{:S(2)}) async-start(f32[16,8,128]{2,1,0:T(8,128)} %bitcast.5), calls=%async_computation.2 | async-start | bytes 131072 | tf_op jit(solution)/shard_map/all_to_all | solution.py:771
  52.1 1.4 %local.1.part_ref = f32[6,20,384]{2,1,0:T(8,128)S(1)} custom-call(f32[6,20,384]{2,1,0:T(8,128)S(1)} %get-tuple-element.20.refs_0_.middle_ref, f32[64,384]{1,0:T(8,128)S(1)} %get-tuple-element.14.derived_ref.refs_1_, s32[4,384]{1,0:T(4,128)S(1)} %copy-done.5, s32[4,384]{1,0:T(4,128)S(1)} %copy-done.6, bf16[80,96]{1,0:T(8,128)(2,1)S(1)} %copy-done.2, ...), custom_call_target="tpu_custom_call" | custom-call | flops 100000000 | bytes 1000000 | tf_op jit(solution)/shard_map/local/pallas_call | solution.py:718
  53.5 2.7 %all-to-all-done.2 = f32[16,8,128]{2,1,0:T(8,128)S(1)} async-done(((f32[16,8,128]{2,1,0:T(8,128)}), f32[16,8,128]{2,1,0:T(8,128)S(1)}, u32[]{:S(2)}, u32[]{:S(2)}) %all-to-all-start.2) | async-done | bytes 65568 | tf_op jit(solution)/shard_map/all_to_all | solution.py:771
  56.2 1.3 %second.1 = (f32[6,20,384]{2,1,0:T(8,128)}, f32[6,20,384]{2,1,0:T(8,128)}) custom-call(f32[128,128]{1,0:T(8,128)S(1)} %bitcast.11, f32[6,20,384]{2,1,0:T(8,128)S(1)} %local.1.part_ref, f32[6,20,384]{2,1,0:T(8,128)S(1)} %get-tuple-element.20.refs_0_.middle_ref, f32[6,20,384]{2,1,0:T(8,128)S(1)} %get-tuple-element.21.first_ref, ...), custom_call_target="tpu_custom_call" | custom-call | flops 100000000 | bytes 1000000 | tf_op jit(solution)/shard_map/second/pallas_call | solution.py:718
Async XLA Ops:
  1.9 28.4 %copy-start = (bf16[256,256]{1,0:T(8,128)(2,1)S(1)}, bf16[256,256]{1,0:T(8,128)(2,1)}, u32[]{:S(2)}) copy-start(bf16[256,256]{1,0:T(8,128)(2,1)} %constant.11.clone.select_ref) | copy-start | bytes 393220
  2.0 28.4 %copy-start.4 = (s32[1,16,16]{2,1,0:T(8,128)S(1)}, s32[1,16,16]{2,1,0:T(8,128)}, u32[]{:S(2)}) copy-start(s32[1,16,16]{2,1,0:T(8,128)} %list_ref.3) | copy-start | bytes 3076
  31.5 7.6 %copy-start.2 = (bf16[80,96]{1,0:T(8,128)(2,1)S(1)}, bf16[80,96]{1,0:T(8,128)(2,1)}, u32[]{:S(2)}) copy-start(bf16[80,96]{1,0:T(8,128)(2,1)} %constant.8.clone.slope_ref.refs_4_) | copy-start | bytes 46084
  31.5 7.6 %copy-start.3 = (bf16[32,144]{1,0:T(8,128)(2,1)S(1)}, bf16[32,144]{1,0:T(8,128)(2,1)}, u32[]{:S(2)}) copy-start(bf16[32,144]{1,0:T(8,128)(2,1)} %constant.9.clone.lift_ref.refs_5_) | copy-start | bytes 27652
  31.5 7.6 %copy-start.5 = (s32[4,384]{1,0:T(4,128)S(1)}, s32[4,384]{1,0:T(4,128)}, u32[]{:S(2)}) copy-start(s32[4,384]{1,0:T(4,128)} %refs_2_.1) | copy-start | bytes 18436
  31.5 7.7 %copy-start.6 = (s32[4,384]{1,0:T(4,128)S(1)}, s32[4,384]{1,0:T(4,128)}, u32[]{:S(2)}) copy-start(s32[4,384]{1,0:T(4,128)} %refs_3_.1) | copy-start | bytes 18436
  31.5 11.9 %all-to-all-start.1 = ((f32[16,8,128]{2,1,0:T(8,128)}), f32[16,8,128]{2,1,0:T(8,128)S(1)}, u32[]{:S(2)}, u32[]{:S(2)}) async-start(f32[16,8,128]{2,1,0:T(8,128)} %bitcast.3), calls=%async_computation.1 | async-start | bytes 131072 | tf_op jit(solution)/shard_map/all_to_all | solution.py:771
  39.2 4.2 %copy-start.1 = (bf16[96,48]{1,0:T(8,128)(2,1)S(1)}, bf16[96,48]{1,0:T(8,128)(2,1)}, u32[]{:S(2)}) copy-start(bf16[96,48]{1,0:T(8,128)(2,1)} %constant.10.clone.lift_ref) | copy-start | bytes 27652
  45.1 11.2 %all-to-all-start.2 = ((f32[16,8,128]{2,1,0:T(8,128)}), f32[16,8,128]{2,1,0:T(8,128)S(1)}, u32[]{:S(2)}, u32[]{:S(2)}) async-start(f32[16,8,128]{2,1,0:T(8,128)} %bitcast.5), calls=%async_computation.2 | async-start | bytes 131072 | tf_op jit(solution)/shard_map/all_to_all | solution.py:771

commit v5 on v4

--- a/solution.py
+++ b/solution.py
@@ -222,17 +222,6 @@
     return jnp.asarray(np.concatenate([high, high, rest], axis=1))
 
 
-def select_operand():
-    table = np.zeros((2 * lane, faces * half_lane), np.float32)
-    for face_id in range(faces):
-        for part_id in range(2):
-            for node_id in range(face_nodes):
-                for comp_id in range(components):
-                    row_id = part_id * lane + comp_id * node_count + face_mask[face_id][node_id]
-                    table[row_id, face_id * half_lane + node_id * components + comp_id] = 1.0
-    return jnp.asarray(table.astype(ml_dtypes.bfloat16))
-
-
 def split_two(value):
     high = value.astype(jnp.bfloat16)
     rest = (value - high.astype(jnp.float32)).astype(jnp.bfloat16)
@@ -322,10 +311,10 @@
     )
 
 
-def plan(list_ref, link_ref, orient_ref, slot_pick_ref, face_ref, spread_ref, about_ref, codes_ref):
+def plan(list_ref, link_ref, orient_ref, chosen_ref, spread_ref, about_ref, codes_ref):
     face, element = trace_codes(list_ref, codes_ref)
-    face_ref[...] = face
-    slot_pick_ref[...] = lane_picks(element, tiles)
+    chosen_ref[...] = node_lanes(face)
+    slot_picks = lane_picks(element, tiles)
     rows = lax.broadcasted_iota(jnp.int32, (remote_count, new_count), 0)
     about_rows = lax.broadcasted_iota(jnp.int32, (16, new_count), 0)
     about = None
@@ -343,21 +332,33 @@
         spread = picks if spread is None else spread + picks
     spread_ref[...] = spread
     about_ref[...] = about[:8]
-
-
-def trace_rows(found, face, select_ref, trace_ref):
-    wide = dot_rows(found.astype(jnp.bfloat16), select_ref[...])
-    near = jnp.where(face >= 2, wide[:, lane:], wide[:, :lane])
-    odd = (face & 1) == 1
+    return slot_picks
+
+
+def node_lanes(face):
+    lanes = lax.broadcasted_iota(jnp.int32, (1, lane), 1) % half_lane
+    node = lanes // components
+    comp = lanes - node * components
+    tables = []
+    for face_id in range(faces):
+        row = jnp.zeros((1, lane), jnp.int32)
+        for node_id in range(face_nodes):
+            row = jnp.where(node == node_id, face_mask[face_id][node_id], row)
+        tables.append(comp * node_count + row)
+    chosen = tables[0]
+    for face_id in range(1, faces):
+        chosen = jnp.where(face == face_id, tables[face_id], chosen)
+    return chosen
+
+
+def trace_rows(found, chosen):
+    turned = jnp.take_along_axis(found, chosen, axis=1, mode="promise_in_bounds")
     half = remote_count // 2
-    upper, lower = near[:half], near[half:]
-    upper = jnp.where(odd[:half], pltpu.roll(upper, half_lane, 1), upper)
-    lower = jnp.where(odd[half:], lower, pltpu.roll(lower, half_lane, 1))
     lanes = lax.broadcasted_iota(jnp.int32, (half, lane), 1)
-    trace_ref[...] = jnp.where(lanes < half_lane, upper, lower)
-
-
-def start_kernel(came_ref, list_ref, select_ref, trace_ref, codes_ref):
+    return jnp.where(lanes < half_lane, turned[:half], turned[half:])
+
+
+def start_kernel(came_ref, list_ref, trace_ref, codes_ref):
     face, element = trace_codes(list_ref, codes_ref)
     source = (element * 5462) >> 16
     place = (source + slabs - slab_first) & (slabs - 1)
@@ -366,7 +367,8 @@
     parts = jnp.concatenate(
         [parts, jnp.zeros((4 * lane - slabs * block_rows, 2 * lane), jnp.bfloat16)], axis=0
     )
-    trace_rows(dot_rows(picks, parts), face, select_ref, trace_ref)
+    found = dot_rows(picks, parts)
+    trace_ref[...] = trace_rows(found[:, :lane] + found[:, lane:], node_lanes(face))
 
 
 def unpack(came_ref, state_ref, derived_ref, rows_ref, tail_ref, main_ref):
@@ -512,18 +514,25 @@
         current = state_ref[comp_id]
         tiled_store(nodes_ref, pl.ds(comp_id, node_count, stride=8), current)
         flat_ref[0:node_count, comp_id * new_count : (comp_id + 1) * new_count] = current
-    stacked = jnp.concatenate(split_two(tiled_load(nodes_ref, slice(None))), axis=0)
+    stacked = jnp.concatenate(split_two(tiled_load(nodes_ref, slice(None))), axis=1)
     rows = lax.broadcasted_iota(jnp.int32, (new_count, new_count), 0)
+    links = [link_ref[face_id : face_id + 1, :] for face_id in range(faces)]
+    owners = [face_of(link) for link in links]
+    picks = [
+        one_hot(rows == jnp.where(link < column_count, link - new_count * owner, -1))
+        for link, owner in zip(links, owners)
+    ]
+    found_pairs = []
+    for first in range(0, faces, 2):
+        both = jnp.concatenate(picks[first : first + 2], axis=1)
+        found_pairs.append(dot_rows(stacked, jnp.concatenate([both, both], axis=0)))
     comp_rows = lax.broadcasted_iota(jnp.int32, (8, new_count), 0)
     wall_gain = jnp.where(comp_rows >= 3, -2.0, 0.0)
     for face_id in range(faces):
-        link = link_ref[face_id : face_id + 1, :]
         orient = orient_ref[face_id : face_id + 1, :]
-        owner = face_of(link)
-        element = jnp.where(link < column_count, link - new_count * owner, -1)
-        found = dot_rows(stacked, one_hot(rows == element))
-        found = found[: 8 * node_count] + found[8 * node_count :]
-        owner_masks = [owner == other for other in range(faces)]
+        first_column = (face_id % 2) * new_count
+        found = found_pairs[face_id // 2][:, first_column : first_column + new_count]
+        owner_masks = [owners[face_id] == other for other in range(faces)]
         planes = []
         for node_id in range(face_nodes):
             value = None
@@ -579,9 +588,11 @@
     derived_ref,
     far_ref,
     part_ref,
-    slot_pick_ref,
-    face_ref,
+    chosen_ref,
     spread_ref,
+    shared_ref,
+    known_ref,
+    scale_ref,
     rows_ref,
     tail_ref,
     main_ref,
@@ -589,18 +600,34 @@
     codes_ref,
     *scratches,
 ):
-    plan(list_ref, link_ref, orient_ref, slot_pick_ref, face_ref, spread_ref, about_ref, codes_ref)
+    picks = plan(list_ref, link_ref, orient_ref, chosen_ref, spread_ref, about_ref, codes_ref)
+    shared_ref[...] = dot_lanes(picks, spread_ref[...]).astype(jnp.bfloat16)
     derived_ref[...] = jnp.zeros(derived_ref.shape, jnp.float32)
     unpack(came_ref, state_ref, derived_ref, rows_ref, tail_ref, main_ref)
     compact(derived_ref, spread_ref, about_ref, far_ref)
     local_part(state_ref, derived_ref, link_ref, orient_ref, slope_ref, lift_ref, part_ref, *scratches)
+    field_rows = components * node_count
+    gain = section_b1 * time_step
+    for comp_id in range(components):
+        main_ref[comp_id * node_count : (comp_id + 1) * node_count, :] = (
+            state_ref[comp_id] + gain * part_ref[comp_id]
+        )
+    main_ref[field_rows : field_rows + 1, :] = gain * derived_ref[10:11, :]
+    main_ref[field_rows + 1 : field_rows + 2, :] = gain * derived_ref[9:10, :]
+    main_ref[field_rows + 2 :, :] = jnp.zeros((6, new_count), jnp.float32)
+    found = dot_lanes(picks, jnp.concatenate(split_two(main_ref[...]), axis=0))
+    found = found[:, :lane] + found[:, lane:]
+    known_ref[...] = trace_rows(found, chosen_ref[...])
+    lanes = lax.broadcasted_iota(jnp.int32, (remote_count, lane), 1) % half_lane
+    comp = lanes - (lanes // components) * components
+    scale_ref[...] = trace_rows(found, jnp.where(comp < 3, field_rows, field_rows + 1))
 
 
 def local_kernel(*refs):
     local_part(*refs)
 
 
-def remote_part(came_ref, far_ref, spread_ref, lift_ref, derived_ref, turned_ref, jump_ref):
+def remote_part(came_ref, far_ref, lift_ref, turned_ref, jump_ref):
     turned_ref[...] = jnp.transpose(came_ref[...])
     planes = []
     for node_id in range(face_nodes):
@@ -633,6 +660,10 @@
                 face == face_id, lifted[24 * face_id : 24 * face_id + 24, columns], block
             )
         blocks.append(block)
+    return blocks
+
+
+def placed_part(blocks, spread_ref, derived_ref):
     stacked = jnp.concatenate(blocks, axis=0)
     placed = dot_rows(jnp.concatenate(split_two(stacked), axis=0), spread_ref[...])
     rows = 24 * components
@@ -655,25 +686,33 @@
     far_ref,
     spread_ref,
     lift_ref,
-    pick_ref,
-    face_ref,
-    select_ref,
+    shared_ref,
+    known_ref,
+    scale_ref,
+    chosen_ref,
     residual_ref,
     middle_ref,
     trace_ref,
-    main_ref,
+    send_ref,
+    sem,
+    packed_ref,
     *scratches,
 ):
-    changes = remote_part(came_ref, far_ref, spread_ref, lift_ref, derived_ref, *scratches)
-    main_ref[components * node_count :, :] = jnp.zeros((8, new_count), jnp.float32)
+    blocks = remote_part(came_ref, far_ref, lift_ref, *scratches)
+    for comp_id, block in enumerate(blocks):
+        packed_ref[comp_id * node_count : (comp_id + 1) * node_count, :] = block[:node_count]
+    packed_ref[components * node_count :, :] = jnp.zeros((8, remote_count), jnp.float32)
+    found = dot_lanes(shared_ref[...], jnp.concatenate(split_two(packed_ref[...]), axis=0))
+    found = trace_rows(found[:, :lane] + found[:, lane:], chosen_ref[...])
+    send_ref[...] = known_ref[...] + scale_ref[...] * found
+    copy = pltpu.make_async_copy(send_ref, trace_ref, sem)
+    copy.start()
+    changes = placed_part(blocks, spread_ref, derived_ref)
     for comp_id in range(components):
         residual = time_step * (part_ref[comp_id] + changes[comp_id])
-        middle = state_ref[comp_id] + section_b1 * residual
         residual_ref[comp_id] = residual
-        middle_ref[comp_id] = middle
-        main_ref[comp_id * node_count : (comp_id + 1) * node_count, :] = middle
-    parts = jnp.concatenate(split_two(main_ref[...]), axis=0)
-    trace_rows(dot_lanes(pick_ref[...], parts), face_ref[...], select_ref, trace_ref)
+        middle_ref[comp_id] = state_ref[comp_id] + section_b1 * residual
+    copy.wait()
 
 
 def second_kernel(
@@ -689,7 +728,8 @@
     residual_ref,
     *scratches,
 ):
-    changes = remote_part(came_ref, far_ref, spread_ref, lift_ref, derived_ref, *scratches)
+    blocks = remote_part(came_ref, far_ref, lift_ref, *scratches)
+    changes = placed_part(blocks, spread_ref, derived_ref)
     for comp_id in range(components):
         residual = section_a2 * first_ref[comp_id] + time_step * (
             part_ref[comp_id] + changes[comp_id]
@@ -702,10 +742,6 @@
     return jax.ShapeDtypeStruct(shape, jnp.float32)
 
 
-def near(*shape):
-    return pltpu.VMEM(shape, jnp.float32)
-
-
 def halves(*shape):
     return jax.ShapeDtypeStruct(shape, jnp.bfloat16)
 
@@ -714,12 +750,17 @@
     return pltpu.VMEM(shape, jnp.float32)
 
 
-def run(kernel, name, outs, scratches, operands, in_specs=None):
+fast = pl.BlockSpec(memory_space=pltpu.VMEM)
+free = pl.BlockSpec(memory_space=pl.ANY)
+
+
+def run(kernel, name, outs, scratches, operands, in_specs=None, out_specs=None):
     return pl.pallas_call(
         kernel,
         name=name,
         out_shape=outs,
-        in_specs=in_specs or [pl.BlockSpec(memory_space=pltpu.VMEM)] * len(operands),
+        in_specs=in_specs or [fast] * len(operands),
+        out_specs=out_specs or jax.tree.map(lambda _: fast, outs),
         scratch_shapes=scratches,
         compiler_params=pltpu.CompilerParams(vmem_limit_bytes=24 * 2**20),
         cost_estimate=pl.CostEstimate(flops=10**8, bytes_accessed=10**6, transcendentals=0),
@@ -730,9 +771,8 @@
     slopes = slope_operand()
     lift = lift_operand()
     remote_lift = remote_lift_operand()
-    select = select_operand()
     state_shape = floats(components, node_count, new_count)
-    trace_shape = near(remote_count // 2, lane)
+    trace_shape = floats(remote_count // 2, lane)
     local_scratch = [
         scratch(tiles, 8 * node_count, lane),
         scratch(32, components * new_count),
@@ -743,7 +783,7 @@
     parcel = run(
         pack_kernel,
         "pack",
-        near(slabs * block_rows, lane),
+        floats(slabs * block_rows, lane),
         [
             scratch(components, node_count, old_count),
             scratch(11, old_count),
@@ -763,7 +803,7 @@
     ).reshape(slabs * block_rows, lane)
     code_scratch = pltpu.VMEM((remote_count, lane), jnp.int32)
     outgoing = run(
-        start_kernel, "start", trace_shape, [code_scratch], (arrived, trace_list, select)
+        start_kernel, "start", trace_shape, [code_scratch], (arrived, trace_list)
     )
 
     def exchange(rows):
@@ -774,7 +814,7 @@
         return came.reshape(remote_count // 2, lane)
 
     incoming = exchange(outgoing)
-    state, derived, far, part, slot_pick, trace_face, spread = run(
+    state, derived, far, part, chosen, spread, shared, known, scale = run(
         arrive_kernel,
         "arrive",
         (
@@ -782,9 +822,11 @@
             floats(64, new_count),
             floats(8, remote_count),
             state_shape,
-            halves(remote_count, new_count),
             jax.ShapeDtypeStruct((remote_count, lane), jnp.int32),
             halves(remote_count, new_count),
+            halves(remote_count, remote_count),
+            floats(remote_count // 2, lane),
+            floats(remote_count // 2, lane),
         ),
         [
             scratch(new_count, lane),
@@ -800,7 +842,8 @@
         first_kernel,
         "first",
         (state_shape, state_shape, trace_shape),
-        [scratch(lane, new_count)] + remote_scratch,
+        [scratch(remote_count // 2, lane), pltpu.SemaphoreType.DMA, scratch(lane, remote_count)]
+        + remote_scratch,
         (
             incoming,
             part,
@@ -809,10 +852,12 @@
             far,
             spread,
             remote_lift,
-            slot_pick,
-            trace_face,
-            select,
+            shared,
+            known,
+            scale,
+            chosen,
         ),
+        out_specs=(fast, fast, free),
     )
     incoming = exchange(outgoing)
     part = run(

time: 57.9 us -> 57.4 us (level)
  transfers between devices with their start and end apart: 2 -> 2, of which waited for: 2 -> 2; matrix products, arithmetic and copies ran while one was open for 0% -> 0% of each run, Pallas kernels for 6% -> 7%
where the time goes in v5:
time: 57.4 us; the launch traced here: 57 us
  blocking collectives  28.2 us (49%)
  starting transfers between devices  14.7 us (26%)
  Pallas kernels  8.83 us (15%)
  waiting for transfers between devices  4.55 us (8%)
  between operations  0.71 us (1%)
    all_to_all x1, blocking collectives, shards(): lax.all_to_all(parcel.reshape(slabs, block_rows * lane), 'slab', split_ax...  28.2 us
    all_to_all x2, starting transfers between devices, exchange(): lax.all_to_all(blocks, 'sub', split_axis=0, concat_axis=0, tiled=True, ax...  14.7 us
    pallas_call x6, Pallas kernels, run(): pl.pallas_call(kernel, name=name, out_shape=outs, in_specs=in_specs or [f...  8.83 us
    all_to_all x2, waiting for transfers between devices, exchange(): lax.all_to_all(blocks, 'sub', split_axis=0, concat_axis=0, tiled=True, ax...  4.55 us
  transfers between devices with their start and end apart: 2, of which 2 were waited for; matrix products, arithmetic and copies ran while one was open for 0% of the time, Pallas kernels for 7%

profile of v5, /device:TPU:2, one launch (start us, length us, event | category | flops | bytes accessed | tf_op | source)
XLA Modules:
  0.0 57.0 jit_solution(1887095626950315249)
XLA Ops:
  0.6 1.3 %pack.1 = f32[416,128]{1,0:T(8,128)S(1)} custom-call(f32[6,20,256]{2,1,0:T(8,128)} %fields_ref.1, f32[11,256]{1,0:T(8,128)} %geometry_ref.1, s32[12,1,32]{2,1,0:T(1,128)} %bitcast.12), custom_call_target="tpu_custom_call" | custom-call | flops 100000000 | bytes 1000000 | tf_op jit(solution)/shard_map/pack/pallas_call | solution.py:758
  1.9 0.0 copy-start.5
  2.0 28.2 %all_to_all.19 = f32[32,1,1664]{2,1,0:T(1,128)S(1)} all-to-all(f32[32,1,1664]{2,1,0:T(1,128)S(1)} %bitcast.7), channel_id=1, replica_groups={{336,352,368,384,400,416,432,448,464,480,496,0,16,32,48,64,80,96,112,12..., dimensions={0} | all-to-all | bytes 425984 | tf_op jit(solution)/shard_map/all_to_all | solution.py:800
  30.2 0.0 copy-done.5
  30.2 1.0 %start.1 = f32[128,128]{1,0:T(8,128)} custom-call(f32[416,128]{1,0:T(8,128)S(1)} %bitcast.10, s32[1,16,16]{2,1,0:T(8,128)S(1)} %copy-done.5), custom_call_target="tpu_custom_call" | custom-call | flops 100000000 | bytes 1000000 | tf_op jit(solution)/shard_map/start/pallas_call | solution.py:758
  31.2 0.0 copy-start.1
  31.2 0.0 copy-start.2
  31.2 0.0 copy-start.3
  31.2 0.0 copy-start.4
  31.2 7.6 %all-to-all-start.1 = ((f32[16,8,128]{2,1,0:T(8,128)}), f32[16,8,128]{2,1,0:T(8,128)S(1)}, u32[]{:S(2)}, u32[]{:S(2)}) async-start(f32[16,8,128]{2,1,0:T(8,128)} %bitcast.3), calls=%async_computation.1 | async-start | bytes 131072 | tf_op jit(solution)/shard_map/all_to_all | solution.py:811
  38.8 0.0 copy-done.1
  38.9 0.0 copy-done.2
  38.9 0.0 copy-done.3
  38.9 0.0 copy-done.4
  38.9 0.0 copy-start
  38.9 2.4 %arrive.1 = (f32[6,20,384]{2,1,0:T(8,128)S(1)}, f32[64,384]{1,0:T(8,128)S(1)}, f32[8,256]{1,0:T(8,128)S(1)}, f32[6,20,384]{2,1,0:T(8,128)S(1)}, s32[256,128]{1,0...) custom-call(f32[416,128]{1,0:T(8,128)S(1)} %bitcast.11, ...), custom_call_target="tpu_custom_call" | custom-call | flops 100000000 | bytes 1000000 | tf_op jit(solution)/shard_map/arrive/pallas_call | solution.py:758
  41.3 1.8 %all-to-all-done.1 = f32[16,8,128]{2,1,0:T(8,128)S(1)} async-done(((f32[16,8,128]{2,1,0:T(8,128)}), f32[16,8,128]{2,1,0:T(8,128)S(1)}, u32[]{:S(2)}, u32[]{:S(2)}) %all-to-all-start.1) | async-done | bytes 65568 | tf_op jit(solution)/shard_map/all_to_all | solution.py:811
  43.1 0.0 copy-done
  43.1 1.4 %first.1 = (f32[6,20,384]{2,1,0:T(8,128)S(1)}, f32[6,20,384]{2,1,0:T(8,128)S(1)}, f32[128,128]{1,0:T(8,128)}) custom-call(f32[128,128]{1,0:T(8,128)S(1)} %bitcast.8, f32[6,20,384]{2,1,0:T(8,128)S(1)} %get-tuple-element.14.part_ref, f32[6,20,384]{2,1,0:T(8,128)S(1)} %get-tuple-element.15.state_ref, f32[64,384]{1,0:T(8,128)S(1)} %get-tuple-element.16.derived_ref.refs_1_, ...), custom_call_target="tpu_custom_call" | custom-call | flops 100000000 | bytes 1000000 | tf_op jit(solution)/shard_map/first/pallas_call | solution.py:758
  44.5 7.0 %all-to-all-start.2 = ((f32[16,8,128]{2,1,0:T(8,128)}), f32[16,8,128]{2,1,0:T(8,128)S(1)}, u32[]{:S(2)}, u32[]{:S(2)}) async-start(f32[16,8,128]{2,1,0:T(8,128)} %bitcast.5), calls=%async_computation.2 | async-start | bytes 131072 | tf_op jit(solution)/shard_map/all_to_all | solution.py:811
  51.5 1.4 %local.1.part_ref = f32[6,20,384]{2,1,0:T(8,128)S(1)} custom-call(f32[6,20,384]{2,1,0:T(8,128)S(1)} %get-tuple-element.24.refs_0_.middle_ref, f32[64,384]{1,0:T(8,128)S(1)} %get-tuple-element.16.derived_ref.refs_1_, s32[4,384]{1,0:T(4,128)S(1)} %copy-done.3, s32[4,384]{1,0:T(4,128)S(1)} %copy-done.4, bf16[80,96]{1,0:T(8,128)(2,1)S(1)} %copy-done.1, ...), custom_call_target="tpu_custom_call" | custom-call | flops 100000000 | bytes 1000000 | tf_op jit(solution)/shard_map/local/pallas_call | solution.py:758
  53.0 2.7 %all-to-all-done.2 = f32[16,8,128]{2,1,0:T(8,128)S(1)} async-done(((f32[16,8,128]{2,1,0:T(8,128)}), f32[16,8,128]{2,1,0:T(8,128)S(1)}, u32[]{:S(2)}, u32[]{:S(2)}) %all-to-all-start.2) | async-done | bytes 65568 | tf_op jit(solution)/shard_map/all_to_all | solution.py:811
  55.7 1.3 %second.1 = (f32[6,20,384]{2,1,0:T(8,128)}, f32[6,20,384]{2,1,0:T(8,128)}) custom-call(f32[128,128]{1,0:T(8,128)S(1)} %bitcast.9, f32[6,20,384]{2,1,0:T(8,128)S(1)} %local.1.part_ref, f32[6,20,384]{2,1,0:T(8,128)S(1)} %get-tuple-element.24.refs_0_.middle_ref, f32[6,20,384]{2,1,0:T(8,128)S(1)} %get-tuple-element.25.first_ref, ...), custom_call_target="tpu_custom_call" | custom-call | flops 100000000 | bytes 1000000 | tf_op jit(solution)/shard_map/second/pallas_call | solution.py:758
Async XLA Ops:
  1.9 28.2 %copy-start.5 = (s32[1,16,16]{2,1,0:T(8,128)S(1)}, s32[1,16,16]{2,1,0:T(8,128)}, u32[]{:S(2)}) copy-start(s32[1,16,16]{2,1,0:T(8,128)} %list_ref.3) | copy-start | bytes 3076
  31.2 7.6 %copy-start.1 = (bf16[80,96]{1,0:T(8,128)(2,1)S(1)}, bf16[80,96]{1,0:T(8,128)(2,1)}, u32[]{:S(2)}) copy-start(bf16[80,96]{1,0:T(8,128)(2,1)} %constant.6.clone.slope_ref.refs_4_) | copy-start | bytes 46084
  31.2 7.6 %copy-start.2 = (bf16[32,144]{1,0:T(8,128)(2,1)S(1)}, bf16[32,144]{1,0:T(8,128)(2,1)}, u32[]{:S(2)}) copy-start(bf16[32,144]{1,0:T(8,128)(2,1)} %constant.7.clone.lift_ref.refs_5_) | copy-start | bytes 27652
  31.2 7.6 %copy-start.3 = (s32[4,384]{1,0:T(4,128)S(1)}, s32[4,384]{1,0:T(4,128)}, u32[]{:S(2)}) copy-start(s32[4,384]{1,0:T(4,128)} %refs_2_.1) | copy-start | bytes 18436
  31.2 7.7 %copy-start.4 = (s32[4,384]{1,0:T(4,128)S(1)}, s32[4,384]{1,0:T(4,128)}, u32[]{:S(2)}) copy-start(s32[4,384]{1,0:T(4,128)} %refs_3_.1) | copy-start | bytes 18436
  31.2 11.9 %all-to-all-start.1 = ((f32[16,8,128]{2,1,0:T(8,128)}), f32[16,8,128]{2,1,0:T(8,128)S(1)}, u32[]{:S(2)}, u32[]{:S(2)}) async-start(f32[16,8,128]{2,1,0:T(8,128)} %bitcast.3), calls=%async_computation.1 | async-start | bytes 131072 | tf_op jit(solution)/shard_map/all_to_all | solution.py:811
  38.9 4.2 %copy-start = (bf16[96,48]{1,0:T(8,128)(2,1)S(1)}, bf16[96,48]{1,0:T(8,128)(2,1)}, u32[]{:S(2)}) copy-start(bf16[96,48]{1,0:T(8,128)(2,1)} %constant.8.clone.lift_ref) | copy-start | bytes 27652
  44.5 11.2 %all-to-all-start.2 = ((f32[16,8,128]{2,1,0:T(8,128)}), f32[16,8,128]{2,1,0:T(8,128)S(1)}, u32[]{:S(2)}, u32[]{:S(2)}) async-start(f32[16,8,128]{2,1,0:T(8,128)} %bitcast.5), calls=%async_computation.2 | async-start | bytes 131072 | tf_op jit(solution)/shard_map/all_to_all | solution.py:811

commit v6 on v5

--- a/solution.py
+++ b/solution.py
@@ -179,11 +179,15 @@
     return slopes, lifting, face_mask, node_perms
 
 
-def bf16_pair(matrix):
-    wide = np.asarray(matrix, np.float32)
-    high = wide.astype(ml_dtypes.bfloat16)
-    rest = (wide - high.astype(np.float32)).astype(ml_dtypes.bfloat16)
-    return high, rest
+def bf16_terms(matrix):
+    rest = np.asarray(matrix, np.float64)
+    parts = []
+    for _ in range(3):
+        part = rest.astype(np.float32).astype(ml_dtypes.bfloat16)
+        parts.append(part)
+        rest = rest - part.astype(np.float64)
+    order = (0, 0, 1, 0, 1, 2)
+    return jnp.asarray(np.concatenate([parts[place] for place in order], axis=1))
 
 
 slope_table, lift_table, face_mask, node_perms = dg_tables()
@@ -194,8 +198,7 @@
     for axis_id in range(3):
         first_row = axis_id * 24
         stacked[first_row : first_row + node_count, :node_count] = slope_table[axis_id]
-    high, rest = bf16_pair(stacked)
-    return jnp.asarray(np.concatenate([high, high, rest], axis=1))
+    return bf16_terms(stacked)
 
 
 def lift_operand():
@@ -206,8 +209,7 @@
                 stacked[row_id, node_id * faces + face_id] = lift_table[row_id][
                     face_id * face_nodes + node_id
                 ]
-    high, rest = bf16_pair(stacked)
-    return jnp.asarray(np.concatenate([high, high, rest], axis=1))
+    return bf16_terms(stacked)
 
 
 def remote_lift_operand():
@@ -218,14 +220,30 @@
                 stacked[24 * face_id + row_id, node_id] = lift_table[row_id][
                     face_id * face_nodes + node_id
                 ]
-    high, rest = bf16_pair(stacked)
-    return jnp.asarray(np.concatenate([high, high, rest], axis=1))
+    return bf16_terms(stacked)
 
 
 def split_two(value):
     high = value.astype(jnp.bfloat16)
     rest = (value - high.astype(jnp.float32)).astype(jnp.bfloat16)
     return high, rest
+
+
+def split_three(value):
+    high = value.astype(jnp.bfloat16)
+    left = value - high.astype(jnp.float32)
+    middle = left.astype(jnp.bfloat16)
+    rest = (left - middle.astype(jnp.float32)).astype(jnp.bfloat16)
+    return high, middle, rest
+
+
+def table_terms(value):
+    high, middle, rest = split_three(value)
+    return jnp.concatenate([high, middle, high, rest, middle, high], axis=0)
+
+
+def three_lanes(found):
+    return found[:, :lane] + found[:, lane : 2 * lane] + found[:, 2 * lane :]
 
 
 def dot_rows(left, right):
@@ -273,9 +291,9 @@
         held_ref[comp_id * node_count : (comp_id + 1) * node_count, :] = took_ref[comp_id]
     held_ref[field_rows : field_rows + 11, :] = geo_ref[...]
     held_ref[field_rows + 11 :, :] = jnp.zeros((13, old_count), jnp.float32)
-    parts = jnp.concatenate(split_two(held_ref[...]), axis=1)
-    parts = jnp.concatenate([parts, jnp.zeros((112, 2 * old_count), jnp.bfloat16)], axis=0)
-    moved = dot_lanes(jnp.concatenate([picks, picks], axis=1), parts)
+    parts = jnp.concatenate(split_three(held_ref[...]), axis=1)
+    parts = jnp.concatenate([parts, jnp.zeros((112, 3 * old_count), jnp.bfloat16)], axis=0)
+    moved = dot_lanes(jnp.concatenate([picks, picks, picks], axis=1), parts)
     short = lax.broadcasted_iota(jnp.int32, (slabs, lane), 1)
     diagonal = (short == field_rows) | (short == field_rows + 4)
     tail = jnp.zeros((slabs, lane), jnp.float32)
@@ -363,12 +381,11 @@
     source = (element * 5462) >> 16
     place = (source + slabs - slab_first) & (slabs - 1)
     picks = lane_picks(place * block_rows + element - source * slots, tiles + 1)
-    parts = jnp.concatenate(split_two(came_ref[...]), axis=1)
+    parts = jnp.concatenate(split_three(came_ref[...]), axis=1)
     parts = jnp.concatenate(
-        [parts, jnp.zeros((4 * lane - slabs * block_rows, 2 * lane), jnp.bfloat16)], axis=0
-    )
-    found = dot_rows(picks, parts)
-    trace_ref[...] = trace_rows(found[:, :lane] + found[:, lane:], node_lanes(face))
+        [parts, jnp.zeros((4 * lane - slabs * block_rows, 3 * lane), jnp.bfloat16)], axis=0
+    )
+    trace_ref[...] = trace_rows(three_lanes(dot_rows(picks, parts)), node_lanes(face))
 
 
 def unpack(came_ref, state_ref, derived_ref, rows_ref, tail_ref, main_ref):
@@ -413,9 +430,9 @@
 
 
 def compact(derived_ref, spread_ref, about_ref, far_ref):
-    stacked = jnp.concatenate(split_two(derived_ref[16:64, :]), axis=0)
+    stacked = jnp.concatenate(split_three(derived_ref[16:64, :]), axis=0)
     found = dot_lanes(stacked, spread_ref[...])
-    found = found[:48] + found[48:]
+    found = found[:48] + found[48:96] + found[96:]
     face = about_ref[1:2, :]
     for block in range(5):
         first_row = 8 * block
@@ -482,8 +499,7 @@
             faces * face_nodes, new_count
         )
     flux_ref[40:48, :] = jnp.zeros((8, components * new_count), jnp.float32)
-    high, rest = split_two(flux_ref[...])
-    return dot_rows(lift_ref[...], jnp.concatenate([high, rest, high], axis=0))
+    return dot_rows(lift_ref[...], table_terms(flux_ref[...]))
 
 
 def strided_load(ref, start, size, stride):
@@ -514,7 +530,7 @@
         current = state_ref[comp_id]
         tiled_store(nodes_ref, pl.ds(comp_id, node_count, stride=8), current)
         flat_ref[0:node_count, comp_id * new_count : (comp_id + 1) * new_count] = current
-    stacked = jnp.concatenate(split_two(tiled_load(nodes_ref, slice(None))), axis=1)
+    stacked = jnp.concatenate(split_three(tiled_load(nodes_ref, slice(None))), axis=1)
     rows = lax.broadcasted_iota(jnp.int32, (new_count, new_count), 0)
     links = [link_ref[face_id : face_id + 1, :] for face_id in range(faces)]
     owners = [face_of(link) for link in links]
@@ -525,7 +541,7 @@
     found_pairs = []
     for first in range(0, faces, 2):
         both = jnp.concatenate(picks[first : first + 2], axis=1)
-        found_pairs.append(dot_rows(stacked, jnp.concatenate([both, both], axis=0)))
+        found_pairs.append(dot_rows(stacked, jnp.concatenate([both, both, both], axis=0)))
     comp_rows = lax.broadcasted_iota(jnp.int32, (8, new_count), 0)
     wall_gain = jnp.where(comp_rows >= 3, -2.0, 0.0)
     for face_id in range(faces):
@@ -550,8 +566,7 @@
             target = 8 * (node_id * faces + face_id)
             tiled_store(jump_ref, slice(target, target + 8), jump)
     lifted = lifted_flux(jump_ref, flux_ref, derived_ref, lift_ref)
-    high, rest = split_two(flat_ref[...])
-    slopes = dot_rows(slope_ref[...], jnp.concatenate([high, rest, high], axis=0))
+    slopes = dot_rows(slope_ref[...], table_terms(flat_ref[...]))
     inverse_jac = [
         [derived_ref[3 * row_id + axis_id : 3 * row_id + axis_id + 1, :] for axis_id in range(3)]
         for row_id in range(3)
@@ -615,8 +630,7 @@
     main_ref[field_rows : field_rows + 1, :] = gain * derived_ref[10:11, :]
     main_ref[field_rows + 1 : field_rows + 2, :] = gain * derived_ref[9:10, :]
     main_ref[field_rows + 2 :, :] = jnp.zeros((6, new_count), jnp.float32)
-    found = dot_lanes(picks, jnp.concatenate(split_two(main_ref[...]), axis=0))
-    found = found[:, :lane] + found[:, lane:]
+    found = three_lanes(dot_lanes(picks, jnp.concatenate(split_three(main_ref[...]), axis=0)))
     known_ref[...] = trace_rows(found, chosen_ref[...])
     lanes = lax.broadcasted_iota(jnp.int32, (remote_count, lane), 1) % half_lane
     comp = lanes - (lanes // components) * components
@@ -648,8 +662,7 @@
         far_ref[3:4, :],
         far_ref[4:5, :],
     )
-    high, rest = split_two(jnp.concatenate(fluxes, axis=1))
-    lifted = dot_rows(lift_ref[...], jnp.concatenate([high, rest, high], axis=0))
+    lifted = dot_rows(lift_ref[...], table_terms(jnp.concatenate(fluxes, axis=1)))
     face = far_ref[6:7, :]
     blocks = []
     for comp_id in range(components):
@@ -663,18 +676,20 @@
     return blocks
 
 
-def placed_part(blocks, spread_ref, derived_ref):
-    stacked = jnp.concatenate(blocks, axis=0)
-    placed = dot_rows(jnp.concatenate(split_two(stacked), axis=0), spread_ref[...])
-    rows = 24 * components
-    placed = placed[:rows] + placed[rows:]
-    inverse_eps = derived_ref[9:10, :]
-    inverse_mu = derived_ref[10:11, :]
+def placed_part(blocks, spread_ref, derived_ref, wanted):
+    stacked = jnp.concatenate([blocks[comp_id] for comp_id in wanted], axis=0)
+    rows = stacked.shape[0]
+    parts = split_three(stacked)
+    if rows % 16:
+        blank = jnp.zeros((8, remote_count), jnp.float32)
+        parts = split_three(jnp.concatenate([stacked, blank], axis=0))
+    step = parts[0].shape[0]
+    placed = dot_rows(jnp.concatenate(parts, axis=0), spread_ref[...])
+    placed = placed[:rows] + placed[step : step + rows] + placed[2 * step : 2 * step + rows]
+    scales = [derived_ref[10:11, :] if comp_id < 3 else derived_ref[9:10, :] for comp_id in wanted]
     return [
-        (placed[24 * comp_id : 24 * comp_id + 24] * (inverse_mu if comp_id < 3 else inverse_eps))[
-            :node_count
-        ]
-        for comp_id in range(components)
+        (placed[24 * place : 24 * place + 24] * scale)[:node_count]
+        for place, scale in enumerate(scales)
     ]
 
 
@@ -707,7 +722,7 @@
     send_ref[...] = known_ref[...] + scale_ref[...] * found
     copy = pltpu.make_async_copy(send_ref, trace_ref, sem)
     copy.start()
-    changes = placed_part(blocks, spread_ref, derived_ref)
+    changes = placed_part(blocks, spread_ref, derived_ref, range(components))
     for comp_id in range(components):
         residual = time_step * (part_ref[comp_id] + changes[comp_id])
         residual_ref[comp_id] = residual
@@ -726,16 +741,28 @@
     lift_ref,
     advanced_ref,
     residual_ref,
+    done_ref,
+    sems,
     *scratches,
 ):
     blocks = remote_part(came_ref, far_ref, lift_ref, *scratches)
-    changes = placed_part(blocks, spread_ref, derived_ref)
-    for comp_id in range(components):
-        residual = section_a2 * first_ref[comp_id] + time_step * (
-            part_ref[comp_id] + changes[comp_id]
-        )
-        residual_ref[comp_id] = residual
-        advanced_ref[comp_id] = middle_ref[comp_id] + section_b2 * residual
+    copies = []
+    for first in range(0, components, 3):
+        changes = placed_part(blocks, spread_ref, derived_ref, range(first, first + 3))
+        for comp_id, change in zip(range(first, first + 3), changes):
+            residual = section_a2 * first_ref[comp_id] + time_step * (part_ref[comp_id] + change)
+            done_ref[0, comp_id] = middle_ref[comp_id] + section_b2 * residual
+            done_ref[1, comp_id] = residual
+        for place, out_ref in enumerate((advanced_ref, residual_ref)):
+            copy = pltpu.make_async_copy(
+                done_ref.at[place, pl.ds(first, 3)],
+                out_ref.at[pl.ds(first, 3)],
+                sems.at[place, first // 3],
+            )
+            copy.start()
+            copies.append(copy)
+    for copy in copies:
+        copy.wait()
 
 
 def floats(*shape):
@@ -871,8 +898,10 @@
         second_kernel,
         "second",
         (state_shape, state_shape),
-        remote_scratch,
+        [scratch(2, components, node_count, new_count), pltpu.SemaphoreType.DMA((2, 2))]
+        + remote_scratch,
         (incoming, part, middle, first_res, derived, far, spread, remote_lift),
+        out_specs=(free, free),
     )
 
 

time: 57.4 us -> 57.5 us (level)
  Pallas kernels: 8.83 us -> 9.46 us
    pallas_call x6, Pallas kernels: 8.83 us -> 9.46 us  [run(): pl.pallas_call(kernel, name=name, out_shape=outs, in_specs=in_specs or [f...]
  transfers between devices with their start and end apart: 2 -> 2, of which waited for: 2 -> 2; matrix products, arithmetic and copies ran while one was open for 0% -> 0% of each run, Pallas kernels for 7% -> 8%
where the time goes in v6:
time: 57.5 us; the launch traced here: 57.1 us
  blocking collectives  28.2 us (49%)
  starting transfers between devices  14.7 us (26%)
  Pallas kernels  9.46 us (16%)
  waiting for transfers between devices  4.05 us (7%)
  between operations  0.71 us (1%)
    all_to_all x1, blocking collectives, shards(): lax.all_to_all(parcel.reshape(slabs, block_rows * lane), 'slab', split_ax...  28.2 us
    all_to_all x2, starting transfers between devices, exchange(): lax.all_to_all(blocks, 'sub', split_axis=0, concat_axis=0, tiled=True, ax...  14.7 us
    pallas_call x6, Pallas kernels, run(): pl.pallas_call(kernel, name=name, out_shape=outs, in_specs=in_specs or [f...  9.46 us
    all_to_all x2, waiting for transfers between devices, exchange(): lax.all_to_all(blocks, 'sub', split_axis=0, concat_axis=0, tiled=True, ax...  4.05 us
  transfers between devices with their start and end apart: 2, of which 2 were waited for; matrix products, arithmetic and copies ran while one was open for 0% of the time, Pallas kernels for 8%

profile of v6, /device:TPU:2, one launch (start us, length us, event | category | flops | bytes accessed | tf_op | source)
XLA Modules:
  0.0 57.1 jit_solution(2216523414908457790)
XLA Ops:
  0.6 1.4 %pack.1 = f32[416,128]{1,0:T(8,128)S(1)} custom-call(f32[6,20,256]{2,1,0:T(8,128)} %fields_ref.1, f32[11,256]{1,0:T(8,128)} %geometry_ref.1, s32[12,1,32]{2,1,0:T(1,128)} %bitcast.12), custom_call_target="tpu_custom_call" | custom-call | flops 100000000 | bytes 1000000 | tf_op jit(solution)/shard_map/pack/pallas_call | solution.py:785
  2.0 0.0 copy-start.5
  2.0 28.2 %all_to_all.19 = f32[32,1,1664]{2,1,0:T(1,128)S(1)} all-to-all(f32[32,1,1664]{2,1,0:T(1,128)S(1)} %bitcast.7), channel_id=1, replica_groups={{336,352,368,384,400,416,432,448,464,480,496,0,16,32,48,64,80,96,112,12..., dimensions={0} | all-to-all | bytes 425984 | tf_op jit(solution)/shard_map/all_to_all | solution.py:827
  30.2 0.0 copy-done.5
  30.2 1.1 %start.1 = f32[128,128]{1,0:T(8,128)} custom-call(f32[416,128]{1,0:T(8,128)S(1)} %bitcast.10, s32[1,16,16]{2,1,0:T(8,128)S(1)} %copy-done.5), custom_call_target="tpu_custom_call" | custom-call | flops 100000000 | bytes 1000000 | tf_op jit(solution)/shard_map/start/pallas_call | solution.py:785
  31.4 0.0 copy-start.1
  31.4 0.0 copy-start.2
  31.4 0.0 copy-start.3
  31.4 0.0 copy-start.4
  31.4 7.6 %all-to-all-start.1 = ((f32[16,8,128]{2,1,0:T(8,128)}), f32[16,8,128]{2,1,0:T(8,128)S(1)}, u32[]{:S(2)}, u32[]{:S(2)}) async-start(f32[16,8,128]{2,1,0:T(8,128)} %bitcast.3), calls=%async_computation.1 | async-start | bytes 131072 | tf_op jit(solution)/shard_map/all_to_all | solution.py:838
  39.0 0.0 copy-done.1
  39.0 0.0 copy-done.2
  39.0 0.0 copy-done.3
  39.0 0.0 copy-done.4
  39.0 0.0 copy-start
  39.0 2.7 %arrive.1 = (f32[6,20,384]{2,1,0:T(8,128)S(1)}, f32[64,384]{1,0:T(8,128)S(1)}, f32[8,256]{1,0:T(8,128)S(1)}, f32[6,20,384]{2,1,0:T(8,128)S(1)}, s32[256,128]{1,0...) custom-call(f32[416,128]{1,0:T(8,128)S(1)} %bitcast.11, ...), custom_call_target="tpu_custom_call" | custom-call | flops 100000000 | bytes 1000000 | tf_op jit(solution)/shard_map/arrive/pallas_call | solution.py:785
  41.7 1.5 %all-to-all-done.1 = f32[16,8,128]{2,1,0:T(8,128)S(1)} async-done(((f32[16,8,128]{2,1,0:T(8,128)}), f32[16,8,128]{2,1,0:T(8,128)S(1)}, u32[]{:S(2)}, u32[]{:S(2)}) %all-to-all-start.1) | async-done | bytes 65568 | tf_op jit(solution)/shard_map/all_to_all | solution.py:838
  43.2 0.0 copy-done
  43.2 1.4 %first.1 = (f32[6,20,384]{2,1,0:T(8,128)S(1)}, f32[6,20,384]{2,1,0:T(8,128)S(1)}, f32[128,128]{1,0:T(8,128)}) custom-call(f32[128,128]{1,0:T(8,128)S(1)} %bitcast.8, f32[6,20,384]{2,1,0:T(8,128)S(1)} %get-tuple-element.14.part_ref, f32[6,20,384]{2,1,0:T(8,128)S(1)} %get-tuple-element.15.state_ref, f32[64,384]{1,0:T(8,128)S(1)} %get-tuple-element.16.derived_ref.refs_1_, ...), custom_call_target="tpu_custom_call" | custom-call | flops 100000000 | bytes 1000000 | tf_op jit(solution)/shard_map/first/pallas_call | solution.py:785
  44.6 7.0 %all-to-all-start.2 = ((f32[16,8,128]{2,1,0:T(8,128)}), f32[16,8,128]{2,1,0:T(8,128)S(1)}, u32[]{:S(2)}, u32[]{:S(2)}) async-start(f32[16,8,128]{2,1,0:T(8,128)} %bitcast.5), calls=%async_computation.2 | async-start | bytes 131072 | tf_op jit(solution)/shard_map/all_to_all | solution.py:838
  51.7 1.6 %local.1.part_ref = f32[6,20,384]{2,1,0:T(8,128)S(1)} custom-call(f32[6,20,384]{2,1,0:T(8,128)S(1)} %get-tuple-element.24.refs_0_.middle_ref, f32[64,384]{1,0:T(8,128)S(1)} %get-tuple-element.16.derived_ref.refs_1_, s32[4,384]{1,0:T(4,128)S(1)} %copy-done.3, s32[4,384]{1,0:T(4,128)S(1)} %copy-done.4, bf16[80,192]{1,0:T(8,128)(2,1)S(1)} %copy-done.1, ...), custom_call_target="tpu_custom_call" | custom-call | flops 100000000 | bytes 1000000 | tf_op jit(solution)/shard_map/local/pallas_call | solution.py:785
  53.3 2.5 %all-to-all-done.2 = f32[16,8,128]{2,1,0:T(8,128)S(1)} async-done(((f32[16,8,128]{2,1,0:T(8,128)}), f32[16,8,128]{2,1,0:T(8,128)S(1)}, u32[]{:S(2)}, u32[]{:S(2)}) %all-to-all-start.2) | async-done | bytes 65568 | tf_op jit(solution)/shard_map/all_to_all | solution.py:838
  55.8 1.3 %second.1 = (f32[6,20,384]{2,1,0:T(8,128)}, f32[6,20,384]{2,1,0:T(8,128)}) custom-call(f32[128,128]{1,0:T(8,128)S(1)} %bitcast.9, f32[6,20,384]{2,1,0:T(8,128)S(1)} %local.1.part_ref, f32[6,20,384]{2,1,0:T(8,128)S(1)} %get-tuple-element.24.refs_0_.middle_ref, f32[6,20,384]{2,1,0:T(8,128)S(1)} %get-tuple-element.25.first_ref, ...), custom_call_target="tpu_custom_call" | custom-call | flops 100000000 | bytes 1000000 | tf_op jit(solution)/shard_map/second/pallas_call | solution.py:785
Async XLA Ops:
  2.0 28.2 %copy-start.5 = (s32[1,16,16]{2,1,0:T(8,128)S(1)}, s32[1,16,16]{2,1,0:T(8,128)}, u32[]{:S(2)}) copy-start(s32[1,16,16]{2,1,0:T(8,128)} %list_ref.3) | copy-start | bytes 3076
  31.4 7.6 %copy-start.1 = (bf16[80,192]{1,0:T(8,128)(2,1)S(1)}, bf16[80,192]{1,0:T(8,128)(2,1)}, u32[]{:S(2)}) copy-start(bf16[80,192]{1,0:T(8,128)(2,1)} %constant.6.clone.slope_ref.refs_4_) | copy-start | bytes 92164
  31.4 7.6 %copy-start.2 = (bf16[32,288]{1,0:T(8,128)(2,1)S(1)}, bf16[32,288]{1,0:T(8,128)(2,1)}, u32[]{:S(2)}) copy-start(bf16[32,288]{1,0:T(8,128)(2,1)} %constant.7.clone.lift_ref.refs_5_) | copy-start | bytes 55300
  31.4 7.6 %copy-start.3 = (s32[4,384]{1,0:T(4,128)S(1)}, s32[4,384]{1,0:T(4,128)}, u32[]{:S(2)}) copy-start(s32[4,384]{1,0:T(4,128)} %refs_2_.1) | copy-start | bytes 18436
  31.4 7.7 %copy-start.4 = (s32[4,384]{1,0:T(4,128)S(1)}, s32[4,384]{1,0:T(4,128)}, u32[]{:S(2)}) copy-start(s32[4,384]{1,0:T(4,128)} %refs_3_.1) | copy-start | bytes 18436
  31.4 11.9 %all-to-all-start.1 = ((f32[16,8,128]{2,1,0:T(8,128)}), f32[16,8,128]{2,1,0:T(8,128)S(1)}, u32[]{:S(2)}, u32[]{:S(2)}) async-start(f32[16,8,128]{2,1,0:T(8,128)} %bitcast.3), calls=%async_computation.1 | async-start | bytes 131072 | tf_op jit(solution)/shard_map/all_to_all | solution.py:838
  39.0 4.2 %copy-start = (bf16[96,96]{1,0:T(8,128)(2,1)S(1)}, bf16[96,96]{1,0:T(8,128)(2,1)}, u32[]{:S(2)}) copy-start(bf16[96,96]{1,0:T(8,128)(2,1)} %constant.8.clone.lift_ref) | copy-start | bytes 55300
  44.6 11.2 %all-to-all-start.2 = ((f32[16,8,128]{2,1,0:T(8,128)}), f32[16,8,128]{2,1,0:T(8,128)S(1)}, u32[]{:S(2)}, u32[]{:S(2)}) async-start(f32[16,8,128]{2,1,0:T(8,128)} %bitcast.5), calls=%async_computation.2 | async-start | bytes 131072 | tf_op jit(solution)/shard_map/all_to_all | solution.py:838

commit v7 on v6

--- a/solution.py
+++ b/solution.py
@@ -329,10 +329,7 @@
     )
 
 
-def plan(list_ref, link_ref, orient_ref, chosen_ref, spread_ref, about_ref, codes_ref):
-    face, element = trace_codes(list_ref, codes_ref)
-    chosen_ref[...] = node_lanes(face)
-    slot_picks = lane_picks(element, tiles)
+def plan(link_ref, orient_ref, spread_ref, about_ref):
     rows = lax.broadcasted_iota(jnp.int32, (remote_count, new_count), 0)
     about_rows = lax.broadcasted_iota(jnp.int32, (16, new_count), 0)
     about = None
@@ -350,7 +347,6 @@
         spread = picks if spread is None else spread + picks
     spread_ref[...] = spread
     about_ref[...] = about[:8]
-    return slot_picks
 
 
 def node_lanes(face):
@@ -376,8 +372,18 @@
     return jnp.where(lanes < half_lane, turned[:half], turned[half:])
 
 
-def start_kernel(came_ref, list_ref, trace_ref, codes_ref):
+def start_kernel(
+    came_ref,
+    list_ref,
+    trace_ref,
+    chosen_ref,
+    picks_ref,
+    send_ref,
+    codes_ref,
+    sem,
+):
     face, element = trace_codes(list_ref, codes_ref)
+    chosen = node_lanes(face)
     source = (element * 5462) >> 16
     place = (source + slabs - slab_first) & (slabs - 1)
     picks = lane_picks(place * block_rows + element - source * slots, tiles + 1)
@@ -385,7 +391,12 @@
     parts = jnp.concatenate(
         [parts, jnp.zeros((4 * lane - slabs * block_rows, 3 * lane), jnp.bfloat16)], axis=0
     )
-    trace_ref[...] = trace_rows(three_lanes(dot_rows(picks, parts)), node_lanes(face))
+    send_ref[...] = trace_rows(three_lanes(dot_rows(picks, parts)), chosen)
+    copy = pltpu.make_async_copy(send_ref, trace_ref, sem)
+    copy.start()
+    chosen_ref[...] = chosen
+    picks_ref[...] = lane_picks(element, tiles)
+    copy.wait()
 
 
 def unpack(came_ref, state_ref, derived_ref, rows_ref, tail_ref, main_ref):
@@ -598,25 +609,24 @@
     orient_ref,
     slope_ref,
     lift_ref,
-    list_ref,
+    chosen_ref,
+    picks_ref,
     state_ref,
     derived_ref,
     far_ref,
     part_ref,
-    chosen_ref,
+    known_ref,
+    scale_ref,
     spread_ref,
     shared_ref,
-    known_ref,
-    scale_ref,
     rows_ref,
     tail_ref,
     main_ref,
     about_ref,
-    codes_ref,
     *scratches,
 ):
-    picks = plan(list_ref, link_ref, orient_ref, chosen_ref, spread_ref, about_ref, codes_ref)
-    shared_ref[...] = dot_lanes(picks, spread_ref[...]).astype(jnp.bfloat16)
+    plan(link_ref, orient_ref, spread_ref, about_ref)
+    shared_ref[...] = dot_lanes(picks_ref[...], spread_ref[...]).astype(jnp.bfloat16)
     derived_ref[...] = jnp.zeros(derived_ref.shape, jnp.float32)
     unpack(came_ref, state_ref, derived_ref, rows_ref, tail_ref, main_ref)
     compact(derived_ref, spread_ref, about_ref, far_ref)
@@ -630,7 +640,7 @@
     main_ref[field_rows : field_rows + 1, :] = gain * derived_ref[10:11, :]
     main_ref[field_rows + 1 : field_rows + 2, :] = gain * derived_ref[9:10, :]
     main_ref[field_rows + 2 :, :] = jnp.zeros((6, new_count), jnp.float32)
-    found = three_lanes(dot_lanes(picks, jnp.concatenate(split_three(main_ref[...]), axis=0)))
+    found = three_lanes(dot_lanes(picks_ref[...], jnp.concatenate(split_three(main_ref[...]), axis=0)))
     known_ref[...] = trace_rows(found, chosen_ref[...])
     lanes = lax.broadcasted_iota(jnp.int32, (remote_count, lane), 1) % half_lane
     comp = lanes - (lanes // components) * components
@@ -828,9 +838,21 @@
         parcel.reshape(slabs, block_rows * lane), "slab", split_axis=0, concat_axis=0, tiled=True,
         axis_index_groups=[slab_order],
     ).reshape(slabs * block_rows, lane)
-    code_scratch = pltpu.VMEM((remote_count, lane), jnp.int32)
-    outgoing = run(
-        start_kernel, "start", trace_shape, [code_scratch], (arrived, trace_list)
+    outgoing, chosen, picks = run(
+        start_kernel,
+        "start",
+        (
+            trace_shape,
+            jax.ShapeDtypeStruct((remote_count, lane), jnp.int32),
+            halves(remote_count, new_count),
+        ),
+        [
+            scratch(remote_count // 2, lane),
+            pltpu.VMEM((remote_count, lane), jnp.int32),
+            pltpu.SemaphoreType.DMA,
+        ],
+        (arrived, trace_list),
+        out_specs=(free, fast, fast),
     )
 
     def exchange(rows):
@@ -841,7 +863,7 @@
         return came.reshape(remote_count // 2, lane)
 
     incoming = exchange(outgoing)
-    state, derived, far, part, chosen, spread, shared, known, scale = run(
+    state, derived, far, part, known, scale, spread, shared = run(
         arrive_kernel,
         "arrive",
         (
@@ -849,21 +871,19 @@
             floats(64, new_count),
             floats(8, remote_count),
             state_shape,
-            jax.ShapeDtypeStruct((remote_count, lane), jnp.int32),
+            floats(remote_count // 2, lane),
+            floats(remote_count // 2, lane),
             halves(remote_count, new_count),
             halves(remote_count, remote_count),
-            floats(remote_count // 2, lane),
-            floats(remote_count // 2, lane),
         ),
         [
             scratch(new_count, lane),
             scratch(new_count, lane),
             scratch(lane, new_count),
             scratch(8, remote_count),
-            code_scratch,
         ]
         + local_scratch,
-        (arrived, face_link, face_orient, slopes, lift, trace_list),
+        (arrived, face_link, face_orient, slopes, lift, chosen, picks),
     )
     first_res, middle, outgoing = run(
         first_kernel,

time: 57.5 us -> 57.6 us (level)
  transfers between devices with their start and end apart: 2 -> 2, of which waited for: 2 -> 2; matrix products, arithmetic and copies ran while one was open for 0% -> 0% of each run, Pallas kernels for 8% -> 7%
where the time goes in v7:
time: 57.6 us; the launch traced here: 57.2 us
  blocking collectives  28.2 us (49%)
  starting transfers between devices  14.7 us (26%)
  Pallas kernels  9.47 us (16%)
  waiting for transfers between devices  4.08 us (7%)
  between operations  0.74 us (1%)
    all_to_all x1, blocking collectives, shards(): lax.all_to_all(parcel.reshape(slabs, block_rows * lane), 'slab', split_ax...  28.2 us
    all_to_all x2, starting transfers between devices, exchange(): lax.all_to_all(blocks, 'sub', split_axis=0, concat_axis=0, tiled=True, ax...  14.7 us
    pallas_call x6, Pallas kernels, run(): pl.pallas_call(kernel, name=name, out_shape=outs, in_specs=in_specs or [f...  9.47 us
    all_to_all x2, waiting for transfers between devices, exchange(): lax.all_to_all(blocks, 'sub', split_axis=0, concat_axis=0, tiled=True, ax...  4.08 us
  transfers between devices with their start and end apart: 2, of which 2 were waited for; matrix products, arithmetic and copies ran while one was open for 0% of the time, Pallas kernels for 7%

profile of v7, /device:TPU:2, one launch (start us, length us, event | category | flops | bytes accessed | tf_op | source)
XLA Modules:
  0.0 57.2 jit_solution(18408878919895709080)
XLA Ops:
  0.6 1.4 %pack.1 = f32[416,128]{1,0:T(8,128)S(1)} custom-call(f32[6,20,256]{2,1,0:T(8,128)} %fields_ref.1, f32[11,256]{1,0:T(8,128)} %geometry_ref.1, s32[12,1,32]{2,1,0:T(1,128)} %bitcast.12), custom_call_target="tpu_custom_call" | custom-call | flops 100000000 | bytes 1000000 | tf_op jit(solution)/shard_map/pack/pallas_call | solution.py:795
  2.0 0.0 copy-start.5
  2.0 28.2 %all_to_all.19 = f32[32,1,1664]{2,1,0:T(1,128)S(1)} all-to-all(f32[32,1,1664]{2,1,0:T(1,128)S(1)} %bitcast.7), channel_id=1, replica_groups={{336,352,368,384,400,416,432,448,464,480,496,0,16,32,48,64,80,96,112,12..., dimensions={0} | all-to-all | bytes 425984 | tf_op jit(solution)/shard_map/all_to_all | solution.py:837
  30.2 0.0 copy-done.5
  30.2 1.2 %start.1 = (f32[128,128]{1,0:T(8,128)}, s32[256,128]{1,0:T(8,128)S(1)}, bf16[256,384]{1,0:T(8,128)(2,1)S(1)}) custom-call(f32[416,128]{1,0:T(8,128)S(1)} %bitcast.8, s32[1,16,16]{2,1,0:T(8,128)S(1)} %copy-done.5), custom_call_target="tpu_custom_call" | custom-call | flops 100000000 | bytes 1000000 | tf_op jit(solution)/shard_map/start/pallas_call | solution.py:795
  31.4 0.0 copy-start
  31.4 0.0 copy-start.1
  31.4 0.0 copy-start.3
  31.4 0.0 copy-start.4
  31.5 7.6 %all-to-all-start.1 = ((f32[16,8,128]{2,1,0:T(8,128)}), f32[16,8,128]{2,1,0:T(8,128)S(1)}, u32[]{:S(2)}, u32[]{:S(2)}) async-start(f32[16,8,128]{2,1,0:T(8,128)} %bitcast.3), calls=%async_computation.1 | async-start | bytes 131072 | tf_op jit(solution)/shard_map/all_to_all | solution.py:860
  39.1 0.0 copy-done
  39.1 0.0 copy-done.1
  39.1 0.0 copy-done.3
  39.1 0.0 copy-done.4
  39.1 0.0 copy-start.2
  39.1 2.7 %arrive.1 = (f32[6,20,384]{2,1,0:T(8,128)S(1)}, f32[64,384]{1,0:T(8,128)S(1)}, f32[8,256]{1,0:T(8,128)S(1)}, f32[6,20,384]{2,1,0:T(8,128)S(1)}, f32[128,128]{1,0...) custom-call(f32[416,128]{1,0:T(8,128)S(1)} %bitcast.9, ...), custom_call_target="tpu_custom_call" | custom-call | flops 100000000 | bytes 1000000 | tf_op jit(solution)/shard_map/arrive/pallas_call | solution.py:795
  41.8 1.5 %all-to-all-done.1 = f32[16,8,128]{2,1,0:T(8,128)S(1)} async-done(((f32[16,8,128]{2,1,0:T(8,128)}), f32[16,8,128]{2,1,0:T(8,128)S(1)}, u32[]{:S(2)}, u32[]{:S(2)}) %all-to-all-start.1) | async-done | bytes 65568 | tf_op jit(solution)/shard_map/all_to_all | solution.py:860
  43.3 0.0 copy-done.2
  43.3 1.4 %first.1 = (f32[6,20,384]{2,1,0:T(8,128)S(1)}, f32[6,20,384]{2,1,0:T(8,128)S(1)}, f32[128,128]{1,0:T(8,128)}) custom-call(f32[128,128]{1,0:T(8,128)S(1)} %bitcast.10, f32[6,20,384]{2,1,0:T(8,128)S(1)} %get-tuple-element.19.part_ref, f32[6,20,384]{2,1,0:T(8,128)S(1)} %get-tuple-element.20.state_ref, f32[64,384]{1,0:T(8,128)S(1)} %get-tuple-element.21.derived_ref.refs_1_, ...), custom_call_target="tpu_custom_call" | custom-call | flops 100000000 | bytes 1000000 | tf_op jit(solution)/shard_map/first/pallas_call | solution.py:795
  44.7 7.0 %all-to-all-start.2 = ((f32[16,8,128]{2,1,0:T(8,128)}), f32[16,8,128]{2,1,0:T(8,128)S(1)}, u32[]{:S(2)}, u32[]{:S(2)}) async-start(f32[16,8,128]{2,1,0:T(8,128)} %bitcast.5), calls=%async_computation.2 | async-start | bytes 131072 | tf_op jit(solution)/shard_map/all_to_all | solution.py:860
  51.7 1.6 %local.1.part_ref = f32[6,20,384]{2,1,0:T(8,128)S(1)} custom-call(f32[6,20,384]{2,1,0:T(8,128)S(1)} %get-tuple-element.28.refs_0_.middle_ref, f32[64,384]{1,0:T(8,128)S(1)} %get-tuple-element.21.derived_ref.refs_1_, s32[4,384]{1,0:T(4,128)S(1)} %copy-done.3, s32[4,384]{1,0:T(4,128)S(1)} %copy-done.4, bf16[80,192]{1,0:T(8,128)(2,1)S(1)} %copy-done, ...), custom_call_target="tpu_custom_call" | custom-call | flops 100000000 | bytes 1000000 | tf_op jit(solution)/shard_map/local/pallas_call | solution.py:795
  53.3 2.5 %all-to-all-done.2 = f32[16,8,128]{2,1,0:T(8,128)S(1)} async-done(((f32[16,8,128]{2,1,0:T(8,128)}), f32[16,8,128]{2,1,0:T(8,128)S(1)}, u32[]{:S(2)}, u32[]{:S(2)}) %all-to-all-start.2) | async-done | bytes 65568 | tf_op jit(solution)/shard_map/all_to_all | solution.py:860
  55.9 1.3 %second.1 = (f32[6,20,384]{2,1,0:T(8,128)}, f32[6,20,384]{2,1,0:T(8,128)}) custom-call(f32[128,128]{1,0:T(8,128)S(1)} %bitcast.11, f32[6,20,384]{2,1,0:T(8,128)S(1)} %local.1.part_ref, f32[6,20,384]{2,1,0:T(8,128)S(1)} %get-tuple-element.28.refs_0_.middle_ref, f32[6,20,384]{2,1,0:T(8,128)S(1)} %get-tuple-element.29.first_ref, ...), custom_call_target="tpu_custom_call" | custom-call | flops 100000000 | bytes 1000000 | tf_op jit(solution)/shard_map/second/pallas_call | solution.py:795
Async XLA Ops:
  2.0 28.2 %copy-start.5 = (s32[1,16,16]{2,1,0:T(8,128)S(1)}, s32[1,16,16]{2,1,0:T(8,128)}, u32[]{:S(2)}) copy-start(s32[1,16,16]{2,1,0:T(8,128)} %list_ref.1) | copy-start | bytes 3076
  31.4 7.7 %copy-start = (bf16[80,192]{1,0:T(8,128)(2,1)S(1)}, bf16[80,192]{1,0:T(8,128)(2,1)}, u32[]{:S(2)}) copy-start(bf16[80,192]{1,0:T(8,128)(2,1)} %constant.6.clone.slope_ref.refs_4_) | copy-start | bytes 92164
  31.4 7.7 %copy-start.1 = (bf16[32,288]{1,0:T(8,128)(2,1)S(1)}, bf16[32,288]{1,0:T(8,128)(2,1)}, u32[]{:S(2)}) copy-start(bf16[32,288]{1,0:T(8,128)(2,1)} %constant.7.clone.lift_ref.refs_5_) | copy-start | bytes 55300
  31.4 7.7 %copy-start.3 = (s32[4,384]{1,0:T(4,128)S(1)}, s32[4,384]{1,0:T(4,128)}, u32[]{:S(2)}) copy-start(s32[4,384]{1,0:T(4,128)} %refs_2_.1) | copy-start | bytes 18436
  31.4 7.7 %copy-start.4 = (s32[4,384]{1,0:T(4,128)S(1)}, s32[4,384]{1,0:T(4,128)}, u32[]{:S(2)}) copy-start(s32[4,384]{1,0:T(4,128)} %refs_3_.1) | copy-start | bytes 18436
  31.5 11.9 %all-to-all-start.1 = ((f32[16,8,128]{2,1,0:T(8,128)}), f32[16,8,128]{2,1,0:T(8,128)S(1)}, u32[]{:S(2)}, u32[]{:S(2)}) async-start(f32[16,8,128]{2,1,0:T(8,128)} %bitcast.3), calls=%async_computation.1 | async-start | bytes 131072 | tf_op jit(solution)/shard_map/all_to_all | solution.py:860
  39.1 4.2 %copy-start.2 = (bf16[96,96]{1,0:T(8,128)(2,1)S(1)}, bf16[96,96]{1,0:T(8,128)(2,1)}, u32[]{:S(2)}) copy-start(bf16[96,96]{1,0:T(8,128)(2,1)} %constant.8.clone.lift_ref) | copy-start | bytes 55300
  44.7 11.2 %all-to-all-start.2 = ((f32[16,8,128]{2,1,0:T(8,128)}), f32[16,8,128]{2,1,0:T(8,128)S(1)}, u32[]{:S(2)}, u32[]{:S(2)}) async-start(f32[16,8,128]{2,1,0:T(8,128)} %bitcast.5), calls=%async_computation.2 | async-start | bytes 131072 | tf_op jit(solution)/shard_map/all_to_all | solution.py:860

commit v8 on v6

--- a/solution.py
+++ b/solution.py
@@ -32,7 +32,17 @@
 block_rows = slots + 1
 slab_first = 21
 sub_first = 10
-slab_order = [(slab_first + place) % slabs for place in range(slabs)]
+slab_order = [
+    (slab_first + slabs // 2 * (place // 2 % 2) + place // 4 * 2 + place % 2) % slabs
+    for place in range(slabs)
+]
+slab_runs = []
+for start in range(4):
+    for place in range(start, slabs, 4):
+        if place > start and slab_order[place] == slab_order[place - 4] + 2:
+            slab_runs[-1][2] += 1
+        else:
+            slab_runs.append([slab_order[place], place, 1])
 sub_order = [(sub_first + place) % subs for place in range(subs)]
 
 
@@ -279,8 +289,10 @@
     turned = jnp.concatenate([codes_ref[slot_id] for slot_id in range(slots)], axis=0)
     turned = jnp.concatenate([turned, jnp.zeros((lane - slots, slabs), jnp.int32)], axis=0)
     turned = jnp.concatenate([turned, jnp.zeros((lane, lane - slabs), jnp.int32)], axis=1)
+    place = lax.broadcasted_iota(jnp.int32, (lane, lane), 1)
+    slab = ((place >> 1) & 1) * (slabs // 2) + (place >> 2) * 2 + (place & 1) + slab_first
+    turned = jnp.take_along_axis(turned, slab & (slabs - 1), axis=1, mode="promise_in_bounds")
     codes = jnp.transpose(turned)[:slabs]
-    codes = jnp.concatenate([codes[slab_first:], codes[:slab_first]], axis=0)
     lanes = lax.broadcasted_iota(jnp.int32, (slabs, old_count), 1)
     picks = jnp.concatenate(
         [one_hot(codes[:, slot_id : slot_id + 1] == lanes) for slot_id in range(slots)], axis=0
@@ -379,7 +391,8 @@
 def start_kernel(came_ref, list_ref, trace_ref, codes_ref):
     face, element = trace_codes(list_ref, codes_ref)
     source = (element * 5462) >> 16
-    place = (source + slabs - slab_first) & (slabs - 1)
+    turn = (source + slabs - slab_first) & (slabs - 1)
+    place = ((turn & (slabs // 2 - 1)) >> 1) * 4 + (turn >> 4) * 2 + (turn & 1)
     picks = lane_picks(place * block_rows + element - source * slots, tiles + 1)
     parts = jnp.concatenate(split_three(came_ref[...]), axis=1)
     parts = jnp.concatenate(
@@ -390,18 +403,15 @@
 
 def unpack(came_ref, state_ref, derived_ref, rows_ref, tail_ref, main_ref):
     field_rows = components * node_count
-    runs = ((slab_first, 0, slabs - slab_first), (0, slabs - slab_first, slab_first))
-    tail = jnp.concatenate(
-        [
-            came_ref[pl.ds(place * block_rows + slots, count, stride=block_rows), :]
-            for _, place, count in reversed(runs)
-        ],
-        axis=0,
-    )
+    for source, place, count in slab_runs:
+        tail_ref[pl.ds(source, count, stride=2), :] = came_ref[
+            pl.ds(place * block_rows + slots, count, stride=4 * block_rows), :
+        ]
+    tail = tail_ref[0:slabs, :]
     for slot_id in range(slots):
-        for source, place, count in runs:
-            rows_ref[pl.ds(source * slots + slot_id, count, stride=slots), :] = came_ref[
-                pl.ds(place * block_rows + slot_id, count, stride=block_rows), :
+        for source, place, count in slab_runs:
+            rows_ref[pl.ds(source * slots + slot_id, count, stride=2 * slots), :] = came_ref[
+                pl.ds(place * block_rows + slot_id, count, stride=4 * block_rows), :
             ]
         shifted = pltpu.roll(tail, lane - 3 * slot_id, 1) if slot_id else tail
         tail_ref[pl.ds(slot_id, slabs, stride=slots), :] = shifted

time: 57.5 us -> 57.5 us (level)
  the two profiles are of different devices: /device:TPU:2 before, /device:TPU:1 now
where the time goes in v8:
time: 57.5 us; the launch traced here: 57.2 us
  blocking collectives  30.1 us (52%)
  starting transfers between devices  16.4 us (29%)
  Pallas kernels  9.55 us (17%)
  between operations  0.71 us (1%)
    all_to_all x1, blocking collectives, shards(): lax.all_to_all(parcel.reshape(slabs, block_rows * lane), 'slab', split_ax...  30.1 us
    all_to_all x2, starting transfers between devices, exchange(): lax.all_to_all(blocks, 'sub', split_axis=0, concat_axis=0, tiled=True, ax...  16.4 us
    pallas_call x6, Pallas kernels, run(): pl.pallas_call(kernel, name=name, out_shape=outs, in_specs=in_specs or [f...  9.55 us
  transfers between devices with their start and end apart: 2, of which 1 were waited for; matrix products, arithmetic and copies ran while one was open for 0% of the time, Pallas kernels for 8%

profile of v8, /device:TPU:1, one launch (start us, length us, event | category | flops | bytes accessed | tf_op | source)
XLA Modules:
  0.0 57.2 jit_solution(3825614664551004260)
XLA Ops:
  0.6 1.4 %pack.1 = f32[416,128]{1,0:T(8,128)S(1)} custom-call(f32[6,20,256]{2,1,0:T(8,128)} %fields_ref.1, f32[11,256]{1,0:T(8,128)} %geometry_ref.1, s32[12,1,32]{2,1,0:T(1,128)} %bitcast.12), custom_call_target="tpu_custom_call" | custom-call | flops 100000000 | bytes 1000000 | tf_op jit(solution)/shard_map/pack/pallas_call | solution.py:795
  2.0 0.0 copy-start.5
  2.1 30.1 %all_to_all.19 = f32[32,1,1664]{2,1,0:T(1,128)S(1)} all-to-all(f32[32,1,1664]{2,1,0:T(1,128)S(1)} %bitcast.7), channel_id=1, replica_groups={{336,352,80,96,368,384,112,128,400,416,144,160,432,448,176,192,464,480,..., dimensions={0} | all-to-all | bytes 425984 | tf_op jit(solution)/shard_map/all_to_all | solution.py:837
  32.2 0.0 copy-done.5
  32.2 1.2 %start.1 = f32[128,128]{1,0:T(8,128)} custom-call(f32[416,128]{1,0:T(8,128)S(1)} %bitcast.10, s32[1,16,16]{2,1,0:T(8,128)S(1)} %copy-done.5), custom_call_target="tpu_custom_call" | custom-call | flops 100000000 | bytes 1000000 | tf_op jit(solution)/shard_map/start/pallas_call | solution.py:795
  33.3 0.0 copy-start.1
  33.3 0.0 copy-start.2
  33.3 0.0 copy-start.3
  33.3 0.0 copy-start.4
  33.3 8.8 %all-to-all-start.1 = ((f32[16,8,128]{2,1,0:T(8,128)}), f32[16,8,128]{2,1,0:T(8,128)S(1)}, u32[]{:S(2)}, u32[]{:S(2)}) async-start(f32[16,8,128]{2,1,0:T(8,128)} %bitcast.3), calls=%async_computation.1 | async-start | bytes 131072 | tf_op jit(solution)/shard_map/all_to_all | solution.py:848
  42.2 0.0 copy-done.1
  42.2 0.0 copy-done.2
  42.2 0.0 copy-done.3
  42.2 0.0 copy-done.4
  42.2 0.0 copy-start
  42.2 2.7 %arrive.1 = (f32[6,20,384]{2,1,0:T(8,128)S(1)}, f32[64,384]{1,0:T(8,128)S(1)}, f32[8,256]{1,0:T(8,128)S(1)}, f32[6,20,384]{2,1,0:T(8,128)S(1)}, s32[256,128]{1,0...) custom-call(f32[416,128]{1,0:T(8,128)S(1)} %bitcast.11, ...), custom_call_target="tpu_custom_call" | custom-call | flops 100000000 | bytes 1000000 | tf_op jit(solution)/shard_map/arrive/pallas_call | solution.py:795
  44.9 0.0 all-to-all-done.1
  44.9 0.0 copy-done
  44.9 1.4 %first.1 = (f32[6,20,384]{2,1,0:T(8,128)S(1)}, f32[6,20,384]{2,1,0:T(8,128)S(1)}, f32[128,128]{1,0:T(8,128)}) custom-call(f32[128,128]{1,0:T(8,128)S(1)} %bitcast.8, f32[6,20,384]{2,1,0:T(8,128)S(1)} %get-tuple-element.14.part_ref, f32[6,20,384]{2,1,0:T(8,128)S(1)} %get-tuple-element.15.state_ref, f32[64,384]{1,0:T(8,128)S(1)} %get-tuple-element.16.derived_ref.refs_1_, ...), custom_call_target="tpu_custom_call" | custom-call | flops 100000000 | bytes 1000000 | tf_op jit(solution)/shard_map/first/pallas_call | solution.py:795
  46.3 7.5 %all-to-all-start.2 = ((f32[16,8,128]{2,1,0:T(8,128)}), f32[16,8,128]{2,1,0:T(8,128)S(1)}, u32[]{:S(2)}, u32[]{:S(2)}) async-start(f32[16,8,128]{2,1,0:T(8,128)} %bitcast.5), calls=%async_computation.2 | async-start | bytes 131072 | tf_op jit(solution)/shard_map/all_to_all | solution.py:848
  53.9 1.6 %local.1.part_ref = f32[6,20,384]{2,1,0:T(8,128)S(1)} custom-call(f32[6,20,384]{2,1,0:T(8,128)S(1)} %get-tuple-element.24.refs_0_.middle_ref, f32[64,384]{1,0:T(8,128)S(1)} %get-tuple-element.16.derived_ref.refs_1_, s32[4,384]{1,0:T(4,128)S(1)} %copy-done.3, s32[4,384]{1,0:T(4,128)S(1)} %copy-done.4, bf16[80,192]{1,0:T(8,128)(2,1)S(1)} %copy-done.1, ...), custom_call_target="tpu_custom_call" | custom-call | flops 100000000 | bytes 1000000 | tf_op jit(solution)/shard_map/local/pallas_call | solution.py:795
  55.5 0.4 all-to-all-done.2
  55.8 1.3 %second.1 = (f32[6,20,384]{2,1,0:T(8,128)}, f32[6,20,384]{2,1,0:T(8,128)}) custom-call(f32[128,128]{1,0:T(8,128)S(1)} %bitcast.9, f32[6,20,384]{2,1,0:T(8,128)S(1)} %local.1.part_ref, f32[6,20,384]{2,1,0:T(8,128)S(1)} %get-tuple-element.24.refs_0_.middle_ref, f32[6,20,384]{2,1,0:T(8,128)S(1)} %get-tuple-element.25.first_ref, ...), custom_call_target="tpu_custom_call" | custom-call | flops 100000000 | bytes 1000000 | tf_op jit(solution)/shard_map/second/pallas_call | solution.py:795
Async XLA Ops:
  2.0 30.1 %copy-start.5 = (s32[1,16,16]{2,1,0:T(8,128)S(1)}, s32[1,16,16]{2,1,0:T(8,128)}, u32[]{:S(2)}) copy-start(s32[1,16,16]{2,1,0:T(8,128)} %list_ref.3) | copy-start | bytes 3076
  33.3 8.9 %copy-start.1 = (bf16[80,192]{1,0:T(8,128)(2,1)S(1)}, bf16[80,192]{1,0:T(8,128)(2,1)}, u32[]{:S(2)}) copy-start(bf16[80,192]{1,0:T(8,128)(2,1)} %constant.6.clone.slope_ref.refs_4_) | copy-start | bytes 92164
  33.3 8.9 %copy-start.2 = (bf16[32,288]{1,0:T(8,128)(2,1)S(1)}, bf16[32,288]{1,0:T(8,128)(2,1)}, u32[]{:S(2)}) copy-start(bf16[32,288]{1,0:T(8,128)(2,1)} %constant.7.clone.lift_ref.refs_5_) | copy-start | bytes 55300
  33.3 8.9 %copy-start.3 = (s32[4,384]{1,0:T(4,128)S(1)}, s32[4,384]{1,0:T(4,128)}, u32[]{:S(2)}) copy-start(s32[4,384]{1,0:T(4,128)} %refs_2_.1) | copy-start | bytes 18436
  33.3 8.9 %copy-start.4 = (s32[4,384]{1,0:T(4,128)S(1)}, s32[4,384]{1,0:T(4,128)}, u32[]{:S(2)}) copy-start(s32[4,384]{1,0:T(4,128)} %refs_3_.1) | copy-start | bytes 18436
  33.3 11.6 %all-to-all-start.1 = ((f32[16,8,128]{2,1,0:T(8,128)}), f32[16,8,128]{2,1,0:T(8,128)S(1)}, u32[]{:S(2)}, u32[]{:S(2)}) async-start(f32[16,8,128]{2,1,0:T(8,128)} %bitcast.3), calls=%async_computation.1 | async-start | bytes 131072 | tf_op jit(solution)/shard_map/all_to_all | solution.py:848
  42.2 2.7 %copy-start = (bf16[96,96]{1,0:T(8,128)(2,1)S(1)}, bf16[96,96]{1,0:T(8,128)(2,1)}, u32[]{:S(2)}) copy-start(bf16[96,96]{1,0:T(8,128)(2,1)} %constant.8.clone.lift_ref) | copy-start | bytes 55300
  46.3 9.5 %all-to-all-start.2 = ((f32[16,8,128]{2,1,0:T(8,128)}), f32[16,8,128]{2,1,0:T(8,128)S(1)}, u32[]{:S(2)}, u32[]{:S(2)}) async-start(f32[16,8,128]{2,1,0:T(8,128)} %bitcast.5), calls=%async_computation.2 | async-start | bytes 131072 | tf_op jit(solution)/shard_map/all_to_all | solution.py:848
